TPU v7x, 256 devices: a whole 4x4x8 slice. The times are simulated.
256 devices in a mesh: grp: 8 (over z), ep: 32 (over x, y, core).
Axes of the slice: x: 4, y: 4, z: 8, core: 2. Of those that a mesh axis runs over, the one named last changes fastest.
Arguments:
- tokens: bfloat16 [8, 1, 1024, 4096], P('grp', None, 'ep'), may hold values from -6 to 6
- gates: float32 [8, 1, 1024, 8], P('grp', None, 'ep'), may hold values from 0.1 to 1
- routes: int32 [8, 1, 1024, 8], P('grp'), may hold values from 0 to 31, all different within a row; in each aligned block of 32 rows (0 to 31, 32 to 63, ..., all dimensions but the last counted through in order) at most 16 rows name the same one
- master_up: float32 [32, 4096, 1536], P('ep', 'grp'), may hold values from -0.09375 to 0.09375
- master_down: float32 [32, 1536, 4096], P('ep', None, 'grp'), may hold values from -0.15625 to 0.15625
Outputs:
- mixed: bfloat16 [8, 1, 1024, 4096], P('grp', None, 'ep')
Inputs may be any that keep to these rules, and one draw needn't show every extreme that they name: `routes`: each token names 8 different experts; among the 32 tokens of one aligned block of one group in one step no expert is named more than 16 times, and in some block one expert exactly 16 times.
All inputs are finite; a program needn't handle non-finite values.
Results may differ from a plain program's by a relative error of at most 0.024.
Values may be sent and summed in bfloat16 or wider, within the bound.
No kernel may reach another device: no remote copies, remote signals or barrier semaphores. Data moves between devices by JAX's collectives and lax.ppermute only.
A program may use at most 320 MiB of HBM per device.

v0:
```python
import jax
import jax.numpy as jnp
from jax import lax
from jax.sharding import PartitionSpec as P

E = 32
BLK = 128
CAP = 16


def requantize(master):
    count, height, width = master.shape
    blocks = master.reshape(count, height // BLK, BLK, width // BLK, BLK)
    largest = jnp.max(jnp.abs(blocks), axis=(2, 4), keepdims=True)
    scale = (largest / 448.0 + 1e-06).astype(jnp.bfloat16).astype(jnp.float32)
    coded = (blocks / scale).astype(jnp.bfloat16)
    return (coded.astype(jnp.float32) * scale).astype(jnp.bfloat16).reshape(count, height, width)


def slot_rank(route_ids):
    onehot = (route_ids[..., None] == jnp.arange(E, dtype=jnp.int32)).astype(jnp.int32)
    running = jnp.cumsum(onehot, axis=-2)
    return jnp.sum((running - 1) * onehot, axis=-1)


def fill_slots(source, slot_pos, token_of, slot_total):
    owner = jnp.full((slot_total,), -1, jnp.int32).at[slot_pos].set(token_of, mode="drop")
    chosen = jnp.take(source, jnp.maximum(owner, 0), axis=0)
    return jnp.where((owner >= 0)[:, None], chosen, jnp.zeros_like(chosen))


def local(tokens, gates, routes, master_up, master_down):
    tokens = tokens[0]
    gates = gates[0]
    routes = routes[0]
    ep_count = lax.axis_size("ep")
    local_count = E // ep_count
    steps, tok_dev, width = tokens.shape
    top = gates.shape[2]
    route_count = tok_dev * top
    slot_total = local_count * ep_count * CAP
    up_w, down_w = (
        lax.all_gather(requantize(master_up), "grp", axis=1, tiled=True),
        lax.all_gather(requantize(master_down), "grp", axis=2, tiled=True),
    )
    my_index = lax.axis_index("ep")
    own_routes = lax.dynamic_slice_in_dim(routes, my_index * tok_dev, tok_dev, 1).reshape(
        steps, route_count
    )
    own_rank = slot_rank(own_routes)
    own_pos = (own_routes % local_count * ep_count + own_routes // local_count) * CAP + own_rank
    token_of = jnp.arange(route_count, dtype=jnp.int32) // top
    send = jax.vmap(lambda source, places: fill_slots(source, places, token_of, slot_total))(
        tokens, own_pos
    )
    received = lax.all_to_all(
        send.reshape(steps, local_count, ep_count, CAP, width),
        "ep",
        split_axis=2,
        concat_axis=2,
        tiled=True,
    )
    expert_rows = received.reshape(steps, local_count, ep_count * CAP, width)
    up_acts = jnp.einsum("slrd,ldf->slrf", expert_rows, up_w, preferred_element_type=jnp.float32)
    hidden = jax.nn.silu(up_acts).astype(jnp.bfloat16)
    expert_out = jnp.einsum(
        "slrf,lfd->slrd", hidden, down_w, preferred_element_type=jnp.float32
    ).astype(jnp.bfloat16)
    returned = lax.all_to_all(
        expert_out.reshape(steps, local_count, ep_count, CAP, width),
        "ep",
        split_axis=2,
        concat_axis=2,
        tiled=True,
    )
    returned = returned.reshape(steps, slot_total, width)
    picked = jax.vmap(lambda source, places: jnp.take(source, places, axis=0))(returned, own_pos)
    picked = picked.reshape(steps, tok_dev, top, width)
    mixed = jnp.sum(gates[..., None] * picked.astype(jnp.float32), axis=2)
    return mixed.astype(jnp.bfloat16)[None]


def solution(mesh):
    placed = (
        P("grp", None, "ep", None),
        P("grp", None, "ep", None),
        P("grp", None, None, None),
        P("ep", "grp", None),
        P("ep", None, "grp"),
    )
    return jax.shard_map(
        local, mesh=mesh, in_specs=placed, out_specs=P("grp", None, "ep", None), check_vma=False
    )
```

profile of v0, /device:TPU:1, one launch (start us, length us, event | category | flops | bytes accessed | tf_op | source)
XLA Modules:
  0.0 412.0 jit_solution(11550617301716076210)
XLA Ops:
  6.5 0.0 copy-start
  6.5 0.0 copy-start.2
  6.5 0.0 all-gather.5.cloned.1.call-start
  6.5 4.1 abs.36
  10.6 0.0 copy-done.2
  10.6 2.4 copy.21
  13.0 2.4 copy.20
  15.3 2.7 abs.37
  18.1 2.4 reduce_max.19
  20.5 0.5 div.61
  21.0 2.9 div.62
  23.9 0.0 copy-start.3
  23.9 5.1 %multiply_convert_fusion.1 = bf16[1,512,1536]{1,2,0:T(8,128)(2,1)} fusion(f32[1,512,1536]{1,2,0:T(8,128)} %div.62, f32[1,512,1536]{1,2,0:T(8,128)} %copy.21), kind=kLoop, calls=%fused_computation.12 | loop fusion | flops 3932160 | bytes 7864320 | tf_op jit(solution)/shard_map/convert_element_type | solution.py:17
  28.9 0.0 all-gather.5.cloned.1.call-update
  28.9 0.0 all-gather.3.cloned.1.call-start
  29.0 0.0 copy-done.3
  29.0 2.1 abs.34
  31.1 3.1 abs.35
  34.2 0.6 reduce_max.18
  34.8 0.5 div.56
  35.3 2.9 div.57
  38.1 4.8 %multiply_convert_fusion.2 = bf16[1,1536,512]{2,1,0:T(8,128)(2,1)} fusion(f32[1,1536,512]{2,1,0:T(8,128)} %div.57, f32[1,1536,512]{2,1,0:T(8,128)} %param.9), kind=kLoop, calls=%fused_computation.14 | loop fusion | flops 3932160 | bytes 7864320 | tf_op jit(solution)/shard_map/convert_element_type | solution.py:17
  43.0 0.0 all-gather.3.cloned.1.call-update
  43.0 0.8 constant_dynamic-slice_fusion
  43.8 0.1 copy.24
  43.9 0.1 eq.29
  44.0 0.6 reduce-window.6
  44.6 0.2 slice_reduce_fusion
  44.8 0.1 copy.19
  44.9 0.1 mul.104
  45.1 0.1 broadcast.469
  45.2 0.1 fusion.15
  45.3 1.6 scatter_custom_fusion
  46.9 0.1 broadcast_in_dim.51
  47.0 0.1 broadcast_in_dim.53
  47.1 0.0 copy-done
  47.1 17.4 %gather_fusion = bf16[512,4096]{1,0:T(8,128)(2,1)} fusion(bf16[1,32,4096]{2,1,0:T(8,128)(2,1)S(1)} %bitcast.99, s32[512]{0:T(512)S(1)} %bitcast.100), kind=kCustom, calls=%fused_computation | custom fusion | bytes 8392704 | tf_op jit(solution)/shard_map/vmap(jit(_take))/gather | solution.py:28
  64.5 2.6 select_select_fusion
  67.1 59.2 %all_to_all.10 = bf16[1,1,32,16,4096]{4,3,1,0,2:T(8,128)(2,1)} all-to-all(bf16[1,1,32,16,4096]{4,3,1,0,2:T(8,128)(2,1)S(1)} %select_select_fusion), channel_id=1, replica_groups=mesh['grp'=8,'ep'=32] {'ep'}, dimensions={2} | all-to-all | bytes 8388608 | tf_op jit(solution)/shard_map/all_to_all | solution.py:56
  126.3 40.0 %all-gather.5.cloned.1.call-done = bf16[1,4096,1536]{1,2,0:T(8,128)(2,1)} async-done(((bf16[1,512,1536]{1,2,0:T(8,128)(2,1)}), bf16[1,4096,1536]{1,2,0:T(8,128)(2,1)}) %all-gather.5.cloned.1.call-update) | async-done | bytes 12582928 | tf_op jit(solution)/shard_map/all_gather | solution.py:43
  166.3 133.9 %all-gather.3.cloned.1.call-done = bf16[1,1536,4096]{2,1,0:T(8,128)(2,1)} async-done(((bf16[1,1536,512]{2,1,0:T(8,128)(2,1)}), bf16[1,1536,4096]{2,1,0:T(8,128)(2,1)}) %all-gather.3.cloned.1.call-update) | async-done | bytes 12582928 | tf_op jit(solution)/shard_map/all_gather | solution.py:44
  300.2 36.3 %fusion.4 = bf16[4096,512]{0,1:T(8,128)(2,1)} fusion(bf16[1,1536,4096]{2,1,0:T(8,128)(2,1)} %all-gather.3.cloned.1.call-done, bf16[512,4096]{1,0:T(8,128)(2,1)} %bitcast.104, bf16[1,4096,1536]{1,2,0:T(8,128)(2,1)} %all-gather.5.cloned.1.call-done), kind=kOutput, calls=%fused_computation.7 | convolution fusion | flops 12890931200 | bytes 33554432 | tf_op jit(solution)/shard_map/slrf,lfd->slrd/dot_general | solution.py:66
  336.6 0.0 copy-start.4
  336.6 7.7 %all-to-all-start.1 = ((bf16[1,1,32,16,4096]{4,3,1,0,2:T(8,128)(2,1)}), bf16[1,1,32,16,4096]{4,3,1,0,2:T(8,128)(2,1)}, u32[]{:S(2)}, u32[]{:S(2)}) async-start(bf16[1,1,32,16,4096]{4,3,1,0,2:T(8,128)(2,1)} %bitcast.103), calls=%async_computation.1 | async-start | bytes 8388608 | tf_op jit(solution)/shard_map/all_to_all | solution.py:69
  344.3 0.1 reduce_sum.23
  344.4 0.0 copy-done.4
  344.4 0.1 copy.15
  344.5 52.0 %all-to-all-done.1 = bf16[1,1,32,16,4096]{4,3,1,0,2:T(8,128)(2,1)} async-done(((bf16[1,1,32,16,4096]{4,3,1,0,2:T(8,128)(2,1)}), bf16[1,1,32,16,4096]{4,3,1,0,2:T(8,128)(2,1)}, u32[]{:S(2)}, u32[]{:S(2)}) %all-to-all-start.1) | async-done | bytes 4194336 | tf_op jit(solution)/shard_map/all_to_all | solution.py:69
  396.5 0.0 copy-start.1
  396.5 6.1 %gather_fusion.1 = bf16[256,4096]{1,0:T(8,128)(2,1)S(1)} fusion(bf16[1,512,4096]{2,1,0:T(8,128)(2,1)} %bitcast.29, s32[256]{0:T(256)S(1)} %bitcast.101), kind=kCustom, calls=%fused_computation.1 | custom fusion | bytes 4196352 | tf_op jit(solution)/shard_map/vmap(jit(_take))/gather | solution.py:77
  402.6 2.6 multiply_reduce_fusion
  405.2 0.0 copy-done.1
  (17 shorter events, 0.2 us)
Async XLA Ops:
  6.5 40.5 %copy-start = (bf16[1,1,32,4096]{3,2,1,0:T(8,128)(2,1)S(1)}, bf16[1,1,32,4096]{3,2,1,0:T(8,128)(2,1)}, u32[]{:S(2)}) copy-start(bf16[1,1,32,4096]{3,2,1,0:T(8,128)(2,1)} %param.5) | copy-start | bytes 786436
  6.5 4.1 copy-start.2
  6.5 159.8 %all-gather.5.cloned.1.call-start = ((), (), s32[]{:S(2)}) async-start(), calls=%async_computation.3 | async-start | bytes 14155776 | tf_op jit(solution)/shard_map/all_gather | solution.py:43
  23.9 5.1 %copy-start.3 = (f32[1,1536,512]{2,1,0:T(8,128)S(1)}, f32[1,1536,512]{2,1,0:T(8,128)}, u32[]{:S(2)}) copy-start(f32[1,1536,512]{2,1,0:T(8,128)} %param.9) | copy-start | bytes 9437188
  28.9 271.3 %all-gather.3.cloned.1.call-start = ((), (), s32[]{:S(2)}) async-start(), calls=%async_computation.2 | async-start | bytes 14155776 | tf_op jit(solution)/shard_map/all_gather | solution.py:44
  336.6 7.8 %copy-start.4 = (f32[1,1,32,8]{2,3,1,0:T(8,128)S(1)}, f32[1,1,32,8]{2,3,1,0:T(8,128)}, u32[]{:S(2)}) copy-start(f32[1,1,32,8]{2,3,1,0:T(8,128)} %param.6) | copy-start | bytes 3076
  336.6 59.9 %all-to-all-start.1 = ((bf16[1,1,32,16,4096]{4,3,1,0,2:T(8,128)(2,1)}), bf16[1,1,32,16,4096]{4,3,1,0,2:T(8,128)(2,1)}, u32[]{:S(2)}, u32[]{:S(2)}) async-start(bf16[1,1,32,16,4096]{4,3,1,0,2:T(8,128)(2,1)} %bitcast.103), calls=%async_computation.1 | async-start | bytes 8388608 | tf_op jit(solution)/shard_map/all_to_all | solution.py:69
  396.5 8.7 %copy-start.1 = (bf16[1,1,32,4096]{3,2,1,0:T(8,128)(2,1)S(1)}, bf16[1,1,32,4096]{3,2,1,0:T(8,128)(2,1)}, u32[]{:S(2)}) copy-start(bf16[1,1,32,4096]{3,2,1,0:T(8,128)(2,1)} %param.5) | copy-start | bytes 786436
Sparse Core Ops, SparseCore 0:
  29.1 137.2 all-gather.4
  168.1 132.0 all-gather.2
where the time goes:
time: 413 us; the launch traced here: 412 us
  waiting for transfers between devices  226 us (55%)
  blocking collectives  59.2 us (14%)
  local copies, waits for them, and re-layouts  44.2 us (11%)
  matrix products  36.3 us (9%)
  other arithmetic  25.1 us (6%)
  between operations  13.6 us (3%)
  starting transfers between devices  7.77 us (2%)
    all_gather x1, waiting for transfers between devices, local(): lax.all_gather(requantize(master_down), 'grp', axis=2, tiled=True)  134 us
    all_to_all x1, blocking collectives, local(): lax.all_to_all(send.reshape(steps, local_count, ep_count, CAP, width), 'e...  59.2 us
    all_to_all x1, waiting for transfers between devices, local(): lax.all_to_all(expert_out.reshape(steps, local_count, ep_count, CAP, widt...  52 us
    all_gather x1, waiting for transfers between devices, local(): lax.all_gather(requantize(master_up), 'grp', axis=1, tiled=True)  40 us
    dot_general x1, matrix products, local(): jnp.einsum('slrf,lfd->slrd', hidden, down_w, preferred_element_type=jnp.f...  36.3 us
    gather x2, local copies, waits for them, and re-layouts, fill_slots(): chosen = jnp.take(source, jnp.maximum(owner, 0), axis=0)  17.4 us
    convert_element_type x2, other arithmetic, requantize(): (coded.astype(jnp.float32) * scale).astype(jnp.bfloat16)  9.9 us
  transfers between devices with their start and end apart: 3, of which 3 were waited for; matrix products, arithmetic and copies ran while one was open for 9% of the time, Pallas kernels for 0%

commit v1 on v0

v1 whole, which is shorter than its diff:
```python
import jax
import jax.numpy as jnp
from jax import lax
from jax.experimental import pallas as pl
from jax.experimental.pallas import tpu as pltpu
from jax.sharding import PartitionSpec as P

E = 32
BLK = 128
CAP = 16
PARTS = 4


def coded_block(entries):
    largest = jnp.max(jnp.max(jnp.abs(entries), axis=0, keepdims=True), axis=1, keepdims=True)
    scale = (largest / 448.0 + 1e-06).astype(jnp.bfloat16).astype(jnp.float32)
    coded = (entries / scale).astype(jnp.bfloat16)
    return (coded.astype(jnp.float32) * scale).astype(jnp.bfloat16)


def requantize_rows_kernel(master_ref, out_ref):
    for part in range(master_ref.shape[1] // BLK):
        columns = slice(part * BLK, (part + 1) * BLK)
        out_ref[:, columns] = coded_block(master_ref[:, columns])


def requantize_rows(master):
    height, width = master.shape
    return pl.pallas_call(
        requantize_rows_kernel,
        grid=(height // BLK,),
        in_specs=[pl.BlockSpec((BLK, width), lambda i: (i, 0))],
        out_specs=pl.BlockSpec((BLK, width), lambda i: (i, 0)),
        out_shape=jax.ShapeDtypeStruct((height, width), jnp.bfloat16),
        cost_estimate=pl.CostEstimate(
            flops=6 * height * width, bytes_accessed=6 * height * width, transcendentals=0
        ),
        name="requantize_up",
    )(master)


def requantize_columns_kernel(master_ref, *out_refs):
    for row in range(master_ref.shape[0] // BLK):
        rows = slice(row * BLK, (row + 1) * BLK)
        for part, out_ref in enumerate(out_refs):
            out_ref[rows, :] = coded_block(master_ref[rows, part * BLK:(part + 1) * BLK])


def requantize_columns(master):
    height, width = master.shape
    step = 3 * BLK
    return pl.pallas_call(
        requantize_columns_kernel,
        grid=(height // step,),
        in_specs=[pl.BlockSpec((step, width), lambda i: (i, 0))],
        out_specs=[pl.BlockSpec((step, BLK), lambda i: (i, 0))] * (width // BLK),
        out_shape=[jax.ShapeDtypeStruct((height, BLK), jnp.bfloat16)] * (width // BLK),
        cost_estimate=pl.CostEstimate(
            flops=6 * height * width, bytes_accessed=6 * height * width, transcendentals=0
        ),
        name="requantize_down",
    )(master)


def local(tokens, gates, routes, master_up, master_down):
    tokens = tokens[0, 0]
    gates = gates[0, 0]
    routes = routes[0, 0]
    ep_count = lax.axis_size("ep")
    tok_dev, width = tokens.shape
    slot_total = ep_count * CAP

    up_q = requantize_rows(master_up[0])
    up_w = lax.all_gather(up_q, "grp", axis=0, tiled=True)
    down_q = requantize_columns(master_down[0])
    down_w = [lax.all_gather(part, "grp", axis=1, tiled=True) for part in down_q]

    own_routes = lax.dynamic_slice_in_dim(routes, lax.axis_index("ep") * tok_dev, tok_dev, 0)
    named = own_routes[:, :, None] == jnp.arange(E, dtype=jnp.int32)
    mask = jnp.any(named, axis=1)
    gate_of = jnp.sum(jnp.where(named, gates[:, :, None], 0.0), axis=1)
    earlier = jnp.tril(jnp.ones((tok_dev, tok_dev), jnp.bfloat16), -1)
    rank = jnp.dot(earlier, mask.astype(jnp.bfloat16), preferred_element_type=jnp.float32)
    rank = jnp.where(mask, rank.astype(jnp.int32), -1)
    in_slot = rank[:, :, None] == jnp.arange(CAP, dtype=jnp.int32)
    place = in_slot.reshape(tok_dev, slot_total).astype(jnp.bfloat16)
    gate_hi = gate_of.astype(jnp.bfloat16)
    gate_lo = (gate_of - gate_hi.astype(jnp.float32)).astype(jnp.bfloat16)
    weigh = jnp.concatenate(
        [
            jnp.where(in_slot, part[:, :, None], 0.0).astype(jnp.bfloat16).reshape(tok_dev, slot_total)
            for part in (gate_hi, gate_lo)
        ],
        axis=0,
    )

    send = lax.dot_general(place, tokens, (((0,), (0,)), ((), ())), preferred_element_type=jnp.float32)
    send = send.astype(jnp.bfloat16).reshape(ep_count, CAP, width)
    rows = lax.all_to_all(send, "ep", split_axis=0, concat_axis=0, tiled=True).reshape(slot_total, width)

    hidden = jnp.dot(rows, up_w, preferred_element_type=jnp.float32)
    hidden = jax.nn.silu(hidden).astype(jnp.bfloat16)
    hidden = lax.optimization_barrier(hidden)

    pieces = []
    for weights in down_w:
        answer = jnp.dot(hidden, weights, preferred_element_type=jnp.float32).astype(jnp.bfloat16)
        part = answer.shape[1]
        back = lax.all_to_all(
            answer.reshape(ep_count, CAP, part), "ep", split_axis=0, concat_axis=0, tiled=True
        ).reshape(slot_total, part)
        both = jnp.dot(weigh, back, preferred_element_type=jnp.float32)
        mixed = (both[:tok_dev] + both[tok_dev:]).astype(jnp.bfloat16)
        pieces.append(mixed.reshape(tok_dev, -1, 1, BLK))
    return jnp.concatenate(pieces, axis=2).reshape(1, 1, tok_dev, width)


def solution(mesh):
    placed = (
        P("grp", None, "ep", None),
        P("grp", None, "ep", None),
        P("grp", None, None, None),
        P("ep", "grp", None),
        P("ep", None, "grp"),
    )
    return jax.shard_map(
        local, mesh=mesh, in_specs=placed, out_specs=P("grp", None, "ep", None), check_vma=False
    )
```

time: 413 us -> 408 us (0.988)
  waiting for transfers between devices: 226 us -> 291 us
  blocking collectives: 59.2 us -> 0 us
  starting transfers between devices: 7.77 us -> 52.3 us
  local copies, waits for them, and re-layouts: 44.2 us -> 3.04 us
  other arithmetic: 25.1 us -> 1.66 us
  Pallas kernels: 0 us -> 8.57 us
    all_to_all x1 -> x0, blocking collectives: 59.2 us -> none  [local(): lax.all_to_all(send.reshape(steps, local_count, ep_count, CAP, width), 'e...]
    all_gather x2 -> x5, waiting for transfers between devices: 174 us -> 223 us  [the longest x4 157 us: local(): lax.all_gather(part, 'grp', axis=1, tiled=True)]
    all_to_all x1 -> x5, starting transfers between devices: 7.73 us -> 52.2 us  [the longest x4 43.5 us: local(): lax.all_to_all(answer.reshape(ep_count, CAP, part), 'ep', split_axis=0, c...]
    gather x3 -> x0, local copies, waits for them, and re-layouts: 23.5 us -> none  [the longest x2 17.4 us: fill_slots(): chosen = jnp.take(source, jnp.maximum(owner, 0), axis=0)]
    all_to_all x1 -> x5, waiting for transfers between devices: 52 us -> 66.2 us  [the longest x1 51.6 us: local(): lax.all_to_all(send, 'ep', split_axis=0, concat_axis=0, tiled=True)]
    convert_element_type x4 -> x1, other arithmetic: 9.91 us -> 0.01 us  [local(): gate_lo = (gate_of - gate_hi.astype(jnp.float32)).astype(jnp.bfloat16)]
    pallas_call x0 -> x2, Pallas kernels: none -> 8.57 us  [the longest x1 4.34 us: requantize_rows(): pl.pallas_call(requantize_rows_kernel, grid=(height // BLK,), in_specs=[p...]
    abs x3 -> x0, local copies, waits for them, and re-layouts: 8.25 us -> none  [requantize(): largest = jnp.max(jnp.abs(blocks), axis=(2, 4), keepdims=True)]
  transfers between devices with their start and end apart: 3 -> 10, of which waited for: 3 -> 7; matrix products, arithmetic and copies ran while one was open for 9% -> 10% of each run, Pallas kernels for 0% -> 1%
where the time goes in v1:
time: 408 us; the launch traced here: 407 us
  waiting for transfers between devices  291 us (71%)
  starting transfers between devices  52.3 us (13%)
  matrix products  36.6 us (9%)
  between operations  13.4 us (3%)
  Pallas kernels  8.57 us (2%)
    all_gather x4, waiting for transfers between devices, local(): lax.all_gather(part, 'grp', axis=1, tiled=True)  157 us
    all_gather x1, waiting for transfers between devices, local(): up_w = lax.all_gather(up_q, 'grp', axis=0, tiled=True)  66.4 us
    all_to_all x1, waiting for transfers between devices, local(): lax.all_to_all(send, 'ep', split_axis=0, concat_axis=0, tiled=True)  51.6 us
    all_to_all x4, starting transfers between devices, local(): lax.all_to_all(answer.reshape(ep_count, CAP, part), 'ep', split_axis=0, c...  43.5 us
    dot_general x4, matrix products, local(): jnp.dot(hidden, weights, preferred_element_type=jnp.float32)  20.1 us
    all_to_all x4, waiting for transfers between devices, local(): lax.all_to_all(answer.reshape(ep_count, CAP, part), 'ep', split_axis=0, c...  14.5 us
    dot_general x1, matrix products, local(): hidden = jnp.dot(rows, up_w, preferred_element_type=jnp.float32)  11.2 us
    all_to_all x1, starting transfers between devices, local(): lax.all_to_all(send, 'ep', split_axis=0, concat_axis=0, tiled=True)  8.64 us
  transfers between devices with their start and end apart: 10, of which 7 were waited for; matrix products, arithmetic and copies ran while one was open for 10% of the time, Pallas kernels for 1%

profile of v1, /device:TPU:1, one launch (start us, length us, event | category | flops | bytes accessed | tf_op | source)
XLA Modules:
  0.0 406.8 jit_solution(6262715803804222995)
XLA Ops:
  6.5 0.0 copy-start
  6.5 0.0 all-gather.6.cloned.1.call-start
  6.5 4.3 %requantize_up.1 = bf16[512,1536]{1,0:T(8,128)(2,1)} custom-call(f32[512,1536]{1,0:T(8,128)} %bitcast.74), custom_call_target="tpu_custom_call" | custom-call | flops 4718592 | bytes 4718592 | tf_op jit(solution)/shard_map/requantize_up/pallas_call | solution.py:29
  10.9 0.0 all-gather.6.cloned.1.call-update
  10.9 0.0 all-gather.8.cloned.1.call-start
  11.0 4.2 %requantize_down.1 = (bf16[1536,128]{1,0:T(8,128)(2,1)}, bf16[1536,128]{1,0:T(8,128)(2,1)}, bf16[1536,128]{1,0:T(8,128)(2,1)}, bf16[1536,128]{1,0:T(8,128)(2,1)}) custom-call(f32[1536,512]{1,0:T(8,128)} %bitcast.75), custom_call_target="tpu_custom_call" | custom-call | flops 4718592 | bytes 4718592 | tf_op jit(solution)/shard_map/requantize_down/pallas_call | solution.py:52
  15.2 0.0 all-gather.8.cloned.1.call-update
  15.2 0.0 all-gather.10.cloned.1.call-start
  15.3 0.7 all-gather.10.cloned.1.call-update
  15.9 0.0 all-gather.12.cloned.1.call-start
  16.0 0.5 all-gather.12.cloned.1.call-update
  16.5 0.8 dynamic-slice_bitcast_fusion
  17.3 0.1 copy.12
  17.4 0.1 fusion.8
  17.5 0.2 fusion
  17.7 0.1 copy.13
  17.8 0.0 copy-done
  17.8 3.2 convolution_convert_fusion
  21.0 8.6 %all-to-all-start = ((bf16[32,16,4096]{2,1,0:T(8,128)(2,1)}), bf16[32,16,4096]{2,1,0:T(8,128)(2,1)}, u32[]{:S(2)}, u32[]{:S(2)}) async-start(bf16[32,16,4096]{2,1,0:T(8,128)(2,1)} %bitcast.69), calls=%async_computation | async-start | bytes 8388608 | tf_op jit(solution)/shard_map/all_to_all | solution.py:99
  29.6 0.0 all-gather.14.cloned.1.call-start
  29.7 0.5 all-gather.14.cloned.1.call-update
  30.2 51.6 %all-to-all-done = bf16[32,16,4096]{2,1,0:T(8,128)(2,1)} async-done(((bf16[32,16,4096]{2,1,0:T(8,128)(2,1)}), bf16[32,16,4096]{2,1,0:T(8,128)(2,1)}, u32[]{:S(2)}, u32[]{:S(2)}) %all-to-all-start) | async-done | bytes 4194336 | tf_op jit(solution)/shard_map/all_to_all | solution.py:99
  81.9 66.4 %all-gather.6.cloned.1.call-done = bf16[4096,1536]{1,0:T(8,128)(2,1)} async-done(((bf16[512,1536]{1,0:T(8,128)(2,1)}), bf16[4096,1536]{1,0:T(8,128)(2,1)}) %all-gather.6.cloned.1.call-update) | async-done | bytes 12582928 | tf_op jit(solution)/shard_map/all_gather | solution.py:74
  148.3 11.2 %multiply_convert_fusion = bf16[512,1536]{1,0:T(8,128)(2,1)S(1)} fusion(bf16[512,4096]{1,0:T(8,128)(2,1)} %bitcast.8, bf16[4096,1536]{1,0:T(8,128)(2,1)} %all-gather.6.cloned.1.call-done), kind=kOutput, calls=%fused_computation.1 | convolution fusion | flops 6446383104 | bytes 18350080 | tf_op jit(solution)/shard_map/dot_general | solution.py:101
  159.5 0.0 copy-start.3
  159.5 40.7 %all-gather.8.cloned.1.call-done = bf16[1536,1024]{1,0:T(8,128)(2,1)} async-done(((bf16[1536,128]{1,0:T(8,128)(2,1)}), bf16[1536,1024]{1,0:T(8,128)(2,1)}) %all-gather.8.cloned.1.call-update) | async-done | bytes 3145744 | tf_op jit(solution)/shard_map/all_gather | solution.py:76
  200.1 4.7 %convolution_convert_fusion.4 = bf16[512,1024]{1,0:T(8,128)(2,1)} fusion(bf16[512,1536]{1,0:T(8,128)(2,1)S(1)} %multiply_convert_fusion, bf16[1536,1024]{1,0:T(8,128)(2,1)} %all-gather.8.cloned.1.call-done), kind=kOutput, calls=%fused_computation.5 | convolution fusion | flops 1611137024 | bytes 5767168 | tf_op jit(solution)/shard_map/dot_general | solution.py:107
  204.8 0.0 copy-done.3
  204.8 10.9 %all-to-all-start.1 = ((bf16[32,16,1024]{2,1,0:T(8,128)(2,1)}), bf16[32,16,1024]{2,1,0:T(8,128)(2,1)S(1)}, u32[]{:S(2)}, u32[]{:S(2)}) async-start(bf16[32,16,1024]{2,1,0:T(8,128)(2,1)} %bitcast.11), calls=%async_computation.1 | async-start | bytes 2097152 | tf_op jit(solution)/shard_map/all_to_all | solution.py:109
  215.7 0.0 copy-start.2
  215.7 39.5 %all-gather.10.cloned.1.call-done = bf16[1536,1024]{1,0:T(8,128)(2,1)} async-done(((bf16[1536,128]{1,0:T(8,128)(2,1)}), bf16[1536,1024]{1,0:T(8,128)(2,1)}) %all-gather.10.cloned.1.call-update) | async-done | bytes 3145744 | tf_op jit(solution)/shard_map/all_gather | solution.py:76
  255.2 5.2 %convolution_convert_fusion.3 = bf16[512,1024]{1,0:T(8,128)(2,1)} fusion(bf16[512,1536]{1,0:T(8,128)(2,1)} %copy-done.3, bf16[1536,1024]{1,0:T(8,128)(2,1)} %all-gather.10.cloned.1.call-done), kind=kOutput, calls=%fused_computation.4 | convolution fusion | flops 1611137024 | bytes 5767168 | tf_op jit(solution)/shard_map/dot_general | solution.py:107
  260.4 0.0 all-to-all-done.1
  260.4 10.9 %all-to-all-start.2 = ((bf16[32,16,1024]{2,1,0:T(8,128)(2,1)}), bf16[32,16,1024]{2,1,0:T(8,128)(2,1)S(1)}, u32[]{:S(2)}, u32[]{:S(2)}) async-start(bf16[32,16,1024]{2,1,0:T(8,128)(2,1)} %bitcast.13), calls=%async_computation.2 | async-start | bytes 2097152 | tf_op jit(solution)/shard_map/all_to_all | solution.py:109
  271.3 0.0 copy-done.2
  271.3 0.1 copy.14
  271.4 0.1 select_reduce_fusion
  271.5 38.5 %all-gather.12.cloned.1.call-done = bf16[1536,1024]{1,0:T(8,128)(2,1)} async-done(((bf16[1536,128]{1,0:T(8,128)(2,1)}), bf16[1536,1024]{1,0:T(8,128)(2,1)}) %all-gather.12.cloned.1.call-update) | async-done | bytes 3145744 | tf_op jit(solution)/shard_map/all_gather | solution.py:76
  310.0 5.1 %convolution_convert_fusion.2 = bf16[512,1024]{1,0:T(8,128)(2,1)} fusion(bf16[512,1536]{1,0:T(8,128)(2,1)} %copy-done.3, bf16[1536,1024]{1,0:T(8,128)(2,1)} %all-gather.12.cloned.1.call-done), kind=kOutput, calls=%fused_computation.3 | convolution fusion | flops 1611137024 | bytes 5767168 | tf_op jit(solution)/shard_map/dot_general | solution.py:107
  315.2 0.0 all-to-all-done.2
  315.2 10.9 %all-to-all-start.3 = ((bf16[32,16,1024]{2,1,0:T(8,128)(2,1)}), bf16[32,16,1024]{2,1,0:T(8,128)(2,1)S(1)}, u32[]{:S(2)}, u32[]{:S(2)}) async-start(bf16[32,16,1024]{2,1,0:T(8,128)(2,1)} %bitcast.76), calls=%async_computation.3 | async-start | bytes 2097152 | tf_op jit(solution)/shard_map/all_to_all | solution.py:109
  326.0 0.1 copy.15
  326.1 0.1 copy.16
  326.2 0.1 eq.57
  326.3 0.1 fusion.3
  326.5 0.1 pad_maximum_fusion.1
  326.6 38.2 %all-gather.14.cloned.1.call-done = bf16[1536,1024]{1,0:T(8,128)(2,1)} async-done(((bf16[1536,128]{1,0:T(8,128)(2,1)}), bf16[1536,1024]{1,0:T(8,128)(2,1)}) %all-gather.14.cloned.1.call-update) | async-done | bytes 3145744 | tf_op jit(solution)/shard_map/all_gather | solution.py:76
  364.8 5.1 %convolution_convert_fusion.1 = bf16[512,1024]{1,0:T(8,128)(2,1)} fusion(bf16[512,1536]{1,0:T(8,128)(2,1)} %copy-done.3, bf16[1536,1024]{1,0:T(8,128)(2,1)} %all-gather.14.cloned.1.call-done), kind=kOutput, calls=%fused_computation.2 | convolution fusion | flops 1611137024 | bytes 5767168 | tf_op jit(solution)/shard_map/dot_general | solution.py:107
  369.9 1.0 fusion.20
  371.0 0.0 all-to-all-done.3
  371.0 10.9 %all-to-all-start.4 = ((bf16[32,16,1024]{2,1,0:T(8,128)(2,1)}), bf16[32,16,1024]{2,1,0:T(8,128)(2,1)S(1)}, u32[]{:S(2)}, u32[]{:S(2)}) async-start(bf16[32,16,1024]{2,1,0:T(8,128)(2,1)} %bitcast.77), calls=%async_computation.4 | async-start | bytes 2097152 | tf_op jit(solution)/shard_map/all_to_all | solution.py:109
  381.8 1.0 fusion.9
  382.8 0.6 copy.18
  383.4 0.3 fusion.21
  383.8 0.0 copy-start.1
  383.8 0.3 fusion.22
  384.2 14.5 %all-to-all-done.4 = bf16[32,16,1024]{2,1,0:T(8,128)(2,1)S(1)} async-done(((bf16[32,16,1024]{2,1,0:T(8,128)(2,1)}), bf16[32,16,1024]{2,1,0:T(8,128)(2,1)S(1)}, u32[]{:S(2)}, u32[]{:S(2)}) %all-to-all-start.4) | async-done | bytes 1048608 | tf_op jit(solution)/shard_map/all_to_all | solution.py:109
  398.7 0.3 fusion.23
  399.1 0.0 copy-done.1
  399.2 0.2 copy.17
  399.4 0.9 reshape.113
  (11 shorter events, 0.2 us)
Async XLA Ops:
  6.5 11.3 %copy-start = (bf16[1,1,32,4096]{3,2,1,0:T(8,128)(2,1)S(1)}, bf16[1,1,32,4096]{3,2,1,0:T(8,128)(2,1)}, u32[]{:S(2)}) copy-start(bf16[1,1,32,4096]{3,2,1,0:T(8,128)(2,1)} %param.5) | copy-start | bytes 786436
  6.5 141.8 %all-gather.6.cloned.1.call-start = ((), (), s32[]{:S(2)}) async-start(), calls=%async_computation.5 | async-start | bytes 14155776 | tf_op jit(solution)/shard_map/all_gather | solution.py:74
  10.9 189.2 %all-gather.8.cloned.1.call-start = ((), (), s32[]{:S(2)}) async-start(), calls=%async_computation.6 | async-start | bytes 3538944 | tf_op jit(solution)/shard_map/all_gather | solution.py:76
  15.2 240.0 %all-gather.10.cloned.1.call-start = ((), (), s32[]{:S(2)}) async-start(), calls=%async_computation.7 | async-start | bytes 3538944 | tf_op jit(solution)/shard_map/all_gather | solution.py:76
  15.9 294.1 %all-gather.12.cloned.1.call-start = ((), (), s32[]{:S(2)}) async-start(), calls=%async_computation.8 | async-start | bytes 3538944 | tf_op jit(solution)/shard_map/all_gather | solution.py:76
  21.0 60.9 %all-to-all-start = ((bf16[32,16,4096]{2,1,0:T(8,128)(2,1)}), bf16[32,16,4096]{2,1,0:T(8,128)(2,1)}, u32[]{:S(2)}, u32[]{:S(2)}) async-start(bf16[32,16,4096]{2,1,0:T(8,128)(2,1)} %bitcast.69), calls=%async_computation | async-start | bytes 8388608 | tf_op jit(solution)/shard_map/all_to_all | solution.py:99
  29.6 335.2 %all-gather.14.cloned.1.call-start = ((), (), s32[]{:S(2)}) async-start(), calls=%async_computation.9 | async-start | bytes 3538944 | tf_op jit(solution)/shard_map/all_gather | solution.py:76
  159.5 45.3 %copy-start.3 = (bf16[512,1536]{1,0:T(8,128)(2,1)}, bf16[512,1536]{1,0:T(8,128)(2,1)S(1)}, u32[]{:S(2)}) copy-start(bf16[512,1536]{1,0:T(8,128)(2,1)S(1)} %multiply_convert_fusion) | copy-start | bytes 4718596
  204.8 55.6 %all-to-all-start.1 = ((bf16[32,16,1024]{2,1,0:T(8,128)(2,1)}), bf16[32,16,1024]{2,1,0:T(8,128)(2,1)S(1)}, u32[]{:S(2)}, u32[]{:S(2)}) async-start(bf16[32,16,1024]{2,1,0:T(8,128)(2,1)} %bitcast.11), calls=%async_computation.1 | async-start | bytes 2097152 | tf_op jit(solution)/shard_map/all_to_all | solution.py:109
  215.7 55.6 %copy-start.2 = (f32[1,1,32,8]{2,3,1,0:T(8,128)S(1)}, f32[1,1,32,8]{2,3,1,0:T(8,128)}, u32[]{:S(2)}) copy-start(f32[1,1,32,8]{2,3,1,0:T(8,128)} %param.6) | copy-start | bytes 3076
  260.4 54.8 %all-to-all-start.2 = ((bf16[32,16,1024]{2,1,0:T(8,128)(2,1)}), bf16[32,16,1024]{2,1,0:T(8,128)(2,1)S(1)}, u32[]{:S(2)}, u32[]{:S(2)}) async-start(bf16[32,16,1024]{2,1,0:T(8,128)(2,1)} %bitcast.13), calls=%async_computation.2 | async-start | bytes 2097152 | tf_op jit(solution)/shard_map/all_to_all | solution.py:109
  315.2 55.8 %all-to-all-start.3 = ((bf16[32,16,1024]{2,1,0:T(8,128)(2,1)}), bf16[32,16,1024]{2,1,0:T(8,128)(2,1)S(1)}, u32[]{:S(2)}, u32[]{:S(2)}) async-start(bf16[32,16,1024]{2,1,0:T(8,128)(2,1)} %bitcast.76), calls=%async_computation.3 | async-start | bytes 2097152 | tf_op jit(solution)/shard_map/all_to_all | solution.py:109
  371.0 27.8 %all-to-all-start.4 = ((bf16[32,16,1024]{2,1,0:T(8,128)(2,1)}), bf16[32,16,1024]{2,1,0:T(8,128)(2,1)S(1)}, u32[]{:S(2)}, u32[]{:S(2)}) async-start(bf16[32,16,1024]{2,1,0:T(8,128)(2,1)} %bitcast.77), calls=%async_computation.4 | async-start | bytes 2097152 | tf_op jit(solution)/shard_map/all_to_all | solution.py:109
  383.8 15.3 %copy-start.1 = (bf16[4,8,8,128]{3,2,1,0:T(8,128)(2,1)S(1)}, bf16[4,8,8,128]{3,2,1,0:T(8,128)(2,1)}, u32[]{:S(2)}) copy-start(bf16[4,8,8,128]{3,2,1,0:T(8,128)(2,1)} %copy.18) | copy-start | bytes 196612
Sparse Core Ops, SparseCore 0:
  11.0 137.2 all-gather.5
  150.0 50.0 all-gather.7
  201.9 53.2 all-gather.9
  256.8 53.2 all-gather.11
  311.6 53.1 all-gather.13

commit v2 on v1

v2 whole, which is shorter than its diff:
```python
import jax
import jax.numpy as jnp
from jax import lax
from jax.experimental import pallas as pl
from jax.experimental.pallas import tpu as pltpu
from jax.sharding import PartitionSpec as P

E = 32
BLK = 128
CAP = 16
UP_GROUPS = ((0, 1, 2, 3), (4, 5), (6, 7))
DOWN_GROUPS = ((0, 1), (2, 3), (4, 5), (6, 7))
LIGHT = pl.CostEstimate(flops=2_000_000_000, bytes_accessed=4_000_000, transcendentals=0)
VMEM = 56 * 1024 * 1024
UNREAD = pl.BlockSpec(memory_space=pl.ANY)


def coded_block(entries):
    largest = jnp.max(jnp.max(jnp.abs(entries), axis=0, keepdims=True), axis=1, keepdims=True)
    scale = (largest / 448.0 + 1e-06).astype(jnp.bfloat16).astype(jnp.float32)
    coded = (entries / scale).astype(jnp.bfloat16)
    return (coded.astype(jnp.float32) * scale).astype(jnp.bfloat16)


def requantize_kernel(master_ref, *refs):
    out_refs = refs[-2:]
    width = out_refs[0].shape[1]
    for column in range(0, master_ref.shape[1], BLK):
        place = column % width
        for row in range(0, master_ref.shape[0], BLK):
            out_refs[column // width][row:row + BLK, place:place + BLK] = coded_block(
                master_ref[row:row + BLK, column:column + BLK]
            )


def requantize(master, step, name, after=()):
    height, width = master.shape
    return pl.pallas_call(
        requantize_kernel,
        grid=(height // step,),
        in_specs=[pl.BlockSpec((step, width), lambda i: (i, 0))] + [UNREAD] * len(after),
        out_specs=[pl.BlockSpec((step, width // 2), lambda i: (i, 0))] * 2,
        out_shape=[jax.ShapeDtypeStruct((height, width // 2), jnp.bfloat16)] * 2,
        cost_estimate=LIGHT,
        name=name,
    )(master, *after)


def silu(total):
    return total / (1.0 + jnp.exp(-total))


def up_kernel(steps, size, place_ref, *refs):
    out_ref = refs[-1]
    count = 2 * len(steps)
    rows, weights = refs[:count], refs[count:2 * count]
    part = weights[0].shape[1]
    for side in range(2):
        place = slice(side * part, (side + 1) * part)
        total = None if steps[0] == 0 else refs[2 * count][:, place]
        for index in range(side, count, 2):
            product = jnp.dot(
                rows[index][...], weights[index][...], preferred_element_type=jnp.float32
            )
            total = product if total is None else total + product
        if steps[-1] == size - 1:
            total = silu(total)
        out_ref[:, place] = total.astype(out_ref.dtype)


def up_step(here, rows, slices, total, steps, size, after=()):
    parts = [part for one in slices for part in one]
    if total is not None:
        parts.append(total)
    count, depth = rows.shape[0], rows.shape[1] // size
    width = 2 * parts[0].shape[1]
    last = steps[-1] == size - 1
    whole = lambda shape: pl.BlockSpec(shape, lambda i, place: (0, 0))
    block = lambda offset: pl.BlockSpec(
        (count, depth), lambda i, place: (0, lax.rem(place[0] + offset, size))
    )
    blocks = [block(size + sign * step) for step in steps for sign in (-1, 1)]
    return pl.pallas_call(
        lambda *refs: up_kernel(steps, size, *refs),
        grid_spec=pltpu.PrefetchScalarGridSpec(
            num_scalar_prefetch=1,
            grid=(1,),
            in_specs=blocks + [whole(part.shape) for part in parts] + [UNREAD] * len(after),
            out_specs=whole((count, width)),
        ),
        out_shape=jax.ShapeDtypeStruct((count, width), jnp.bfloat16 if last else jnp.float32),
        compiler_params=pltpu.CompilerParams(vmem_limit_bytes=VMEM),
        cost_estimate=LIGHT,
        name="up_step",
    )(here.reshape(1), *[rows] * len(blocks), *parts, *after)


def down_kernel(count, hidden_ref, *refs):
    out_ref = refs[-1]
    part = refs[0].shape[1]
    for index in range(count):
        out_ref[:, index * part:(index + 1) * part] = jnp.dot(
            hidden_ref[...], refs[index][...], preferred_element_type=jnp.float32
        ).astype(out_ref.dtype)


def down_step(hidden, slices, after=()):
    parts = [part for one in slices for part in one]
    count = hidden.shape[0]
    width = sum(part.shape[1] for part in parts)
    whole = lambda shape: pl.BlockSpec(shape, lambda i: (0, 0))
    return pl.pallas_call(
        lambda *refs: down_kernel(len(parts), *refs),
        grid=(1,),
        in_specs=[whole(part.shape) for part in (hidden, *parts)] + [UNREAD] * len(after),
        out_specs=whole((count, width)),
        out_shape=jax.ShapeDtypeStruct((count, width), jnp.bfloat16),
        compiler_params=pltpu.CompilerParams(vmem_limit_bytes=VMEM),
        cost_estimate=LIGHT,
        name="down_step",
    )(hidden, *parts, *after)


def wait_for(parts, after):
    return [lax.optimization_barrier((part, *after))[0] for part in parts] if after else parts


def shift(parts):
    size = lax.axis_size("grp")
    right = [(i, (i + 1) % size) for i in range(size)]
    left = [(i, (i - 1) % size) for i in range(size)]
    return [lax.ppermute(part, "grp", way) for part, way in zip(parts, (right, left))]


def advance(held, *beside):
    now, beside = lax.optimization_barrier((shift(held[-1]), beside))
    held.append(now)
    return beside


def local(tokens, gates, routes, master_up, master_down):
    tokens = tokens[0, 0]
    gates = gates[0, 0]
    routes = routes[0, 0]
    ep_count = lax.axis_size("ep")
    size = lax.axis_size("grp")
    tok_dev, width = tokens.shape
    slot_total = ep_count * CAP
    here = lax.axis_index("grp").astype(jnp.int32)

    everyone = lax.all_gather(tokens, "ep", axis=0, tiled=True)

    up = [requantize(master_up[0], BLK, "requantize_up")]
    advance(up)

    own_routes = lax.dynamic_slice_in_dim(routes, lax.axis_index("ep") * tok_dev, tok_dev, 0)
    named = own_routes[:, :, None] == jnp.arange(E, dtype=jnp.int32)
    mask = jnp.any(named, axis=1)
    gate_of = jnp.sum(jnp.where(named, gates[:, :, None], 0.0), axis=1)
    earlier = jnp.tril(jnp.ones((tok_dev, tok_dev), jnp.bfloat16), -1)
    rank = jnp.dot(earlier, mask.astype(jnp.bfloat16), preferred_element_type=jnp.float32)
    rank = jnp.where(mask, rank.astype(jnp.int32), -1)
    in_slot = rank[:, :, None] == jnp.arange(CAP, dtype=jnp.int32)
    gate_hi = gate_of.astype(jnp.bfloat16)
    gate_lo = (gate_of - gate_hi.astype(jnp.float32)).astype(jnp.bfloat16)
    weigh = jnp.concatenate(
        [
            jnp.where(in_slot, part[:, :, None], 0.0).astype(jnp.bfloat16).reshape(tok_dev, slot_total)
            for part in (gate_hi, gate_lo)
        ],
        axis=0,
    )

    own = lax.axis_index("ep").astype(jnp.int32)
    asks = jnp.any(routes == own, axis=1).reshape(ep_count, tok_dev)
    ahead = jnp.triu(jnp.ones((tok_dev, tok_dev), jnp.bfloat16), 1)
    slot = jnp.dot(asks.astype(jnp.bfloat16), ahead, preferred_element_type=jnp.float32)
    slot = slot.astype(jnp.int32) + CAP * jnp.arange(ep_count, dtype=jnp.int32)[:, None]
    slot = jnp.where(asks, slot, -1).reshape(1, ep_count * tok_dev)
    take = (slot == jnp.arange(slot_total, dtype=jnp.int32)[:, None]).astype(jnp.bfloat16)

    down = [requantize(master_down[0], 3 * BLK, "requantize_down", up[1][:1])]
    (down[0],) = advance(up, down[0])
    advance(up)
    advance(up)
    rows = jnp.dot(
        wait_for([take], up[4][:1])[0], everyone, preferred_element_type=jnp.float32
    ).astype(jnp.bfloat16)
    (rows,) = advance(up, rows)

    def send_back(answer):
        part = answer.shape[1]
        return lax.all_to_all(
            answer.reshape(ep_count, CAP, part), "ep", split_axis=0, concat_axis=0, tiled=True
        ).reshape(slot_total, part)

    def mix(back, after):
        both = jnp.dot(wait_for([weigh], after)[0], back, preferred_element_type=jnp.float32)
        return (both[:tok_dev] + both[tok_dev:]).astype(jnp.bfloat16)

    def add_up(steps, total):
        return up_step(here, rows, [up[step] for step in steps], total, steps, size)

    def answers(steps):
        return down_step(hidden, [down[step] for step in steps])

    (total,) = advance(up, add_up(UP_GROUPS[0], None))
    total, down[0] = advance(up, add_up(UP_GROUPS[1], total), down[0])
    (hidden,) = advance(down, add_up(UP_GROUPS[2], total))
    (first,) = advance(down, answers(DOWN_GROUPS[0]))
    back = send_back(first)
    advance(down)
    second, back = advance(down, answers(DOWN_GROUPS[1]), back)
    backs = [back]
    back = send_back(second)
    advance(down)
    third, back = advance(down, answers(DOWN_GROUPS[2]), back)
    backs.append(back)
    backs.append(send_back(third))
    advance(down)
    backs.append(send_back(answers(DOWN_GROUPS[3])))
    mixed = [mix(back, ()) for back in backs]

    half = width // size // 2
    out = jnp.zeros((tok_dev, width), jnp.bfloat16)
    for steps, piece in zip(DOWN_GROUPS, mixed):
        for turn, step in enumerate(steps):
            for side, sign in enumerate((-1, 1)):
                start = (2 * turn + side) * half
                source = lax.rem(here + sign * step + size, size)
                out = lax.dynamic_update_slice(
                    out, piece[:, start:start + half], (0, (2 * source + side) * half)
                )
    return out[None, None]


def solution(mesh):
    placed = (
        P("grp", None, "ep", None),
        P("grp", None, "ep", None),
        P("grp", None, None, None),
        P("ep", "grp", None),
        P("ep", None, "grp"),
    )
    return jax.shard_map(
        local, mesh=mesh, in_specs=placed, out_specs=P("grp", None, "ep", None), check_vma=False
    )
```

time: 408 us -> 323 us (0.79)
  waiting for transfers between devices: 291 us -> 137 us
  starting transfers between devices: 52.3 us -> 100 us
  Pallas kernels: 8.57 us -> 51.6 us
  matrix products: 36.6 us -> 11 us
    all_gather x5 -> x1, waiting for transfers between devices: 223 us -> 0.01 us  [local(): everyone = lax.all_gather(tokens, 'ep', axis=0, tiled=True)]
    ppermute x0 -> x28, waiting for transfers between devices: none -> 95.4 us  [shift(): lax.ppermute(part, 'grp', way)]
    ppermute x0 -> x28, starting transfers between devices: none -> 51.4 us  [shift(): lax.ppermute(part, 'grp', way)]
    pallas_call x2 -> x9, Pallas kernels: 8.57 us -> 51.6 us  [the longest x3 22.8 us: up_step(): pl.pallas_call(lambda *refs: up_kernel(steps, size, *refs), grid_spec=plt...]
    dot_general x10 -> x6, matrix products: 36.4 us -> 10.8 us  [the longest x1 9.49 us: local(): jnp.dot(wait_for([take], up[4][:1])[0], everyone, preferred_element_type=...]
    all_to_all x5 -> x4, waiting for transfers between devices: 66.2 us -> 41.3 us  [send_back(): lax.all_to_all(answer.reshape(ep_count, CAP, part), 'ep', split_axis=0, c...]
    all_to_all x5 -> x4, starting transfers between devices: 52.2 us -> 48.7 us  [send_back(): lax.all_to_all(answer.reshape(ep_count, CAP, part), 'ep', split_axis=0, c...]
  transfers between devices with their start and end apart: 10 -> 33, of which waited for: 7 -> 16; matrix products, arithmetic and copies ran while one was open for 10% -> 4% of each run, Pallas kernels for 1% -> 16%
where the time goes in v2:
time: 323 us; the launch traced here: 318 us
  waiting for transfers between devices  137 us (42%)
  starting transfers between devices  100 us (31%)
  Pallas kernels  51.6 us (16%)
  between operations  14.1 us (4%)
  matrix products  11 us (3%)
    ppermute x28, waiting for transfers between devices, shift(): lax.ppermute(part, 'grp', way)  95.4 us
    ppermute x28, starting transfers between devices, shift(): lax.ppermute(part, 'grp', way)  51.4 us
    all_to_all x4, starting transfers between devices, send_back(): lax.all_to_all(answer.reshape(ep_count, CAP, part), 'ep', split_axis=0, c...  48.7 us
    all_to_all x4, waiting for transfers between devices, send_back(): lax.all_to_all(answer.reshape(ep_count, CAP, part), 'ep', split_axis=0, c...  41.3 us
    pallas_call x3, Pallas kernels, up_step(): pl.pallas_call(lambda *refs: up_kernel(steps, size, *refs), grid_spec=plt...  22.8 us
    pallas_call x4, Pallas kernels, down_step(): pl.pallas_call(lambda *refs: down_kernel(len(parts), *refs), grid=(1,), i...  20.4 us
    dot_general x1, matrix products, local(): jnp.dot(wait_for([take], up[4][:1])[0], everyone, preferred_element_type=...  9.49 us
    pallas_call x2, Pallas kernels, requantize(): pl.pallas_call(requantize_kernel, grid=(height // step,), in_specs=[pl.Bl...  8.43 us
  transfers between devices with their start and end apart: 33, of which 16 were waited for; matrix products, arithmetic and copies ran while one was open for 4% of the time, Pallas kernels for 16%

profile of v2, /device:TPU:1, one launch (start us, length us, event | category | flops | bytes accessed | tf_op | source)
XLA Modules:
  0.0 318.4 jit_solution(14110688832970628238)
XLA Ops:
  6.5 0.7 all-gather.3.cloned.1.call-update
  7.3 4.2 %requantize_up.1 = (bf16[512,768]{1,0:T(8,128)(2,1)}, bf16[512,768]{1,0:T(8,128)(2,1)}) custom-call(f32[512,1536]{1,0:T(8,128)} %bitcast.113), custom_call_target="tpu_custom_call" | custom-call | flops 2000000000 | bytes 4000000 | tf_op jit(solution)/shard_map/requantize_up/pallas_call | solution.py:38
  11.5 2.5 collective-permute-start
  13.9 4.0 %collective-permute-start.1 = (bf16[512,768]{1,0:T(8,128)(2,1)}, bf16[512,768]{1,0:T(8,128)(2,1)S(1)}, u32[]{:S(2)}, u32[]{:S(2)}) collective-permute-start(bf16[512,768]{1,0:T(8,128)(2,1)} %get-tuple-element.52.refs_10_), channel_id=1, source_target_pairs={{0,224},{32,0},{64,32},{96,64},{128,96},{160,128},{192,160},{224,1... | collective-permute-start | bytes 2359304 | tf_op jit(solution)/shard_map/ppermute | solution.py:132
  17.9 17.4 %collective-permute-done.refs_0_.refs_11_ = bf16[512,768]{1,0:T(8,128)(2,1)S(1)} collective-permute-done((bf16[512,768]{1,0:T(8,128)(2,1)}, bf16[512,768]{1,0:T(8,128)(2,1)S(1)}, u32[]{:S(2)}, u32[]{:S(2)}) %collective-permute-start) | collective-permute-done | bytes 786464 | tf_op jit(solution)/shard_map/ppermute | solution.py:132
  35.4 2.7 collective-permute-start.3
  38.1 4.2 %requantize_down.1 = (bf16[1536,256]{1,0:T(8,128)(2,1)}, bf16[1536,256]{1,0:T(8,128)(2,1)}) custom-call(f32[1536,512]{1,0:T(8,128)} %bitcast.114, bf16[512,768]{1,0:T(8,128)(2,1)} %copy-done.3), custom_call_target="tpu_custom_call" | custom-call | flops 2000000000 | bytes 4000000 | tf_op jit(solution)/shard_map/requantize_down/pallas_call | solution.py:38
  42.3 12.2 %collective-permute-done.2.refs_13_ = bf16[512,768]{1,0:T(8,128)(2,1)S(1)} collective-permute-done((bf16[512,768]{1,0:T(8,128)(2,1)S(1)}, bf16[512,768]{1,0:T(8,128)(2,1)S(1)}, u32[]{:S(2)}, u32[]{:S(2)}) %collective-permute-start.2) | collective-permute-done | bytes 786464 | tf_op jit(solution)/shard_map/ppermute | solution.py:132
  54.6 1.0 collective-permute-start.4
  55.6 1.7 collective-permute-start.5
  57.3 15.6 %collective-permute-done.4.refs_15_ = bf16[512,768]{1,0:T(8,128)(2,1)} collective-permute-done((bf16[512,768]{1,0:T(8,128)(2,1)S(1)}, bf16[512,768]{1,0:T(8,128)(2,1)}, u32[]{:S(2)}, u32[]{:S(2)}) %collective-permute-start.4) | collective-permute-done | bytes 786464 | tf_op jit(solution)/shard_map/ppermute | solution.py:132
  72.9 0.3 collective-permute-start.6
  73.3 2.4 collective-permute-start.7
  76.0 0.3 fusion.5
  76.3 14.2 %collective-permute-done.6.refs_5_ = bf16[512,768]{1,0:T(8,128)(2,1)S(1)} collective-permute-done((bf16[512,768]{1,0:T(8,128)(2,1)}, bf16[512,768]{1,0:T(8,128)(2,1)S(1)}, u32[]{:S(2)}, u32[]{:S(2)}) %collective-permute-start.6) | collective-permute-done | bytes 786464 | tf_op jit(solution)/shard_map/ppermute | solution.py:132
  90.6 2.7 collective-permute-start.9
  93.3 9.5 %fusion.2.refs_1_.refs_2_.refs_3_.refs_4_.refs_5_.refs_6_.refs_7_.refs_8_ = bf16[512,4096]{1,0:T(8,128)(2,1)} fusion(bf16[512,1024]{1,0:T(8,128)(2,1)S(1)} %fusion.5, bf16[1,1,1024,4096]{3,2,1,0:T(8,128)(2,1)} %all-gather.3.cloned.1.call-done), kind=kOutput, calls=%fused_computation.2 | convolution fusion | flops 4297064448 | bytes 13631488 | tf_op jit(solution)/shard_map/dot_general | solution.py:186
  102.8 4.2 %collective-permute-done.8.refs_7_ = bf16[512,768]{1,0:T(8,128)(2,1)S(1)} collective-permute-done((bf16[512,768]{1,0:T(8,128)(2,1)S(1)}, bf16[512,768]{1,0:T(8,128)(2,1)S(1)}, u32[]{:S(2)}, u32[]{:S(2)}) %collective-permute-start.8) | collective-permute-done | bytes 786464 | tf_op jit(solution)/shard_map/ppermute | solution.py:132
  107.0 2.9 collective-permute-start.11
  109.9 9.1 %up_step.3.refs_9_ = f32[512,1536]{1,0:T(8,128)} custom-call(s32[1]{0:T(128)} %bitcast.8.refs_0_, bf16[512,4096]{1,0:T(8,128)(2,1)} %fusion.2.refs_1_.refs_2_.refs_3_.refs_4_.refs_5_.refs_6_.refs_7_.refs_8_, bf16[512,4096]{1,0:T(8,128)(2,1)} %fusion.2.refs_1_.refs_2_.refs_3_.refs_4_.refs_5_.refs_6_.refs_7_.refs_8_, ...), custom_call_target="tpu_custom_call" | custom-call | flops 2000000000 | bytes 4000000 | tf_op jit(solution)/shard_map/up_step/pallas_call | solution.py:83
  119.0 4.0 %collective-permute-done.10.refs_5_ = bf16[512,768]{1,0:T(8,128)(2,1)S(1)} collective-permute-done((bf16[512,768]{1,0:T(8,128)(2,1)S(1)}, bf16[512,768]{1,0:T(8,128)(2,1)S(1)}, u32[]{:S(2)}, u32[]{:S(2)}) %collective-permute-start.10) | collective-permute-done | bytes 786464 | tf_op jit(solution)/shard_map/ppermute | solution.py:132
  123.1 2.7 collective-permute-start.13
  125.7 7.0 %up_step.4.refs_9_ = f32[512,1536]{1,0:T(8,128)} custom-call(s32[1]{0:T(128)} %bitcast.8.refs_0_, bf16[512,4096]{1,0:T(8,128)(2,1)} %fusion.2.refs_1_.refs_2_.refs_3_.refs_4_.refs_5_.refs_6_.refs_7_.refs_8_, bf16[512,4096]{1,0:T(8,128)(2,1)} %fusion.2.refs_1_.refs_2_.refs_3_.refs_4_.refs_5_.refs_6_.refs_7_.refs_8_, ...), custom_call_target="tpu_custom_call" | custom-call | flops 2000000000 | bytes 4000000 | tf_op jit(solution)/shard_map/up_step/pallas_call | solution.py:83
  132.7 6.3 %collective-permute-done.12.refs_7_ = bf16[512,768]{1,0:T(8,128)(2,1)S(1)} collective-permute-done((bf16[512,768]{1,0:T(8,128)(2,1)S(1)}, bf16[512,768]{1,0:T(8,128)(2,1)S(1)}, u32[]{:S(2)}, u32[]{:S(2)}) %collective-permute-start.12) | collective-permute-done | bytes 786464 | tf_op jit(solution)/shard_map/ppermute | solution.py:132
  139.1 2.7 collective-permute-start.15
  141.8 6.7 %up_step.5.refs_0_ = bf16[512,1536]{1,0:T(8,128)(2,1)} custom-call(s32[1]{0:T(128)} %bitcast.8.refs_0_, bf16[512,4096]{1,0:T(8,128)(2,1)} %fusion.2.refs_1_.refs_2_.refs_3_.refs_4_.refs_5_.refs_6_.refs_7_.refs_8_, bf16[512,4096]{1,0:T(8,128)(2,1)} %fusion.2.refs_1_.refs_2_.refs_3_.refs_4_.refs_5_.refs_6_.refs_7_.refs_8_, ...), custom_call_target="tpu_custom_call" | custom-call | flops 2000000000 | bytes 4000000 | tf_op jit(solution)/shard_map/up_step/pallas_call | solution.py:83
  148.4 6.5 %collective-permute-done.14.refs_3_ = bf16[1536,256]{1,0:T(8,128)(2,1)S(1)} collective-permute-done((bf16[1536,256]{1,0:T(8,128)(2,1)S(1)}, bf16[1536,256]{1,0:T(8,128)(2,1)S(1)}, u32[]{:S(2)}, u32[]{:S(2)}) %collective-permute-start.14) | collective-permute-done | bytes 786464 | tf_op jit(solution)/shard_map/ppermute | solution.py:132
  155.1 2.7 collective-permute-start.17
  157.7 5.1 %down_step.4 = bf16[512,1024]{1,0:T(8,128)(2,1)} custom-call(bf16[512,1536]{1,0:T(8,128)(2,1)} %up_step.5.refs_0_, bf16[1536,256]{1,0:T(8,128)(2,1)} %get-tuple-element.72.refs_1_, bf16[1536,256]{1,0:T(8,128)(2,1)} %get-tuple-element.73.refs_2_, bf16[1536,256]{1,0:T(8,128)(2,1)} %copy-done.20, bf16[1536,256]{1,0:T(8,128)(2,1)} %copy-done.21), custom_call_target="tpu_custom_call" | custom-call | flops 2000000000 | bytes 4000000 | tf_op jit(solution)/shard_map/down_step/pallas_call | solution.py:112
  162.8 8.1 %collective-permute-done.16.refs_1_ = bf16[1536,256]{1,0:T(8,128)(2,1)S(1)} collective-permute-done((bf16[1536,256]{1,0:T(8,128)(2,1)S(1)}, bf16[1536,256]{1,0:T(8,128)(2,1)S(1)}, u32[]{:S(2)}, u32[]{:S(2)}) %collective-permute-start.16) | collective-permute-done | bytes 786464 | tf_op jit(solution)/shard_map/ppermute | solution.py:132
  171.1 12.0 %collective-permute-start.19 = (bf16[1536,256]{1,0:T(8,128)(2,1)S(1)}, bf16[1536,256]{1,0:T(8,128)(2,1)}, u32[]{:S(2)}, u32[]{:S(2)}) collective-permute-start(bf16[1536,256]{1,0:T(8,128)(2,1)S(1)} %collective-permute-done.17.refs_2_), channel_id=1, source_target_pairs={{0,224},{32,0},{64,32},{96,64},{128,96},{160,128},{192,160},{224,1... | collective-permute-start | bytes 2359304 | tf_op jit(solution)/shard_map/ppermute | solution.py:132
  183.0 19.4 %all-to-all-start = ((bf16[32,16,1024]{2,1,0:T(8,128)(2,1)}), bf16[32,16,1024]{2,1,0:T(8,128)(2,1)S(1)}, u32[]{:S(2)}, u32[]{:S(2)}) async-start(bf16[32,16,1024]{2,1,0:T(8,128)(2,1)} %bitcast.108), calls=%async_computation | async-start | bytes 2097152 | tf_op jit(solution)/shard_map/all_to_all | solution.py:193
  202.8 0.1 select_reduce_fusion
  203.0 2.7 collective-permute-start.21
  205.7 0.1 copy.13
  205.9 0.1 fusion.15
  206.0 0.2 fusion.8
  206.4 0.1 fusion.10
  206.6 5.1 %down_step.5 = bf16[512,1024]{1,0:T(8,128)(2,1)} custom-call(bf16[512,1536]{1,0:T(8,128)(2,1)} %up_step.5.refs_0_, bf16[1536,256]{1,0:T(8,128)(2,1)} %copy-done.14, bf16[1536,256]{1,0:T(8,128)(2,1)} %copy-done.15, bf16[1536,256]{1,0:T(8,128)(2,1)} %collective-permute-done.18.refs_3_, bf16[1536,256]{1,0:T(8,128)(2,1)} %collective-permute-done.19.refs_4_), custom_call_target="tpu_custom_call" | custom-call | flops 2000000000 | bytes 4000000 | tf_op jit(solution)/shard_map/down_step/pallas_call | solution.py:112
  211.7 7.8 %all-to-all-done = bf16[32,16,1024]{2,1,0:T(8,128)(2,1)S(1)} async-done(((bf16[32,16,1024]{2,1,0:T(8,128)(2,1)}), bf16[32,16,1024]{2,1,0:T(8,128)(2,1)S(1)}, u32[]{:S(2)}, u32[]{:S(2)}) %all-to-all-start) | async-done | bytes 1048608 | tf_op jit(solution)/shard_map/all_to_all | solution.py:193
  219.4 1.5 collective-permute-done.20.refs_1_
  220.9 2.7 collective-permute-start.23
  223.6 0.1 pad_maximum_fusion
  223.7 11.2 %all-to-all-start.1 = ((bf16[32,16,1024]{2,1,0:T(8,128)(2,1)}), bf16[32,16,1024]{2,1,0:T(8,128)(2,1)S(1)}, u32[]{:S(2)}, u32[]{:S(2)}) async-start(bf16[32,16,1024]{2,1,0:T(8,128)(2,1)} %bitcast.109), calls=%async_computation.1 | async-start | bytes 2097152 | tf_op jit(solution)/shard_map/all_to_all | solution.py:193
  234.9 0.3 fusion.46
  235.3 2.5 collective-permute-done.22.refs_3_
  237.8 0.9 copy-done.19
  238.7 1.2 collective-permute-start.24
  239.9 1.5 collective-permute-start.25
  241.4 5.1 %down_step.6 = bf16[512,1024]{1,0:T(8,128)(2,1)} custom-call(bf16[512,1536]{1,0:T(8,128)(2,1)} %up_step.5.refs_0_, bf16[1536,256]{1,0:T(8,128)(2,1)} %collective-permute-done.20.refs_1_, bf16[1536,256]{1,0:T(8,128)(2,1)} %collective-permute-done.21.refs_2_, bf16[1536,256]{1,0:T(8,128)(2,1)} %copy-done.19, bf16[1536,256]{1,0:T(8,128)(2,1)} %collective-permute-done.23.refs_4_), custom_call_target="tpu_custom_call" | custom-call | flops 2000000000 | bytes 4000000 | tf_op jit(solution)/shard_map/down_step/pallas_call | solution.py:112
  246.5 5.3 %all-to-all-done.1 = bf16[32,16,1024]{2,1,0:T(8,128)(2,1)S(1)} async-done(((bf16[32,16,1024]{2,1,0:T(8,128)(2,1)}), bf16[32,16,1024]{2,1,0:T(8,128)(2,1)S(1)}, u32[]{:S(2)}, u32[]{:S(2)}) %all-to-all-start.1) | async-done | bytes 1048608 | tf_op jit(solution)/shard_map/all_to_all | solution.py:193
  251.8 2.9 collective-permute-done.24.refs_1_
  254.7 1.5 collective-permute-start.26
  256.2 1.2 collective-permute-start.27
  257.3 0.3 fusion.47
  257.7 14.2 %all-to-all-start.2 = ((bf16[32,16,1024]{2,1,0:T(8,128)(2,1)}), bf16[32,16,1024]{2,1,0:T(8,128)(2,1)S(1)}, u32[]{:S(2)}, u32[]{:S(2)}) async-start(bf16[32,16,1024]{2,1,0:T(8,128)(2,1)} %bitcast.110), calls=%async_computation.2 | async-start | bytes 2097152 | tf_op jit(solution)/shard_map/all_to_all | solution.py:193
  272.0 5.1 %down_step.7 = bf16[512,1024]{1,0:T(8,128)(2,1)} custom-call(bf16[512,1536]{1,0:T(8,128)(2,1)} %up_step.5.refs_0_, bf16[1536,256]{1,0:T(8,128)(2,1)} %copy-done.18, bf16[1536,256]{1,0:T(8,128)(2,1)} %collective-permute-done.25.refs_2_, bf16[1536,256]{1,0:T(8,128)(2,1)} %collective-permute-done.26.refs_3_, bf16[1536,256]{1,0:T(8,128)(2,1)} %collective-permute-done.27.refs_4_), custom_call_target="tpu_custom_call" | custom-call | flops 2000000000 | bytes 4000000 | tf_op jit(solution)/shard_map/down_step/pallas_call | solution.py:112
  277.1 11.7 %all-to-all-done.2 = bf16[32,16,1024]{2,1,0:T(8,128)(2,1)S(1)} async-done(((bf16[32,16,1024]{2,1,0:T(8,128)(2,1)}), bf16[32,16,1024]{2,1,0:T(8,128)(2,1)S(1)}, u32[]{:S(2)}, u32[]{:S(2)}) %all-to-all-start.2) | async-done | bytes 1048608 | tf_op jit(solution)/shard_map/all_to_all | solution.py:193
  288.8 4.0 %all-to-all-start.3 = ((bf16[32,16,1024]{2,1,0:T(8,128)(2,1)}), bf16[32,16,1024]{2,1,0:T(8,128)(2,1)S(1)}, u32[]{:S(2)}, u32[]{:S(2)}) async-start(bf16[32,16,1024]{2,1,0:T(8,128)(2,1)} %bitcast.111), calls=%async_computation.3 | async-start | bytes 2097152 | tf_op jit(solution)/shard_map/all_to_all | solution.py:193
  292.7 0.3 fusion.48
  293.2 16.5 %all-to-all-done.3 = bf16[32,16,1024]{2,1,0:T(8,128)(2,1)S(1)} async-done(((bf16[32,16,1024]{2,1,0:T(8,128)(2,1)}), bf16[32,16,1024]{2,1,0:T(8,128)(2,1)S(1)}, u32[]{:S(2)}, u32[]{:S(2)}) %all-to-all-start.3) | async-done | bytes 1048608 | tf_op jit(solution)/shard_map/all_to_all | solution.py:193
  309.7 0.3 fusion.49
  310.1 0.7 copy-done.11
  310.8 0.6 fusion.16
  (103 shorter events, 1.7 us)
Async XLA Ops:
  6.5 86.8 %all-gather.3.cloned.1.call-start = ((), (), s32[]{:S(2)}) async-start(), calls=%async_computation.4 | async-start | bytes 8650752 | tf_op jit(solution)/shard_map/all_gather | solution.py:151
  11.5 64.2 %copy-start.12 = (s32[1,1,1024,8]{2,3,1,0:T(8,128)S(1)}, s32[1,1,1024,8]{2,3,1,0:T(8,128)}, u32[]{:S(2)}) copy-start(s32[1,1,1024,8]{2,3,1,0:T(8,128)} %param.7) | copy-start | bytes 98308
  11.5 23.9 %collective-permute-start = (bf16[512,768]{1,0:T(8,128)(2,1)}, bf16[512,768]{1,0:T(8,128)(2,1)S(1)}, u32[]{:S(2)}, u32[]{:S(2)}) collective-permute-start(bf16[512,768]{1,0:T(8,128)(2,1)} %get-tuple-element.51.refs_9_), channel_id=1, source_target_pairs={{0,32},{32,64},{64,96},{96,128},{128,160},{160,192},{192,224},{224... | collective-permute-start | bytes 2359304 | tf_op jit(solution)/shard_map/ppermute | solution.py:132
  13.9 21.4 %collective-permute-start.1 = (bf16[512,768]{1,0:T(8,128)(2,1)}, bf16[512,768]{1,0:T(8,128)(2,1)S(1)}, u32[]{:S(2)}, u32[]{:S(2)}) collective-permute-start(bf16[512,768]{1,0:T(8,128)(2,1)} %get-tuple-element.52.refs_10_), channel_id=1, source_target_pairs={{0,224},{32,0},{64,32},{96,64},{128,96},{160,128},{192,160},{224,1... | collective-permute-start | bytes 2359304 | tf_op jit(solution)/shard_map/ppermute | solution.py:132
  35.3 2.8 copy-start.3
  35.4 37.6 %copy-start.4 = (bf16[512,768]{1,0:T(8,128)(2,1)}, bf16[512,768]{1,0:T(8,128)(2,1)S(1)}, u32[]{:S(2)}) copy-start(bf16[512,768]{1,0:T(8,128)(2,1)S(1)} %collective-permute-done.1.refs_12_) | copy-start | bytes 2359300
  35.4 19.2 %collective-permute-start.2 = (bf16[512,768]{1,0:T(8,128)(2,1)S(1)}, bf16[512,768]{1,0:T(8,128)(2,1)S(1)}, u32[]{:S(2)}, u32[]{:S(2)}) collective-permute-start(bf16[512,768]{1,0:T(8,128)(2,1)S(1)} %collective-permute-done.refs_0_.refs_11_), channel_id=1, source_target_pairs={{0,32},{32,64},{64,96},{96,128},{128,160},{160,192},{192,224},{224... | collective-permute-start | bytes 2359304 | tf_op jit(solution)/shard_map/ppermute | solution.py:132
  35.4 19.1 %collective-permute-start.3 = (bf16[512,768]{1,0:T(8,128)(2,1)S(1)}, bf16[512,768]{1,0:T(8,128)(2,1)S(1)}, u32[]{:S(2)}, u32[]{:S(2)}) collective-permute-start(bf16[512,768]{1,0:T(8,128)(2,1)S(1)} %collective-permute-done.1.refs_12_), channel_id=1, source_target_pairs={{0,224},{32,0},{64,32},{96,64},{128,96},{160,128},{192,160},{224,1... | collective-permute-start | bytes 2359304 | tf_op jit(solution)/shard_map/ppermute | solution.py:132
  54.5 18.4 %copy-start.5 = (bf16[512,768]{1,0:T(8,128)(2,1)}, bf16[512,768]{1,0:T(8,128)(2,1)S(1)}, u32[]{:S(2)}) copy-start(bf16[512,768]{1,0:T(8,128)(2,1)S(1)} %collective-permute-done.2.refs_13_) | copy-start | bytes 2359300
  54.6 36.0 %copy-start.6 = (bf16[512,768]{1,0:T(8,128)(2,1)}, bf16[512,768]{1,0:T(8,128)(2,1)S(1)}, u32[]{:S(2)}) copy-start(bf16[512,768]{1,0:T(8,128)(2,1)S(1)} %collective-permute-done.3.refs_14_) | copy-start | bytes 2359300
  54.6 18.4 %collective-permute-start.4 = (bf16[512,768]{1,0:T(8,128)(2,1)S(1)}, bf16[512,768]{1,0:T(8,128)(2,1)}, u32[]{:S(2)}, u32[]{:S(2)}) collective-permute-start(bf16[512,768]{1,0:T(8,128)(2,1)S(1)} %collective-permute-done.2.refs_13_), channel_id=1, source_target_pairs={{0,32},{32,64},{64,96},{96,128},{128,160},{160,192},{192,224},{224... | collective-permute-start | bytes 2359304 | tf_op jit(solution)/shard_map/ppermute | solution.py:132
  55.6 17.3 %collective-permute-start.5 = (bf16[512,768]{1,0:T(8,128)(2,1)S(1)}, bf16[512,768]{1,0:T(8,128)(2,1)}, u32[]{:S(2)}, u32[]{:S(2)}) collective-permute-start(bf16[512,768]{1,0:T(8,128)(2,1)S(1)} %collective-permute-done.3.refs_14_), channel_id=1, source_target_pairs={{0,224},{32,0},{64,32},{96,64},{128,96},{160,128},{192,160},{224,1... | collective-permute-start | bytes 2359304 | tf_op jit(solution)/shard_map/ppermute | solution.py:132
  72.9 17.6 %collective-permute-start.6 = (bf16[512,768]{1,0:T(8,128)(2,1)}, bf16[512,768]{1,0:T(8,128)(2,1)S(1)}, u32[]{:S(2)}, u32[]{:S(2)}) collective-permute-start(bf16[512,768]{1,0:T(8,128)(2,1)} %collective-permute-done.4.refs_15_), channel_id=1, source_target_pairs={{0,32},{32,64},{64,96},{96,128},{128,160},{160,192},{192,224},{224... | collective-permute-start | bytes 2359304 | tf_op jit(solution)/shard_map/ppermute | solution.py:132
  73.3 17.2 %collective-permute-start.7 = (bf16[512,768]{1,0:T(8,128)(2,1)}, bf16[512,768]{1,0:T(8,128)(2,1)S(1)}, u32[]{:S(2)}, u32[]{:S(2)}) collective-permute-start(bf16[512,768]{1,0:T(8,128)(2,1)} %collective-permute-done.5.refs_16_), channel_id=1, source_target_pairs={{0,224},{32,0},{64,32},{96,64},{128,96},{160,128},{192,160},{224,1... | collective-permute-start | bytes 2359304 | tf_op jit(solution)/shard_map/ppermute | solution.py:132
  90.5 12.3 %copy-start = (bf16[512,768]{1,0:T(8,128)(2,1)}, bf16[512,768]{1,0:T(8,128)(2,1)S(1)}, u32[]{:S(2)}) copy-start(bf16[512,768]{1,0:T(8,128)(2,1)S(1)} %collective-permute-done.6.refs_5_) | copy-start | bytes 2359300
  90.5 12.3 %copy-start.1 = (bf16[512,768]{1,0:T(8,128)(2,1)}, bf16[512,768]{1,0:T(8,128)(2,1)S(1)}, u32[]{:S(2)}) copy-start(bf16[512,768]{1,0:T(8,128)(2,1)S(1)} %collective-permute-done.7.refs_6_) | copy-start | bytes 2359300
  90.5 16.4 %collective-permute-start.8 = (bf16[512,768]{1,0:T(8,128)(2,1)S(1)}, bf16[512,768]{1,0:T(8,128)(2,1)S(1)}, u32[]{:S(2)}, u32[]{:S(2)}) collective-permute-start(bf16[512,768]{1,0:T(8,128)(2,1)S(1)} %collective-permute-done.6.refs_5_), channel_id=1, source_target_pairs={{0,32},{32,64},{64,96},{96,128},{128,160},{160,192},{192,224},{224... | collective-permute-start | bytes 2359304 | tf_op jit(solution)/shard_map/ppermute | solution.py:132
  90.6 16.3 %collective-permute-start.9 = (bf16[512,768]{1,0:T(8,128)(2,1)S(1)}, bf16[512,768]{1,0:T(8,128)(2,1)}, u32[]{:S(2)}, u32[]{:S(2)}) collective-permute-start(bf16[512,768]{1,0:T(8,128)(2,1)S(1)} %collective-permute-done.7.refs_6_), channel_id=1, source_target_pairs={{0,224},{32,0},{64,32},{96,64},{128,96},{160,128},{192,160},{224,1... | collective-permute-start | bytes 2359304 | tf_op jit(solution)/shard_map/ppermute | solution.py:132
  107.0 12.0 %copy-start.2 = (bf16[512,768]{1,0:T(8,128)(2,1)}, bf16[512,768]{1,0:T(8,128)(2,1)S(1)}, u32[]{:S(2)}) copy-start(bf16[512,768]{1,0:T(8,128)(2,1)S(1)} %collective-permute-done.8.refs_7_) | copy-start | bytes 2359300
  107.0 16.0 %collective-permute-start.10 = (bf16[512,768]{1,0:T(8,128)(2,1)S(1)}, bf16[512,768]{1,0:T(8,128)(2,1)S(1)}, u32[]{:S(2)}, u32[]{:S(2)}) collective-permute-start(bf16[512,768]{1,0:T(8,128)(2,1)S(1)} %collective-permute-done.8.refs_7_), channel_id=1, source_target_pairs={{0,32},{32,64},{64,96},{96,128},{128,160},{160,192},{192,224},{224... | collective-permute-start | bytes 2359304 | tf_op jit(solution)/shard_map/ppermute | solution.py:132
  107.0 16.0 %collective-permute-start.11 = (bf16[512,768]{1,0:T(8,128)(2,1)}, bf16[512,768]{1,0:T(8,128)(2,1)S(1)}, u32[]{:S(2)}, u32[]{:S(2)}) collective-permute-start(bf16[512,768]{1,0:T(8,128)(2,1)} %collective-permute-done.9.refs_8_), channel_id=1, source_target_pairs={{0,224},{32,0},{64,32},{96,64},{128,96},{160,128},{192,160},{224,1... | collective-permute-start | bytes 2359304 | tf_op jit(solution)/shard_map/ppermute | solution.py:132
  119.0 20.0 %copy-start.16 = (bf16[1536,256]{1,0:T(8,128)(2,1)S(1)}, bf16[1536,256]{1,0:T(8,128)(2,1)}, u32[]{:S(2)}) copy-start(bf16[1536,256]{1,0:T(8,128)(2,1)} %get-tuple-element.72.refs_1_) | copy-start | bytes 2359300
  119.0 20.1 %copy-start.17 = (bf16[1536,256]{1,0:T(8,128)(2,1)S(1)}, bf16[1536,256]{1,0:T(8,128)(2,1)}, u32[]{:S(2)}) copy-start(bf16[1536,256]{1,0:T(8,128)(2,1)} %get-tuple-element.73.refs_2_) | copy-start | bytes 2359300
  123.0 9.7 %copy-start.7 = (bf16[512,768]{1,0:T(8,128)(2,1)}, bf16[512,768]{1,0:T(8,128)(2,1)S(1)}, u32[]{:S(2)}) copy-start(bf16[512,768]{1,0:T(8,128)(2,1)S(1)} %collective-permute-done.10.refs_5_) | copy-start | bytes 2359300
  123.0 9.7 %copy-start.8 = (bf16[512,768]{1,0:T(8,128)(2,1)}, bf16[512,768]{1,0:T(8,128)(2,1)S(1)}, u32[]{:S(2)}) copy-start(bf16[512,768]{1,0:T(8,128)(2,1)S(1)} %collective-permute-done.11.refs_6_) | copy-start | bytes 2359300
  123.0 16.0 %collective-permute-start.12 = (bf16[512,768]{1,0:T(8,128)(2,1)S(1)}, bf16[512,768]{1,0:T(8,128)(2,1)S(1)}, u32[]{:S(2)}, u32[]{:S(2)}) collective-permute-start(bf16[512,768]{1,0:T(8,128)(2,1)S(1)} %collective-permute-done.10.refs_5_), channel_id=1, source_target_pairs={{0,32},{32,64},{64,96},{96,128},{128,160},{160,192},{192,224},{224... | collective-permute-start | bytes 2359304 | tf_op jit(solution)/shard_map/ppermute | solution.py:132
  123.1 15.9 %collective-permute-start.13 = (bf16[512,768]{1,0:T(8,128)(2,1)S(1)}, bf16[512,768]{1,0:T(8,128)(2,1)S(1)}, u32[]{:S(2)}, u32[]{:S(2)}) collective-permute-start(bf16[512,768]{1,0:T(8,128)(2,1)S(1)} %collective-permute-done.11.refs_6_), channel_id=1, source_target_pairs={{0,224},{32,0},{64,32},{96,64},{128,96},{160,128},{192,160},{224,1... | collective-permute-start | bytes 2359304 | tf_op jit(solution)/shard_map/ppermute | solution.py:132
  139.0 2.8 copy-start.9
  139.0 2.8 copy-start.10
  139.0 16.0 %collective-permute-start.14 = (bf16[1536,256]{1,0:T(8,128)(2,1)S(1)}, bf16[1536,256]{1,0:T(8,128)(2,1)S(1)}, u32[]{:S(2)}, u32[]{:S(2)}) collective-permute-start(bf16[1536,256]{1,0:T(8,128)(2,1)S(1)} %copy-done.16), channel_id=1, source_target_pairs={{0,32},{32,64},{64,96},{96,128},{128,160},{160,192},{192,224},{224... | collective-permute-start | bytes 2359304 | tf_op jit(solution)/shard_map/ppermute | solution.py:132
  139.1 15.9 %collective-permute-start.15 = (bf16[1536,256]{1,0:T(8,128)(2,1)S(1)}, bf16[1536,256]{1,0:T(8,128)(2,1)S(1)}, u32[]{:S(2)}, u32[]{:S(2)}) collective-permute-start(bf16[1536,256]{1,0:T(8,128)(2,1)S(1)} %copy-done.17), channel_id=1, source_target_pairs={{0,224},{32,0},{64,32},{96,64},{128,96},{160,128},{192,160},{224,1... | collective-permute-start | bytes 2359304 | tf_op jit(solution)/shard_map/ppermute | solution.py:132
  148.4 54.2 %copy-start.13 = (f32[1,1,32,8]{2,3,1,0:T(8,128)S(1)}, f32[1,1,32,8]{2,3,1,0:T(8,128)}, u32[]{:S(2)}) copy-start(f32[1,1,32,8]{2,3,1,0:T(8,128)} %param.6) | copy-start | bytes 3076
  155.0 2.8 copy-start.20
  155.0 2.8 copy-start.21
  155.0 16.0 %collective-permute-start.16 = (bf16[1536,256]{1,0:T(8,128)(2,1)S(1)}, bf16[1536,256]{1,0:T(8,128)(2,1)S(1)}, u32[]{:S(2)}, u32[]{:S(2)}) collective-permute-start(bf16[1536,256]{1,0:T(8,128)(2,1)S(1)} %collective-permute-done.14.refs_3_), channel_id=1, source_target_pairs={{0,32},{32,64},{64,96},{96,128},{128,160},{160,192},{192,224},{224... | collective-permute-start | bytes 2359304 | tf_op jit(solution)/shard_map/ppermute | solution.py:132
  155.1 15.9 %collective-permute-start.17 = (bf16[1536,256]{1,0:T(8,128)(2,1)S(1)}, bf16[1536,256]{1,0:T(8,128)(2,1)S(1)}, u32[]{:S(2)}, u32[]{:S(2)}) collective-permute-start(bf16[1536,256]{1,0:T(8,128)(2,1)S(1)} %collective-permute-done.15.refs_4_), channel_id=1, source_target_pairs={{0,224},{32,0},{64,32},{96,64},{128,96},{160,128},{192,160},{224,1... | collective-permute-start | bytes 2359304 | tf_op jit(solution)/shard_map/ppermute | solution.py:132
  171.0 35.6 %copy-start.14 = (bf16[1536,256]{1,0:T(8,128)(2,1)}, bf16[1536,256]{1,0:T(8,128)(2,1)S(1)}, u32[]{:S(2)}) copy-start(bf16[1536,256]{1,0:T(8,128)(2,1)S(1)} %collective-permute-done.16.refs_1_) | copy-start | bytes 2359300
  171.0 35.6 %copy-start.15 = (bf16[1536,256]{1,0:T(8,128)(2,1)}, bf16[1536,256]{1,0:T(8,128)(2,1)S(1)}, u32[]{:S(2)}) copy-start(bf16[1536,256]{1,0:T(8,128)(2,1)S(1)} %collective-permute-done.17.refs_2_) | copy-start | bytes 2359300
  171.0 31.9 %collective-permute-start.18 = (bf16[1536,256]{1,0:T(8,128)(2,1)S(1)}, bf16[1536,256]{1,0:T(8,128)(2,1)}, u32[]{:S(2)}, u32[]{:S(2)}) collective-permute-start(bf16[1536,256]{1,0:T(8,128)(2,1)S(1)} %collective-permute-done.16.refs_1_), channel_id=1, source_target_pairs={{0,32},{32,64},{64,96},{96,128},{128,160},{160,192},{192,224},{224... | collective-permute-start | bytes 2359304 | tf_op jit(solution)/shard_map/ppermute | solution.py:132
  171.1 31.9 %collective-permute-start.19 = (bf16[1536,256]{1,0:T(8,128)(2,1)S(1)}, bf16[1536,256]{1,0:T(8,128)(2,1)}, u32[]{:S(2)}, u32[]{:S(2)}) collective-permute-start(bf16[1536,256]{1,0:T(8,128)(2,1)S(1)} %collective-permute-done.17.refs_2_), channel_id=1, source_target_pairs={{0,224},{32,0},{64,32},{96,64},{128,96},{160,128},{192,160},{224,1... | collective-permute-start | bytes 2359304 | tf_op jit(solution)/shard_map/ppermute | solution.py:132
  183.0 36.4 %all-to-all-start = ((bf16[32,16,1024]{2,1,0:T(8,128)(2,1)}), bf16[32,16,1024]{2,1,0:T(8,128)(2,1)S(1)}, u32[]{:S(2)}, u32[]{:S(2)}) async-start(bf16[32,16,1024]{2,1,0:T(8,128)(2,1)} %bitcast.108), calls=%async_computation | async-start | bytes 2097152 | tf_op jit(solution)/shard_map/all_to_all | solution.py:193
  202.9 18.0 %collective-permute-start.20 = (bf16[1536,256]{1,0:T(8,128)(2,1)}, bf16[1536,256]{1,0:T(8,128)(2,1)}, u32[]{:S(2)}, u32[]{:S(2)}) collective-permute-start(bf16[1536,256]{1,0:T(8,128)(2,1)} %collective-permute-done.18.refs_3_), channel_id=1, source_target_pairs={{0,32},{32,64},{64,96},{96,128},{128,160},{160,192},{192,224},{224... | collective-permute-start | bytes 2359304 | tf_op jit(solution)/shard_map/ppermute | solution.py:132
  203.0 17.9 %collective-permute-start.21 = (bf16[1536,256]{1,0:T(8,128)(2,1)}, bf16[1536,256]{1,0:T(8,128)(2,1)}, u32[]{:S(2)}, u32[]{:S(2)}) collective-permute-start(bf16[1536,256]{1,0:T(8,128)(2,1)} %collective-permute-done.19.refs_4_), channel_id=1, source_target_pairs={{0,224},{32,0},{64,32},{96,64},{128,96},{160,128},{192,160},{224,1... | collective-permute-start | bytes 2359304 | tf_op jit(solution)/shard_map/ppermute | solution.py:132
  220.9 16.9 %collective-permute-start.22 = (bf16[1536,256]{1,0:T(8,128)(2,1)}, bf16[1536,256]{1,0:T(8,128)(2,1)S(1)}, u32[]{:S(2)}, u32[]{:S(2)}) collective-permute-start(bf16[1536,256]{1,0:T(8,128)(2,1)} %collective-permute-done.20.refs_1_), channel_id=1, source_target_pairs={{0,32},{32,64},{64,96},{96,128},{128,160},{160,192},{192,224},{224... | collective-permute-start | bytes 2359304 | tf_op jit(solution)/shard_map/ppermute | solution.py:132
  220.9 17.8 %collective-permute-start.23 = (bf16[1536,256]{1,0:T(8,128)(2,1)}, bf16[1536,256]{1,0:T(8,128)(2,1)}, u32[]{:S(2)}, u32[]{:S(2)}) collective-permute-start(bf16[1536,256]{1,0:T(8,128)(2,1)} %collective-permute-done.21.refs_2_), channel_id=1, source_target_pairs={{0,224},{32,0},{64,32},{96,64},{128,96},{160,128},{192,160},{224,1... | collective-permute-start | bytes 2359304 | tf_op jit(solution)/shard_map/ppermute | solution.py:132
  223.7 28.1 %all-to-all-start.1 = ((bf16[32,16,1024]{2,1,0:T(8,128)(2,1)}), bf16[32,16,1024]{2,1,0:T(8,128)(2,1)S(1)}, u32[]{:S(2)}, u32[]{:S(2)}) async-start(bf16[32,16,1024]{2,1,0:T(8,128)(2,1)} %bitcast.109), calls=%async_computation.1 | async-start | bytes 2097152 | tf_op jit(solution)/shard_map/all_to_all | solution.py:193
  237.8 0.9 copy-start.19
  238.7 16.0 %collective-permute-start.24 = (bf16[1536,256]{1,0:T(8,128)(2,1)}, bf16[1536,256]{1,0:T(8,128)(2,1)S(1)}, u32[]{:S(2)}, u32[]{:S(2)}) collective-permute-start(bf16[1536,256]{1,0:T(8,128)(2,1)} %copy-done.19), channel_id=1, source_target_pairs={{0,32},{32,64},{64,96},{96,128},{128,160},{160,192},{192,224},{224... | collective-permute-start | bytes 2359304 | tf_op jit(solution)/shard_map/ppermute | solution.py:132
  239.9 14.8 %collective-permute-start.25 = (bf16[1536,256]{1,0:T(8,128)(2,1)}, bf16[1536,256]{1,0:T(8,128)(2,1)}, u32[]{:S(2)}, u32[]{:S(2)}) collective-permute-start(bf16[1536,256]{1,0:T(8,128)(2,1)} %collective-permute-done.23.refs_4_), channel_id=1, source_target_pairs={{0,224},{32,0},{64,32},{96,64},{128,96},{160,128},{192,160},{224,1... | collective-permute-start | bytes 2359304 | tf_op jit(solution)/shard_map/ppermute | solution.py:132
  254.6 17.3 %copy-start.18 = (bf16[1536,256]{1,0:T(8,128)(2,1)}, bf16[1536,256]{1,0:T(8,128)(2,1)S(1)}, u32[]{:S(2)}) copy-start(bf16[1536,256]{1,0:T(8,128)(2,1)S(1)} %collective-permute-done.24.refs_1_) | copy-start | bytes 2359300
  254.7 17.3 %collective-permute-start.26 = (bf16[1536,256]{1,0:T(8,128)(2,1)S(1)}, bf16[1536,256]{1,0:T(8,128)(2,1)}, u32[]{:S(2)}, u32[]{:S(2)}) collective-permute-start(bf16[1536,256]{1,0:T(8,128)(2,1)S(1)} %collective-permute-done.24.refs_1_), channel_id=1, source_target_pairs={{0,32},{32,64},{64,96},{96,128},{128,160},{160,192},{192,224},{224... | collective-permute-start | bytes 2359304 | tf_op jit(solution)/shard_map/ppermute | solution.py:132
  256.2 15.8 %collective-permute-start.27 = (bf16[1536,256]{1,0:T(8,128)(2,1)}, bf16[1536,256]{1,0:T(8,128)(2,1)}, u32[]{:S(2)}, u32[]{:S(2)}) collective-permute-start(bf16[1536,256]{1,0:T(8,128)(2,1)} %collective-permute-done.25.refs_2_), channel_id=1, source_target_pairs={{0,224},{32,0},{64,32},{96,64},{128,96},{160,128},{192,160},{224,1... | collective-permute-start | bytes 2359304 | tf_op jit(solution)/shard_map/ppermute | solution.py:132
  257.7 31.1 %all-to-all-start.2 = ((bf16[32,16,1024]{2,1,0:T(8,128)(2,1)}), bf16[32,16,1024]{2,1,0:T(8,128)(2,1)S(1)}, u32[]{:S(2)}, u32[]{:S(2)}) async-start(bf16[32,16,1024]{2,1,0:T(8,128)(2,1)} %bitcast.110), calls=%async_computation.2 | async-start | bytes 2097152 | tf_op jit(solution)/shard_map/all_to_all | solution.py:193
  288.8 20.9 %all-to-all-start.3 = ((bf16[32,16,1024]{2,1,0:T(8,128)(2,1)}), bf16[32,16,1024]{2,1,0:T(8,128)(2,1)S(1)}, u32[]{:S(2)}, u32[]{:S(2)}) async-start(bf16[32,16,1024]{2,1,0:T(8,128)(2,1)} %bitcast.111), calls=%async_computation.3 | async-start | bytes 2097152 | tf_op jit(solution)/shard_map/all_to_all | solution.py:193
  310.1 0.7 copy-start.11
Sparse Core Ops, SparseCore 0:
  9.9 62.1 all-gather.2

commit v3 on v2

--- a/solution.py
+++ b/solution.py
@@ -11,6 +11,7 @@
 UP_GROUPS = ((0, 1, 2, 3), (4, 5), (6, 7))
 DOWN_GROUPS = ((0, 1), (2, 3), (4, 5), (6, 7))
 LIGHT = pl.CostEstimate(flops=2_000_000_000, bytes_accessed=4_000_000, transcendentals=0)
+TILE = 256
 VMEM = 56 * 1024 * 1024
 UNREAD = pl.BlockSpec(memory_space=pl.ANY)
 
@@ -56,16 +57,20 @@
     rows, weights = refs[:count], refs[count:2 * count]
     part = weights[0].shape[1]
     for side in range(2):
-        place = slice(side * part, (side + 1) * part)
-        total = None if steps[0] == 0 else refs[2 * count][:, place]
-        for index in range(side, count, 2):
-            product = jnp.dot(
-                rows[index][...], weights[index][...], preferred_element_type=jnp.float32
-            )
-            total = product if total is None else total + product
-        if steps[-1] == size - 1:
-            total = silu(total)
-        out_ref[:, place] = total.astype(out_ref.dtype)
+
+        @pl.loop(0, part // TILE)
+        def _(tile, side=side):
+            columns = pl.ds(pl.multiple_of(tile * TILE, TILE), TILE)
+            place = pl.ds(pl.multiple_of(side * part + tile * TILE, TILE), TILE)
+            total = None if steps[0] == 0 else refs[2 * count][:, place]
+            for index in range(side, count, 2):
+                product = jnp.dot(
+                    rows[index][...], weights[index][:, columns], preferred_element_type=jnp.float32
+                )
+                total = product if total is None else total + product
+            if steps[-1] == size - 1:
+                total = silu(total)
+            out_ref[:, place] = total.astype(out_ref.dtype)
 
 
 def up_step(here, rows, slices, total, steps, size, after=()):
@@ -98,10 +103,14 @@
 def down_kernel(count, hidden_ref, *refs):
     out_ref = refs[-1]
     part = refs[0].shape[1]
-    for index in range(count):
-        out_ref[:, index * part:(index + 1) * part] = jnp.dot(
-            hidden_ref[...], refs[index][...], preferred_element_type=jnp.float32
-        ).astype(out_ref.dtype)
+
+    @pl.loop(0, hidden_ref.shape[0] // TILE)
+    def _(tile):
+        rows = pl.ds(pl.multiple_of(tile * TILE, TILE), TILE)
+        for index in range(count):
+            out_ref[rows, index * part:(index + 1) * part] = jnp.dot(
+                hidden_ref[rows, :], refs[index][...], preferred_element_type=jnp.float32
+            ).astype(out_ref.dtype)
 
 
 def down_step(hidden, slices, after=()):
@@ -121,10 +130,6 @@
     )(hidden, *parts, *after)
 
 
-def wait_for(parts, after):
-    return [lax.optimization_barrier((part, *after))[0] for part in parts] if after else parts
-
-
 def shift(parts):
     size = lax.axis_size("grp")
     right = [(i, (i + 1) % size) for i in range(size)]
@@ -148,11 +153,6 @@
     slot_total = ep_count * CAP
     here = lax.axis_index("grp").astype(jnp.int32)
 
-    everyone = lax.all_gather(tokens, "ep", axis=0, tiled=True)
-
-    up = [requantize(master_up[0], BLK, "requantize_up")]
-    advance(up)
-
     own_routes = lax.dynamic_slice_in_dim(routes, lax.axis_index("ep") * tok_dev, tok_dev, 0)
     named = own_routes[:, :, None] == jnp.arange(E, dtype=jnp.int32)
     mask = jnp.any(named, axis=1)
@@ -161,6 +161,7 @@
     rank = jnp.dot(earlier, mask.astype(jnp.bfloat16), preferred_element_type=jnp.float32)
     rank = jnp.where(mask, rank.astype(jnp.int32), -1)
     in_slot = rank[:, :, None] == jnp.arange(CAP, dtype=jnp.int32)
+    place = in_slot.reshape(tok_dev, slot_total).astype(jnp.bfloat16)
     gate_hi = gate_of.astype(jnp.bfloat16)
     gate_lo = (gate_of - gate_hi.astype(jnp.float32)).astype(jnp.bfloat16)
     weigh = jnp.concatenate(
@@ -171,21 +172,15 @@
         axis=0,
     )
 
-    own = lax.axis_index("ep").astype(jnp.int32)
-    asks = jnp.any(routes == own, axis=1).reshape(ep_count, tok_dev)
-    ahead = jnp.triu(jnp.ones((tok_dev, tok_dev), jnp.bfloat16), 1)
-    slot = jnp.dot(asks.astype(jnp.bfloat16), ahead, preferred_element_type=jnp.float32)
-    slot = slot.astype(jnp.int32) + CAP * jnp.arange(ep_count, dtype=jnp.int32)[:, None]
-    slot = jnp.where(asks, slot, -1).reshape(1, ep_count * tok_dev)
-    take = (slot == jnp.arange(slot_total, dtype=jnp.int32)[:, None]).astype(jnp.bfloat16)
-
-    down = [requantize(master_down[0], 3 * BLK, "requantize_down", up[1][:1])]
+    up = [requantize(master_up[0], BLK, "requantize_up")]
+    send = lax.dot_general(place, tokens, (((0,), (0,)), ((), ())), preferred_element_type=jnp.float32)
+    send = send.astype(jnp.bfloat16).reshape(ep_count, CAP, width)
+    advance(up)
+    rows = lax.all_to_all(send, "ep", split_axis=0, concat_axis=0, tiled=True).reshape(slot_total, width)
+    advance(up)
+    down = [requantize(master_down[0], 3 * BLK, "requantize_down", up[2][:1])]
     (down[0],) = advance(up, down[0])
     advance(up)
-    advance(up)
-    rows = jnp.dot(
-        wait_for([take], up[4][:1])[0], everyone, preferred_element_type=jnp.float32
-    ).astype(jnp.bfloat16)
     (rows,) = advance(up, rows)
 
     def send_back(answer):
@@ -194,8 +189,8 @@
             answer.reshape(ep_count, CAP, part), "ep", split_axis=0, concat_axis=0, tiled=True
         ).reshape(slot_total, part)
 
-    def mix(back, after):
-        both = jnp.dot(wait_for([weigh], after)[0], back, preferred_element_type=jnp.float32)
+    def mix(back):
+        both = jnp.dot(weigh, back, preferred_element_type=jnp.float32)
         return (both[:tok_dev] + both[tok_dev:]).astype(jnp.bfloat16)
 
     def add_up(steps, total):
@@ -214,12 +209,13 @@
     backs = [back]
     back = send_back(second)
     advance(down)
-    third, back = advance(down, answers(DOWN_GROUPS[2]), back)
-    backs.append(back)
-    backs.append(send_back(third))
+    third = answers(DOWN_GROUPS[2])
+    last = send_back(third)
+    third, back = advance(down, third, back)
+    backs += [back, last]
     advance(down)
     backs.append(send_back(answers(DOWN_GROUPS[3])))
-    mixed = [mix(back, ()) for back in backs]
+    mixed = [mix(back) for back in backs]
 
     half = width // size // 2
     out = jnp.zeros((tok_dev, width), jnp.bfloat16)

time: 323 us -> 308 us (0.954); the launches traced: 318 us -> 307 us
  between operations: 14.1 us -> 0.52 us
  waiting for transfers between devices: 137 us -> 148 us
  matrix products: 11 us -> 4.66 us
  starting transfers between devices: 100 us -> 94.7 us
    ppermute x28, starting transfers between devices: 51.4 us -> 41.3 us  [shift(): lax.ppermute(part, 'grp', way)]
    all_to_all x0 -> x1, starting transfers between devices: none -> 8.64 us  [local(): lax.all_to_all(send, 'ep', split_axis=0, concat_axis=0, tiled=True)]
    ppermute x28, waiting for transfers between devices: 95.4 us -> 102 us  [shift(): lax.ppermute(part, 'grp', way)]
    dot_general x6 -> x5, matrix products: 10.8 us -> 4.46 us  [the longest x1 3.21 us: local(): lax.dot_general(place, tokens, (((0,), (0,)), ((), ())), preferred_elemen...]
    all_to_all x4, waiting for transfers between devices: 41.3 us -> 45.9 us  [send_back(): lax.all_to_all(answer.reshape(ep_count, CAP, part), 'ep', split_axis=0, c...]
    all_to_all x4, starting transfers between devices: 48.7 us -> 44.8 us  [send_back(): lax.all_to_all(answer.reshape(ep_count, CAP, part), 'ep', split_axis=0, c...]
  transfers between devices with their start and end apart: 33 -> 33, of which waited for: 16 -> 15; matrix products, arithmetic and copies ran while one was open for 4% -> 1% of each run, Pallas kernels for 16% -> 16%
where the time goes in v3:
time: 308 us; the launch traced here: 307 us
  waiting for transfers between devices  148 us (48%)
  starting transfers between devices  94.7 us (31%)
  Pallas kernels  54.7 us (18%)
  matrix products  4.66 us (2%)
  local copies, waits for them, and re-layouts  3.72 us (1%)
    ppermute x28, waiting for transfers between devices, shift(): lax.ppermute(part, 'grp', way)  102 us
    all_to_all x4, waiting for transfers between devices, send_back(): lax.all_to_all(answer.reshape(ep_count, CAP, part), 'ep', split_axis=0, c...  45.9 us
    all_to_all x4, starting transfers between devices, send_back(): lax.all_to_all(answer.reshape(ep_count, CAP, part), 'ep', split_axis=0, c...  44.8 us
    ppermute x28, starting transfers between devices, shift(): lax.ppermute(part, 'grp', way)  41.3 us
    pallas_call x3, Pallas kernels, up_step(): pl.pallas_call(lambda *refs: up_kernel(steps, size, *refs), grid_spec=plt...  25.3 us
    pallas_call x4, Pallas kernels, down_step(): pl.pallas_call(lambda *refs: down_kernel(len(parts), *refs), grid=(1,), i...  21 us
    all_to_all x1, starting transfers between devices, local(): lax.all_to_all(send, 'ep', split_axis=0, concat_axis=0, tiled=True)  8.64 us
    pallas_call x2, Pallas kernels, requantize(): pl.pallas_call(requantize_kernel, grid=(height // step,), in_specs=[pl.Bl...  8.39 us
  transfers between devices with their start and end apart: 33, of which 15 were waited for; matrix products, arithmetic and copies ran while one was open for 1% of the time, Pallas kernels for 16%

profile of v3, /device:TPU:1, one launch (start us, length us, event | category | flops | bytes accessed | tf_op | source)
XLA Modules:
  0.0 307.3 jit_solution(2500357293675374885)
XLA Ops:
  0.0 0.8 fusion.28
  0.9 0.1 fusion.8
  1.0 0.2 fusion
  1.3 3.2 %convolution_convert_fusion = bf16[512,4096]{1,0:T(8,128)(2,1)} fusion(pred[32,512]{0,1:T(8,128)(4,1)S(1)} %bitcast.113, bf16[1,1,32,4096]{3,2,1,0:T(8,128)(2,1)S(1)} %copy-done), kind=kOutput, calls=%fused_computation | convolution fusion | flops 136314880 | bytes 4472832 | tf_op jit(solution)/shard_map/dot_general | solution.py:176
  4.6 8.6 %all-to-all-start = ((bf16[32,16,4096]{2,1,0:T(8,128)(2,1)}), bf16[32,16,4096]{2,1,0:T(8,128)(2,1)}, u32[]{:S(2)}, u32[]{:S(2)}) async-start(bf16[32,16,4096]{2,1,0:T(8,128)(2,1)} %bitcast.104), calls=%async_computation | async-start | bytes 8388608 | tf_op jit(solution)/shard_map/all_to_all | solution.py:179
  13.2 4.2 %requantize_up.1 = (bf16[512,768]{1,0:T(8,128)(2,1)}, bf16[512,768]{1,0:T(8,128)(2,1)}) custom-call(f32[512,1536]{1,0:T(8,128)} %bitcast.115), custom_call_target="tpu_custom_call" | custom-call | flops 2000000000 | bytes 4000000 | tf_op jit(solution)/shard_map/requantize_up/pallas_call | solution.py:39
  17.4 1.6 collective-permute-start
  19.0 3.9 %collective-permute-start.1 = (bf16[512,768]{1,0:T(8,128)(2,1)}, bf16[512,768]{1,0:T(8,128)(2,1)S(1)}, u32[]{:S(2)}, u32[]{:S(2)}) collective-permute-start(bf16[512,768]{1,0:T(8,128)(2,1)} %get-tuple-element.50.refs_10_), channel_id=1, source_target_pairs={{0,224},{32,0},{64,32},{96,64},{128,96},{160,128},{192,160},{224,1... | collective-permute-start | bytes 2359304 | tf_op jit(solution)/shard_map/ppermute | solution.py:137
  23.0 18.0 %collective-permute-done.refs_11_ = bf16[512,768]{1,0:T(8,128)(2,1)S(1)} collective-permute-done((bf16[512,768]{1,0:T(8,128)(2,1)}, bf16[512,768]{1,0:T(8,128)(2,1)S(1)}, u32[]{:S(2)}, u32[]{:S(2)}) %collective-permute-start) | collective-permute-done | bytes 786464 | tf_op jit(solution)/shard_map/ppermute | solution.py:137
  41.1 2.7 collective-permute-start.3
  43.7 17.0 %collective-permute-done.2.refs_0_.refs_13_ = bf16[512,768]{1,0:T(8,128)(2,1)S(1)} collective-permute-done((bf16[512,768]{1,0:T(8,128)(2,1)S(1)}, bf16[512,768]{1,0:T(8,128)(2,1)S(1)}, u32[]{:S(2)}, u32[]{:S(2)}) %collective-permute-start.2) | collective-permute-done | bytes 786464 | tf_op jit(solution)/shard_map/ppermute | solution.py:137
  60.7 0.8 collective-permute-start.4
  61.5 2.0 collective-permute-start.5
  63.5 4.2 %requantize_down.1 = (bf16[1536,256]{1,0:T(8,128)(2,1)}, bf16[1536,256]{1,0:T(8,128)(2,1)}) custom-call(f32[1536,512]{1,0:T(8,128)} %bitcast.116, bf16[512,768]{1,0:T(8,128)(2,1)} %copy-done.6), custom_call_target="tpu_custom_call" | custom-call | flops 2000000000 | bytes 4000000 | tf_op jit(solution)/shard_map/requantize_down/pallas_call | solution.py:39
  67.7 12.0 %collective-permute-done.4.refs_15_ = bf16[512,768]{1,0:T(8,128)(2,1)} collective-permute-done((bf16[512,768]{1,0:T(8,128)(2,1)S(1)}, bf16[512,768]{1,0:T(8,128)(2,1)}, u32[]{:S(2)}, u32[]{:S(2)}) %collective-permute-start.4) | collective-permute-done | bytes 786464 | tf_op jit(solution)/shard_map/ppermute | solution.py:137
  79.7 0.3 collective-permute-start.6
  80.0 2.3 collective-permute-start.7
  82.4 15.4 %collective-permute-done.6.refs_5_ = bf16[512,768]{1,0:T(8,128)(2,1)S(1)} collective-permute-done((bf16[512,768]{1,0:T(8,128)(2,1)}, bf16[512,768]{1,0:T(8,128)(2,1)S(1)}, u32[]{:S(2)}, u32[]{:S(2)}) %collective-permute-start.6) | collective-permute-done | bytes 786464 | tf_op jit(solution)/shard_map/ppermute | solution.py:137
  97.8 2.7 collective-permute-start.9
  100.5 14.2 %collective-permute-done.8.refs_7_ = bf16[512,768]{1,0:T(8,128)(2,1)S(1)} collective-permute-done((bf16[512,768]{1,0:T(8,128)(2,1)S(1)}, bf16[512,768]{1,0:T(8,128)(2,1)S(1)}, u32[]{:S(2)}, u32[]{:S(2)}) %collective-permute-start.8) | collective-permute-done | bytes 786464 | tf_op jit(solution)/shard_map/ppermute | solution.py:137
  114.8 2.7 collective-permute-start.11
  117.5 9.9 %up_step.3.refs_9_ = f32[512,1536]{1,0:T(8,128)} custom-call(s32[1]{0:T(128)} %bitcast.11.refs_0_, bf16[512,4096]{1,0:T(8,128)(2,1)} %bitcast.10.refs_1_.refs_2_.refs_3_.refs_4_.refs_5_.refs_6_.refs_7_.refs_8_, bf16[512,4096]{1,0:T(8,128)(2,1)} %bitcast.10.refs_1_.refs_2_.refs_3_.refs_4_.refs_5_.refs_6_.refs_7_.refs_8_, ...), custom_call_target="tpu_custom_call" | custom-call | flops 2000000000 | bytes 4000000 | tf_op jit(solution)/shard_map/up_step/pallas_call | solution.py:88
  127.5 3.5 %collective-permute-done.10.refs_5_ = bf16[512,768]{1,0:T(8,128)(2,1)} collective-permute-done((bf16[512,768]{1,0:T(8,128)(2,1)S(1)}, bf16[512,768]{1,0:T(8,128)(2,1)}, u32[]{:S(2)}, u32[]{:S(2)}) %collective-permute-start.10) | collective-permute-done | bytes 786464 | tf_op jit(solution)/shard_map/ppermute | solution.py:137
  130.9 2.7 collective-permute-start.13
  133.6 7.8 %up_step.4.refs_9_ = f32[512,1536]{1,0:T(8,128)} custom-call(s32[1]{0:T(128)} %bitcast.11.refs_0_, bf16[512,4096]{1,0:T(8,128)(2,1)} %bitcast.10.refs_1_.refs_2_.refs_3_.refs_4_.refs_5_.refs_6_.refs_7_.refs_8_, bf16[512,4096]{1,0:T(8,128)(2,1)} %bitcast.10.refs_1_.refs_2_.refs_3_.refs_4_.refs_5_.refs_6_.refs_7_.refs_8_, ...), custom_call_target="tpu_custom_call" | custom-call | flops 2000000000 | bytes 4000000 | tf_op jit(solution)/shard_map/up_step/pallas_call | solution.py:88
  141.4 5.2 %collective-permute-done.12.refs_7_ = bf16[512,768]{1,0:T(8,128)(2,1)S(1)} collective-permute-done((bf16[512,768]{1,0:T(8,128)(2,1)}, bf16[512,768]{1,0:T(8,128)(2,1)S(1)}, u32[]{:S(2)}, u32[]{:S(2)}) %collective-permute-start.12) | collective-permute-done | bytes 786464 | tf_op jit(solution)/shard_map/ppermute | solution.py:137
  146.8 2.8 collective-permute-start.15
  149.6 7.5 %up_step.5.refs_0_ = bf16[512,1536]{1,0:T(8,128)(2,1)} custom-call(s32[1]{0:T(128)} %bitcast.11.refs_0_, bf16[512,4096]{1,0:T(8,128)(2,1)} %bitcast.10.refs_1_.refs_2_.refs_3_.refs_4_.refs_5_.refs_6_.refs_7_.refs_8_, bf16[512,4096]{1,0:T(8,128)(2,1)} %bitcast.10.refs_1_.refs_2_.refs_3_.refs_4_.refs_5_.refs_6_.refs_7_.refs_8_, ...), custom_call_target="tpu_custom_call" | custom-call | flops 2000000000 | bytes 4000000 | tf_op jit(solution)/shard_map/up_step/pallas_call | solution.py:88
  157.1 5.6 %collective-permute-done.14.refs_3_ = bf16[1536,256]{1,0:T(8,128)(2,1)S(1)} collective-permute-done((bf16[1536,256]{1,0:T(8,128)(2,1)S(1)}, bf16[1536,256]{1,0:T(8,128)(2,1)S(1)}, u32[]{:S(2)}, u32[]{:S(2)}) %collective-permute-start.14) | collective-permute-done | bytes 786464 | tf_op jit(solution)/shard_map/ppermute | solution.py:137
  162.8 2.7 collective-permute-start.17
  165.5 5.3 %down_step.4 = bf16[512,1024]{1,0:T(8,128)(2,1)} custom-call(bf16[512,1536]{1,0:T(8,128)(2,1)} %up_step.5.refs_0_, bf16[1536,256]{1,0:T(8,128)(2,1)} %get-tuple-element.69.refs_1_, bf16[1536,256]{1,0:T(8,128)(2,1)} %get-tuple-element.70.refs_2_, bf16[1536,256]{1,0:T(8,128)(2,1)} %copy-done.17, bf16[1536,256]{1,0:T(8,128)(2,1)} %copy-done.18), custom_call_target="tpu_custom_call" | custom-call | flops 2000000000 | bytes 4000000 | tf_op jit(solution)/shard_map/down_step/pallas_call | solution.py:121
  170.8 7.9 %collective-permute-done.16.refs_1_ = bf16[1536,256]{1,0:T(8,128)(2,1)S(1)} collective-permute-done((bf16[1536,256]{1,0:T(8,128)(2,1)S(1)}, bf16[1536,256]{1,0:T(8,128)(2,1)S(1)}, u32[]{:S(2)}, u32[]{:S(2)}) %collective-permute-start.16) | collective-permute-done | bytes 786464 | tf_op jit(solution)/shard_map/ppermute | solution.py:137
  178.7 2.9 collective-permute-start.19
  181.6 18.0 %all-to-all-start.1 = ((bf16[32,16,1024]{2,1,0:T(8,128)(2,1)}), bf16[32,16,1024]{2,1,0:T(8,128)(2,1)S(1)}, u32[]{:S(2)}, u32[]{:S(2)}) async-start(bf16[32,16,1024]{2,1,0:T(8,128)(2,1)} %bitcast.109), calls=%async_computation.1 | async-start | bytes 2097152 | tf_op jit(solution)/shard_map/all_to_all | solution.py:188
  199.6 0.1 collective-permute-start.20
  199.7 2.7 collective-permute-start.21
  202.4 0.1 select_reduce_fusion
  202.6 0.1 copy.13
  202.8 0.1 eq.57
  202.9 0.1 fusion.3
  203.1 5.3 %down_step.5 = bf16[512,1024]{1,0:T(8,128)(2,1)} custom-call(bf16[512,1536]{1,0:T(8,128)(2,1)} %up_step.5.refs_0_, bf16[1536,256]{1,0:T(8,128)(2,1)} %copy-done.12, bf16[1536,256]{1,0:T(8,128)(2,1)} %collective-permute-done.17.refs_2_, bf16[1536,256]{1,0:T(8,128)(2,1)} %collective-permute-done.18.refs_3_, bf16[1536,256]{1,0:T(8,128)(2,1)} %collective-permute-done.19.refs_4_), custom_call_target="tpu_custom_call" | custom-call | flops 2000000000 | bytes 4000000 | tf_op jit(solution)/shard_map/down_step/pallas_call | solution.py:121
  208.3 8.2 %all-to-all-done.1 = bf16[32,16,1024]{2,1,0:T(8,128)(2,1)S(1)} async-done(((bf16[32,16,1024]{2,1,0:T(8,128)(2,1)}), bf16[32,16,1024]{2,1,0:T(8,128)(2,1)S(1)}, u32[]{:S(2)}, u32[]{:S(2)}) %all-to-all-start.1) | async-done | bytes 1048608 | tf_op jit(solution)/shard_map/all_to_all | solution.py:188
  216.5 2.7 collective-permute-start.23
  219.2 0.1 pad_maximum_fusion
  219.3 12.3 %all-to-all-start.2 = ((bf16[32,16,1024]{2,1,0:T(8,128)(2,1)}), bf16[32,16,1024]{2,1,0:T(8,128)(2,1)S(1)}, u32[]{:S(2)}, u32[]{:S(2)}) async-start(bf16[32,16,1024]{2,1,0:T(8,128)(2,1)} %bitcast.110), calls=%async_computation.2 | async-start | bytes 2097152 | tf_op jit(solution)/shard_map/all_to_all | solution.py:188
  231.6 0.3 fusion.33
  232.0 0.4 collective-permute-done.22.refs_3_
  232.4 0.9 copy-done.16
  233.3 2.7 collective-permute-start.25
  236.0 5.3 %down_step.6 = bf16[512,1024]{1,0:T(8,128)(2,1)} custom-call(bf16[512,1536]{1,0:T(8,128)(2,1)} %up_step.5.refs_0_, bf16[1536,256]{1,0:T(8,128)(2,1)} %collective-permute-done.20.refs_1_, bf16[1536,256]{1,0:T(8,128)(2,1)} %collective-permute-done.21.refs_2_, bf16[1536,256]{1,0:T(8,128)(2,1)} %copy-done.16, bf16[1536,256]{1,0:T(8,128)(2,1)} %collective-permute-done.23.refs_4_), custom_call_target="tpu_custom_call" | custom-call | flops 2000000000 | bytes 4000000 | tf_op jit(solution)/shard_map/down_step/pallas_call | solution.py:121
  241.3 7.2 %all-to-all-done.2 = bf16[32,16,1024]{2,1,0:T(8,128)(2,1)S(1)} async-done(((bf16[32,16,1024]{2,1,0:T(8,128)(2,1)}), bf16[32,16,1024]{2,1,0:T(8,128)(2,1)S(1)}, u32[]{:S(2)}, u32[]{:S(2)}) %all-to-all-start.2) | async-done | bytes 1048608 | tf_op jit(solution)/shard_map/all_to_all | solution.py:188
  248.5 6.5 %all-to-all-start.3 = ((bf16[32,16,1024]{2,1,0:T(8,128)(2,1)}), bf16[32,16,1024]{2,1,0:T(8,128)(2,1)S(1)}, u32[]{:S(2)}, u32[]{:S(2)}) async-start(bf16[32,16,1024]{2,1,0:T(8,128)(2,1)} %bitcast.111), calls=%async_computation.3 | async-start | bytes 2097152 | tf_op jit(solution)/shard_map/all_to_all | solution.py:188
  255.0 0.1 collective-permute-start.26
  255.1 2.7 collective-permute-start.27
  257.8 0.3 fusion.34
  258.2 13.7 %all-to-all-done.3 = bf16[32,16,1024]{2,1,0:T(8,128)(2,1)S(1)} async-done(((bf16[32,16,1024]{2,1,0:T(8,128)(2,1)}), bf16[32,16,1024]{2,1,0:T(8,128)(2,1)S(1)}, u32[]{:S(2)}, u32[]{:S(2)}) %all-to-all-start.3) | async-done | bytes 1048608 | tf_op jit(solution)/shard_map/all_to_all | solution.py:188
  271.9 0.3 fusion.35
  272.2 3.1 %collective-permute-done.26.refs_3_ = bf16[1536,256]{1,0:T(8,128)(2,1)} collective-permute-done((bf16[1536,256]{1,0:T(8,128)(2,1)S(1)}, bf16[1536,256]{1,0:T(8,128)(2,1)}, u32[]{:S(2)}, u32[]{:S(2)}) %collective-permute-start.26) | collective-permute-done | bytes 786464 | tf_op jit(solution)/shard_map/ppermute | solution.py:137
  275.3 5.3 %down_step.7 = bf16[512,1024]{1,0:T(8,128)(2,1)} custom-call(bf16[512,1536]{1,0:T(8,128)(2,1)} %up_step.5.refs_0_, bf16[1536,256]{1,0:T(8,128)(2,1)} %copy-done.15, bf16[1536,256]{1,0:T(8,128)(2,1)} %collective-permute-done.25.refs_2_, bf16[1536,256]{1,0:T(8,128)(2,1)} %collective-permute-done.26.refs_3_, bf16[1536,256]{1,0:T(8,128)(2,1)} %collective-permute-done.27.refs_4_), custom_call_target="tpu_custom_call" | custom-call | flops 2000000000 | bytes 4000000 | tf_op jit(solution)/shard_map/down_step/pallas_call | solution.py:121
  280.6 8.1 %all-to-all-start.4 = ((bf16[32,16,1024]{2,1,0:T(8,128)(2,1)}), bf16[32,16,1024]{2,1,0:T(8,128)(2,1)S(1)}, u32[]{:S(2)}, u32[]{:S(2)}) async-start(bf16[32,16,1024]{2,1,0:T(8,128)(2,1)} %bitcast.112), calls=%async_computation.4 | async-start | bytes 2097152 | tf_op jit(solution)/shard_map/all_to_all | solution.py:188
  288.7 16.8 %all-to-all-done.4 = bf16[32,16,1024]{2,1,0:T(8,128)(2,1)S(1)} async-done(((bf16[32,16,1024]{2,1,0:T(8,128)(2,1)}), bf16[32,16,1024]{2,1,0:T(8,128)(2,1)S(1)}, u32[]{:S(2)}, u32[]{:S(2)}) %all-to-all-start.4) | async-done | bytes 1048608 | tf_op jit(solution)/shard_map/all_to_all | solution.py:188
  305.6 0.3 fusion.36
  306.0 0.7 copy-done.10
  306.7 0.6 fusion.9
  (91 shorter events, 1.1 us)
Async XLA Ops:
  0.0 1.3 copy-start
  4.6 110.2 %all-to-all-start = ((bf16[32,16,4096]{2,1,0:T(8,128)(2,1)}), bf16[32,16,4096]{2,1,0:T(8,128)(2,1)}, u32[]{:S(2)}, u32[]{:S(2)}) async-start(bf16[32,16,4096]{2,1,0:T(8,128)(2,1)} %bitcast.104), calls=%async_computation | async-start | bytes 8388608 | tf_op jit(solution)/shard_map/all_to_all | solution.py:179
  17.4 23.6 %collective-permute-start = (bf16[512,768]{1,0:T(8,128)(2,1)}, bf16[512,768]{1,0:T(8,128)(2,1)S(1)}, u32[]{:S(2)}, u32[]{:S(2)}) collective-permute-start(bf16[512,768]{1,0:T(8,128)(2,1)} %get-tuple-element.49.refs_9_), channel_id=1, source_target_pairs={{0,32},{32,64},{64,96},{96,128},{128,160},{160,192},{192,224},{224... | collective-permute-start | bytes 2359304 | tf_op jit(solution)/shard_map/ppermute | solution.py:137
  19.0 21.9 %collective-permute-start.1 = (bf16[512,768]{1,0:T(8,128)(2,1)}, bf16[512,768]{1,0:T(8,128)(2,1)S(1)}, u32[]{:S(2)}, u32[]{:S(2)}) collective-permute-start(bf16[512,768]{1,0:T(8,128)(2,1)} %get-tuple-element.50.refs_10_), channel_id=1, source_target_pairs={{0,224},{32,0},{64,32},{96,64},{128,96},{160,128},{192,160},{224,1... | collective-permute-start | bytes 2359304 | tf_op jit(solution)/shard_map/ppermute | solution.py:137
  41.0 26.7 %copy-start.4 = (bf16[512,768]{1,0:T(8,128)(2,1)}, bf16[512,768]{1,0:T(8,128)(2,1)S(1)}, u32[]{:S(2)}) copy-start(bf16[512,768]{1,0:T(8,128)(2,1)S(1)} %collective-permute-done.refs_11_) | copy-start | bytes 2359300
  41.0 19.8 %copy-start.5 = (bf16[512,768]{1,0:T(8,128)(2,1)}, bf16[512,768]{1,0:T(8,128)(2,1)S(1)}, u32[]{:S(2)}) copy-start(bf16[512,768]{1,0:T(8,128)(2,1)S(1)} %collective-permute-done.1.refs_12_) | copy-start | bytes 2359300
  41.0 19.8 %collective-permute-start.2 = (bf16[512,768]{1,0:T(8,128)(2,1)S(1)}, bf16[512,768]{1,0:T(8,128)(2,1)S(1)}, u32[]{:S(2)}, u32[]{:S(2)}) collective-permute-start(bf16[512,768]{1,0:T(8,128)(2,1)S(1)} %collective-permute-done.refs_11_), channel_id=1, source_target_pairs={{0,32},{32,64},{64,96},{96,128},{128,160},{160,192},{192,224},{224... | collective-permute-start | bytes 2359304 | tf_op jit(solution)/shard_map/ppermute | solution.py:137
  41.1 19.7 %collective-permute-start.3 = (bf16[512,768]{1,0:T(8,128)(2,1)S(1)}, bf16[512,768]{1,0:T(8,128)(2,1)S(1)}, u32[]{:S(2)}, u32[]{:S(2)}) collective-permute-start(bf16[512,768]{1,0:T(8,128)(2,1)S(1)} %collective-permute-done.1.refs_12_), channel_id=1, source_target_pairs={{0,224},{32,0},{64,32},{96,64},{128,96},{160,128},{192,160},{224,1... | collective-permute-start | bytes 2359304 | tf_op jit(solution)/shard_map/ppermute | solution.py:137
  60.7 2.8 copy-start.6
  60.7 7.0 %copy-start.7 = (bf16[512,768]{1,0:T(8,128)(2,1)}, bf16[512,768]{1,0:T(8,128)(2,1)S(1)}, u32[]{:S(2)}) copy-start(bf16[512,768]{1,0:T(8,128)(2,1)S(1)} %collective-permute-done.3.refs_14_) | copy-start | bytes 2359300
  60.7 18.9 %collective-permute-start.4 = (bf16[512,768]{1,0:T(8,128)(2,1)S(1)}, bf16[512,768]{1,0:T(8,128)(2,1)}, u32[]{:S(2)}, u32[]{:S(2)}) collective-permute-start(bf16[512,768]{1,0:T(8,128)(2,1)S(1)} %collective-permute-done.2.refs_0_.refs_13_), channel_id=1, source_target_pairs={{0,32},{32,64},{64,96},{96,128},{128,160},{160,192},{192,224},{224... | collective-permute-start | bytes 2359304 | tf_op jit(solution)/shard_map/ppermute | solution.py:137
  61.5 18.2 %collective-permute-start.5 = (bf16[512,768]{1,0:T(8,128)(2,1)S(1)}, bf16[512,768]{1,0:T(8,128)(2,1)}, u32[]{:S(2)}, u32[]{:S(2)}) collective-permute-start(bf16[512,768]{1,0:T(8,128)(2,1)S(1)} %collective-permute-done.3.refs_14_), channel_id=1, source_target_pairs={{0,224},{32,0},{64,32},{96,64},{128,96},{160,128},{192,160},{224,1... | collective-permute-start | bytes 2359304 | tf_op jit(solution)/shard_map/ppermute | solution.py:137
  79.7 18.0 %collective-permute-start.6 = (bf16[512,768]{1,0:T(8,128)(2,1)}, bf16[512,768]{1,0:T(8,128)(2,1)S(1)}, u32[]{:S(2)}, u32[]{:S(2)}) collective-permute-start(bf16[512,768]{1,0:T(8,128)(2,1)} %collective-permute-done.4.refs_15_), channel_id=1, source_target_pairs={{0,32},{32,64},{64,96},{96,128},{128,160},{160,192},{192,224},{224... | collective-permute-start | bytes 2359304 | tf_op jit(solution)/shard_map/ppermute | solution.py:137
  80.0 17.7 %collective-permute-start.7 = (bf16[512,768]{1,0:T(8,128)(2,1)}, bf16[512,768]{1,0:T(8,128)(2,1)S(1)}, u32[]{:S(2)}, u32[]{:S(2)}) collective-permute-start(bf16[512,768]{1,0:T(8,128)(2,1)} %collective-permute-done.5.refs_16_), channel_id=1, source_target_pairs={{0,224},{32,0},{64,32},{96,64},{128,96},{160,128},{192,160},{224,1... | collective-permute-start | bytes 2359304 | tf_op jit(solution)/shard_map/ppermute | solution.py:137
  97.7 29.7 %copy-start.1 = (bf16[512,768]{1,0:T(8,128)(2,1)}, bf16[512,768]{1,0:T(8,128)(2,1)S(1)}, u32[]{:S(2)}) copy-start(bf16[512,768]{1,0:T(8,128)(2,1)S(1)} %collective-permute-done.6.refs_5_) | copy-start | bytes 2359300
  97.7 29.7 %copy-start.2 = (bf16[512,768]{1,0:T(8,128)(2,1)}, bf16[512,768]{1,0:T(8,128)(2,1)S(1)}, u32[]{:S(2)}) copy-start(bf16[512,768]{1,0:T(8,128)(2,1)S(1)} %collective-permute-done.7.refs_6_) | copy-start | bytes 2359300
  97.7 17.0 %collective-permute-start.8 = (bf16[512,768]{1,0:T(8,128)(2,1)S(1)}, bf16[512,768]{1,0:T(8,128)(2,1)S(1)}, u32[]{:S(2)}, u32[]{:S(2)}) collective-permute-start(bf16[512,768]{1,0:T(8,128)(2,1)S(1)} %collective-permute-done.6.refs_5_), channel_id=1, source_target_pairs={{0,32},{32,64},{64,96},{96,128},{128,160},{160,192},{192,224},{224... | collective-permute-start | bytes 2359304 | tf_op jit(solution)/shard_map/ppermute | solution.py:137
  97.8 16.9 %collective-permute-start.9 = (bf16[512,768]{1,0:T(8,128)(2,1)S(1)}, bf16[512,768]{1,0:T(8,128)(2,1)}, u32[]{:S(2)}, u32[]{:S(2)}) collective-permute-start(bf16[512,768]{1,0:T(8,128)(2,1)S(1)} %collective-permute-done.7.refs_6_), channel_id=1, source_target_pairs={{0,224},{32,0},{64,32},{96,64},{128,96},{160,128},{192,160},{224,1... | collective-permute-start | bytes 2359304 | tf_op jit(solution)/shard_map/ppermute | solution.py:137
  114.7 12.7 %copy-start.3 = (bf16[512,768]{1,0:T(8,128)(2,1)}, bf16[512,768]{1,0:T(8,128)(2,1)S(1)}, u32[]{:S(2)}) copy-start(bf16[512,768]{1,0:T(8,128)(2,1)S(1)} %collective-permute-done.8.refs_7_) | copy-start | bytes 2359300
  114.7 16.2 %collective-permute-start.10 = (bf16[512,768]{1,0:T(8,128)(2,1)S(1)}, bf16[512,768]{1,0:T(8,128)(2,1)}, u32[]{:S(2)}, u32[]{:S(2)}) collective-permute-start(bf16[512,768]{1,0:T(8,128)(2,1)S(1)} %collective-permute-done.8.refs_7_), channel_id=1, source_target_pairs={{0,32},{32,64},{64,96},{96,128},{128,160},{160,192},{192,224},{224... | collective-permute-start | bytes 2359304 | tf_op jit(solution)/shard_map/ppermute | solution.py:137
  114.8 16.1 %collective-permute-start.11 = (bf16[512,768]{1,0:T(8,128)(2,1)}, bf16[512,768]{1,0:T(8,128)(2,1)}, u32[]{:S(2)}, u32[]{:S(2)}) collective-permute-start(bf16[512,768]{1,0:T(8,128)(2,1)} %collective-permute-done.9.refs_8_), channel_id=1, source_target_pairs={{0,224},{32,0},{64,32},{96,64},{128,96},{160,128},{192,160},{224,1... | collective-permute-start | bytes 2359304 | tf_op jit(solution)/shard_map/ppermute | solution.py:137
  127.5 19.2 %copy-start.13 = (bf16[1536,256]{1,0:T(8,128)(2,1)S(1)}, bf16[1536,256]{1,0:T(8,128)(2,1)}, u32[]{:S(2)}) copy-start(bf16[1536,256]{1,0:T(8,128)(2,1)} %get-tuple-element.69.refs_1_) | copy-start | bytes 2359300
  127.5 19.3 %copy-start.14 = (bf16[1536,256]{1,0:T(8,128)(2,1)S(1)}, bf16[1536,256]{1,0:T(8,128)(2,1)}, u32[]{:S(2)}) copy-start(bf16[1536,256]{1,0:T(8,128)(2,1)} %get-tuple-element.70.refs_2_) | copy-start | bytes 2359300
  130.9 15.8 %collective-permute-start.12 = (bf16[512,768]{1,0:T(8,128)(2,1)}, bf16[512,768]{1,0:T(8,128)(2,1)S(1)}, u32[]{:S(2)}, u32[]{:S(2)}) collective-permute-start(bf16[512,768]{1,0:T(8,128)(2,1)} %collective-permute-done.10.refs_5_), channel_id=1, source_target_pairs={{0,32},{32,64},{64,96},{96,128},{128,160},{160,192},{192,224},{224... | collective-permute-start | bytes 2359304 | tf_op jit(solution)/shard_map/ppermute | solution.py:137
  130.9 15.8 %collective-permute-start.13 = (bf16[512,768]{1,0:T(8,128)(2,1)}, bf16[512,768]{1,0:T(8,128)(2,1)S(1)}, u32[]{:S(2)}, u32[]{:S(2)}) collective-permute-start(bf16[512,768]{1,0:T(8,128)(2,1)} %collective-permute-done.11.refs_6_), channel_id=1, source_target_pairs={{0,224},{32,0},{64,32},{96,64},{128,96},{160,128},{192,160},{224,1... | collective-permute-start | bytes 2359304 | tf_op jit(solution)/shard_map/ppermute | solution.py:137
  146.7 2.9 copy-start.8
  146.7 2.9 copy-start.9
  146.7 16.0 %collective-permute-start.14 = (bf16[1536,256]{1,0:T(8,128)(2,1)S(1)}, bf16[1536,256]{1,0:T(8,128)(2,1)S(1)}, u32[]{:S(2)}, u32[]{:S(2)}) collective-permute-start(bf16[1536,256]{1,0:T(8,128)(2,1)S(1)} %copy-done.13), channel_id=1, source_target_pairs={{0,32},{32,64},{64,96},{96,128},{128,160},{160,192},{192,224},{224... | collective-permute-start | bytes 2359304 | tf_op jit(solution)/shard_map/ppermute | solution.py:137
  146.8 15.9 %collective-permute-start.15 = (bf16[1536,256]{1,0:T(8,128)(2,1)S(1)}, bf16[1536,256]{1,0:T(8,128)(2,1)S(1)}, u32[]{:S(2)}, u32[]{:S(2)}) collective-permute-start(bf16[1536,256]{1,0:T(8,128)(2,1)S(1)} %copy-done.14), channel_id=1, source_target_pairs={{0,224},{32,0},{64,32},{96,64},{128,96},{160,128},{192,160},{224,1... | collective-permute-start | bytes 2359304 | tf_op jit(solution)/shard_map/ppermute | solution.py:137
  157.1 45.3 %copy-start.11 = (f32[1,1,32,8]{2,3,1,0:T(8,128)S(1)}, f32[1,1,32,8]{2,3,1,0:T(8,128)}, u32[]{:S(2)}) copy-start(f32[1,1,32,8]{2,3,1,0:T(8,128)} %param.6) | copy-start | bytes 3076
  162.7 2.8 copy-start.17
  162.7 2.8 copy-start.18
  162.7 15.9 %collective-permute-start.16 = (bf16[1536,256]{1,0:T(8,128)(2,1)S(1)}, bf16[1536,256]{1,0:T(8,128)(2,1)S(1)}, u32[]{:S(2)}, u32[]{:S(2)}) collective-permute-start(bf16[1536,256]{1,0:T(8,128)(2,1)S(1)} %collective-permute-done.14.refs_3_), channel_id=1, source_target_pairs={{0,32},{32,64},{64,96},{96,128},{128,160},{160,192},{192,224},{224... | collective-permute-start | bytes 2359304 | tf_op jit(solution)/shard_map/ppermute | solution.py:137
  162.8 15.9 %collective-permute-start.17 = (bf16[1536,256]{1,0:T(8,128)(2,1)S(1)}, bf16[1536,256]{1,0:T(8,128)(2,1)}, u32[]{:S(2)}, u32[]{:S(2)}) collective-permute-start(bf16[1536,256]{1,0:T(8,128)(2,1)S(1)} %collective-permute-done.15.refs_4_), channel_id=1, source_target_pairs={{0,224},{32,0},{64,32},{96,64},{128,96},{160,128},{192,160},{224,1... | collective-permute-start | bytes 2359304 | tf_op jit(solution)/shard_map/ppermute | solution.py:137
  178.7 24.4 %copy-start.12 = (bf16[1536,256]{1,0:T(8,128)(2,1)}, bf16[1536,256]{1,0:T(8,128)(2,1)S(1)}, u32[]{:S(2)}) copy-start(bf16[1536,256]{1,0:T(8,128)(2,1)S(1)} %collective-permute-done.16.refs_1_) | copy-start | bytes 2359300
  178.7 20.9 %collective-permute-start.18 = (bf16[1536,256]{1,0:T(8,128)(2,1)S(1)}, bf16[1536,256]{1,0:T(8,128)(2,1)}, u32[]{:S(2)}, u32[]{:S(2)}) collective-permute-start(bf16[1536,256]{1,0:T(8,128)(2,1)S(1)} %collective-permute-done.16.refs_1_), channel_id=1, source_target_pairs={{0,32},{32,64},{64,96},{96,128},{128,160},{160,192},{192,224},{224... | collective-permute-start | bytes 2359304 | tf_op jit(solution)/shard_map/ppermute | solution.py:137
  178.7 20.9 %collective-permute-start.19 = (bf16[1536,256]{1,0:T(8,128)(2,1)}, bf16[1536,256]{1,0:T(8,128)(2,1)}, u32[]{:S(2)}, u32[]{:S(2)}) collective-permute-start(bf16[1536,256]{1,0:T(8,128)(2,1)} %collective-permute-done.17.refs_2_), channel_id=1, source_target_pairs={{0,224},{32,0},{64,32},{96,64},{128,96},{160,128},{192,160},{224,1... | collective-permute-start | bytes 2359304 | tf_op jit(solution)/shard_map/ppermute | solution.py:137
  181.6 34.9 %all-to-all-start.1 = ((bf16[32,16,1024]{2,1,0:T(8,128)(2,1)}), bf16[32,16,1024]{2,1,0:T(8,128)(2,1)S(1)}, u32[]{:S(2)}, u32[]{:S(2)}) async-start(bf16[32,16,1024]{2,1,0:T(8,128)(2,1)} %bitcast.109), calls=%async_computation.1 | async-start | bytes 2097152 | tf_op jit(solution)/shard_map/all_to_all | solution.py:188
  199.6 16.9 %collective-permute-start.20 = (bf16[1536,256]{1,0:T(8,128)(2,1)}, bf16[1536,256]{1,0:T(8,128)(2,1)}, u32[]{:S(2)}, u32[]{:S(2)}) collective-permute-start(bf16[1536,256]{1,0:T(8,128)(2,1)} %collective-permute-done.18.refs_3_), channel_id=1, source_target_pairs={{0,32},{32,64},{64,96},{96,128},{128,160},{160,192},{192,224},{224... | collective-permute-start | bytes 2359304 | tf_op jit(solution)/shard_map/ppermute | solution.py:137
  199.7 16.8 %collective-permute-start.21 = (bf16[1536,256]{1,0:T(8,128)(2,1)}, bf16[1536,256]{1,0:T(8,128)(2,1)}, u32[]{:S(2)}, u32[]{:S(2)}) collective-permute-start(bf16[1536,256]{1,0:T(8,128)(2,1)} %collective-permute-done.19.refs_4_), channel_id=1, source_target_pairs={{0,224},{32,0},{64,32},{96,64},{128,96},{160,128},{192,160},{224,1... | collective-permute-start | bytes 2359304 | tf_op jit(solution)/shard_map/ppermute | solution.py:137
  216.5 15.9 %collective-permute-start.22 = (bf16[1536,256]{1,0:T(8,128)(2,1)}, bf16[1536,256]{1,0:T(8,128)(2,1)S(1)}, u32[]{:S(2)}, u32[]{:S(2)}) collective-permute-start(bf16[1536,256]{1,0:T(8,128)(2,1)} %collective-permute-done.20.refs_1_), channel_id=1, source_target_pairs={{0,32},{32,64},{64,96},{96,128},{128,160},{160,192},{192,224},{224... | collective-permute-start | bytes 2359304 | tf_op jit(solution)/shard_map/ppermute | solution.py:137
  216.5 16.8 %collective-permute-start.23 = (bf16[1536,256]{1,0:T(8,128)(2,1)}, bf16[1536,256]{1,0:T(8,128)(2,1)}, u32[]{:S(2)}, u32[]{:S(2)}) collective-permute-start(bf16[1536,256]{1,0:T(8,128)(2,1)} %collective-permute-done.21.refs_2_), channel_id=1, source_target_pairs={{0,224},{32,0},{64,32},{96,64},{128,96},{160,128},{192,160},{224,1... | collective-permute-start | bytes 2359304 | tf_op jit(solution)/shard_map/ppermute | solution.py:137
  219.3 29.2 %all-to-all-start.2 = ((bf16[32,16,1024]{2,1,0:T(8,128)(2,1)}), bf16[32,16,1024]{2,1,0:T(8,128)(2,1)S(1)}, u32[]{:S(2)}, u32[]{:S(2)}) async-start(bf16[32,16,1024]{2,1,0:T(8,128)(2,1)} %bitcast.110), calls=%async_computation.2 | async-start | bytes 2097152 | tf_op jit(solution)/shard_map/all_to_all | solution.py:188
  232.4 0.9 copy-start.16
  233.3 21.7 %collective-permute-start.24 = (bf16[1536,256]{1,0:T(8,128)(2,1)}, bf16[1536,256]{1,0:T(8,128)(2,1)S(1)}, u32[]{:S(2)}, u32[]{:S(2)}) collective-permute-start(bf16[1536,256]{1,0:T(8,128)(2,1)} %copy-done.16), channel_id=1, source_target_pairs={{0,32},{32,64},{64,96},{96,128},{128,160},{160,192},{192,224},{224... | collective-permute-start | bytes 2359304 | tf_op jit(solution)/shard_map/ppermute | solution.py:137
  233.3 21.7 %collective-permute-start.25 = (bf16[1536,256]{1,0:T(8,128)(2,1)}, bf16[1536,256]{1,0:T(8,128)(2,1)}, u32[]{:S(2)}, u32[]{:S(2)}) collective-permute-start(bf16[1536,256]{1,0:T(8,128)(2,1)} %collective-permute-done.23.refs_4_), channel_id=1, source_target_pairs={{0,224},{32,0},{64,32},{96,64},{128,96},{160,128},{192,160},{224,1... | collective-permute-start | bytes 2359304 | tf_op jit(solution)/shard_map/ppermute | solution.py:137
  248.5 23.4 %all-to-all-start.3 = ((bf16[32,16,1024]{2,1,0:T(8,128)(2,1)}), bf16[32,16,1024]{2,1,0:T(8,128)(2,1)S(1)}, u32[]{:S(2)}, u32[]{:S(2)}) async-start(bf16[32,16,1024]{2,1,0:T(8,128)(2,1)} %bitcast.111), calls=%async_computation.3 | async-start | bytes 2097152 | tf_op jit(solution)/shard_map/all_to_all | solution.py:188
  255.0 20.3 %copy-start.15 = (bf16[1536,256]{1,0:T(8,128)(2,1)}, bf16[1536,256]{1,0:T(8,128)(2,1)S(1)}, u32[]{:S(2)}) copy-start(bf16[1536,256]{1,0:T(8,128)(2,1)S(1)} %collective-permute-done.24.refs_1_) | copy-start | bytes 2359300
  255.0 20.3 %collective-permute-start.26 = (bf16[1536,256]{1,0:T(8,128)(2,1)S(1)}, bf16[1536,256]{1,0:T(8,128)(2,1)}, u32[]{:S(2)}, u32[]{:S(2)}) collective-permute-start(bf16[1536,256]{1,0:T(8,128)(2,1)S(1)} %collective-permute-done.24.refs_1_), channel_id=1, source_target_pairs={{0,32},{32,64},{64,96},{96,128},{128,160},{160,192},{192,224},{224... | collective-permute-start | bytes 2359304 | tf_op jit(solution)/shard_map/ppermute | solution.py:137
  255.1 20.2 %collective-permute-start.27 = (bf16[1536,256]{1,0:T(8,128)(2,1)}, bf16[1536,256]{1,0:T(8,128)(2,1)}, u32[]{:S(2)}, u32[]{:S(2)}) collective-permute-start(bf16[1536,256]{1,0:T(8,128)(2,1)} %collective-permute-done.25.refs_2_), channel_id=1, source_target_pairs={{0,224},{32,0},{64,32},{96,64},{128,96},{160,128},{192,160},{224,1... | collective-permute-start | bytes 2359304 | tf_op jit(solution)/shard_map/ppermute | solution.py:137
  280.6 25.0 %all-to-all-start.4 = ((bf16[32,16,1024]{2,1,0:T(8,128)(2,1)}), bf16[32,16,1024]{2,1,0:T(8,128)(2,1)S(1)}, u32[]{:S(2)}, u32[]{:S(2)}) async-start(bf16[32,16,1024]{2,1,0:T(8,128)(2,1)} %bitcast.112), calls=%async_computation.4 | async-start | bytes 2097152 | tf_op jit(solution)/shard_map/all_to_all | solution.py:188
  306.0 0.7 copy-start.10

commit v4 on v3

--- a/solution.py
+++ b/solution.py
@@ -12,39 +12,46 @@
 DOWN_GROUPS = ((0, 1), (2, 3), (4, 5), (6, 7))
 LIGHT = pl.CostEstimate(flops=2_000_000_000, bytes_accessed=4_000_000, transcendentals=0)
 TILE = 256
+CUTS = 4
 VMEM = 56 * 1024 * 1024
 UNREAD = pl.BlockSpec(memory_space=pl.ANY)
 
 
-def coded_block(entries):
-    largest = jnp.max(jnp.max(jnp.abs(entries), axis=0, keepdims=True), axis=1, keepdims=True)
-    scale = (largest / 448.0 + 1e-06).astype(jnp.bfloat16).astype(jnp.float32)
-    coded = (entries / scale).astype(jnp.bfloat16)
-    return (coded.astype(jnp.float32) * scale).astype(jnp.bfloat16)
-
-
-def requantize_kernel(master_ref, *refs):
-    out_refs = refs[-2:]
-    width = out_refs[0].shape[1]
-    for column in range(0, master_ref.shape[1], BLK):
-        place = column % width
-        for row in range(0, master_ref.shape[0], BLK):
-            out_refs[column // width][row:row + BLK, place:place + BLK] = coded_block(
-                master_ref[row:row + BLK, column:column + BLK]
-            )
+def requantize_kernel(*refs):
+    master_refs, out_refs = refs[:CUTS], refs[-2:]
+    height, part = master_refs[0].shape
+    share = out_refs[0].shape[1]
+    blocks = [
+        (cut, row, column)
+        for cut in range(CUTS)
+        for row in range(0, height, BLK)
+        for column in range(0, part, BLK)
+    ]
+    entries = lambda cut, row, column: master_refs[cut][row:row + BLK, column:column + BLK]
+    largest = [jnp.max(jnp.abs(entries(*block)), axis=0, keepdims=True) for block in blocks]
+    largest = jnp.max(jnp.concatenate(largest, axis=0), axis=1, keepdims=True)
+    scales = (largest / 448.0 + 1e-06).astype(jnp.bfloat16).astype(jnp.float32)
+    for index, (cut, row, column) in enumerate(blocks):
+        scale = scales[index:index + 1, :]
+        coded = (entries(cut, row, column) / scale).astype(jnp.bfloat16)
+        side, place = divmod(cut * part + column, share)
+        out_refs[side][row:row + BLK, place:place + BLK] = (
+            coded.astype(jnp.float32) * scale
+        ).astype(jnp.bfloat16)
 
 
 def requantize(master, step, name, after=()):
     height, width = master.shape
+    cuts = [pl.BlockSpec((step, width // CUTS), lambda i, cut=cut: (i, cut)) for cut in range(CUTS)]
     return pl.pallas_call(
         requantize_kernel,
         grid=(height // step,),
-        in_specs=[pl.BlockSpec((step, width), lambda i: (i, 0))] + [UNREAD] * len(after),
+        in_specs=cuts + [UNREAD] * len(after),
         out_specs=[pl.BlockSpec((step, width // 2), lambda i: (i, 0))] * 2,
         out_shape=[jax.ShapeDtypeStruct((height, width // 2), jnp.bfloat16)] * 2,
         cost_estimate=LIGHT,
         name=name,
-    )(master, *after)
+    )(*[master] * CUTS, *after)
 
 
 def silu(total):
@@ -113,21 +120,24 @@
             ).astype(out_ref.dtype)
 
 
-def down_step(hidden, slices, after=()):
+def down_step(hidden, slices, groups=1, buffer=None):
     parts = [part for one in slices for part in one]
     count = hidden.shape[0]
     width = sum(part.shape[1] for part in parts)
     whole = lambda shape: pl.BlockSpec(shape, lambda i: (0, 0))
+    given = [] if buffer is None else [buffer]
+    second = len(given)
     return pl.pallas_call(
         lambda *refs: down_kernel(len(parts), *refs),
         grid=(1,),
-        in_specs=[whole(part.shape) for part in (hidden, *parts)] + [UNREAD] * len(after),
-        out_specs=whole((count, width)),
-        out_shape=jax.ShapeDtypeStruct((count, width), jnp.bfloat16),
+        in_specs=[whole(part.shape) for part in (hidden, *parts)] + [UNREAD] * second,
+        out_specs=pl.BlockSpec((count, width), lambda i: (0, second)),
+        out_shape=jax.ShapeDtypeStruct((count, width * groups), jnp.bfloat16),
+        input_output_aliases={1 + len(parts): 0} if second else {},
         compiler_params=pltpu.CompilerParams(vmem_limit_bytes=VMEM),
         cost_estimate=LIGHT,
         name="down_step",
-    )(hidden, *parts, *after)
+    )(hidden, *parts, *given)
 
 
 def shift(parts):
@@ -196,8 +206,8 @@
     def add_up(steps, total):
         return up_step(here, rows, [up[step] for step in steps], total, steps, size)
 
-    def answers(steps):
-        return down_step(hidden, [down[step] for step in steps])
+    def answers(steps, groups=1, buffer=None):
+        return down_step(hidden, [down[step] for step in steps], groups, buffer)
 
     (total,) = advance(up, add_up(UP_GROUPS[0], None))
     total, down[0] = advance(up, add_up(UP_GROUPS[1], total), down[0])
@@ -213,8 +223,9 @@
     last = send_back(third)
     third, back = advance(down, third, back)
     backs += [back, last]
-    advance(down)
-    backs.append(send_back(answers(DOWN_GROUPS[3])))
+    fourth = answers(DOWN_GROUPS[3][:1], 2)
+    (fourth,) = advance(down, fourth)
+    backs.append(send_back(answers(DOWN_GROUPS[3][1:], 2, fourth)))
     mixed = [mix(back) for back in backs]
 
     half = width // size // 2

time: 308 us -> 306 us (level)
  waiting for transfers between devices: 148 us -> 144 us
    all_to_all x4, waiting for transfers between devices: 45.9 us -> 42.1 us  [send_back(): lax.all_to_all(answer.reshape(ep_count, CAP, part), 'ep', split_axis=0, c...]
    pallas_call x4 -> x5, Pallas kernels: 21 us -> 23.5 us  [down_step(): pl.pallas_call(lambda *refs: down_kernel(len(parts), *refs), grid=(1,), i...]
  transfers between devices with their start and end apart: 33 -> 33, of which waited for: 15 -> 15; matrix products, arithmetic and copies ran while one was open for 1% -> 1% of each run, Pallas kernels for 16% -> 18%
where the time goes in v4:
time: 306 us
  waiting for transfers between devices  144 us (47%)
  starting transfers between devices  94.8 us (31%)
  Pallas kernels  57.4 us (19%)
  matrix products  4.61 us (2%)
  local copies, waits for them, and re-layouts  3.73 us (1%)
    ppermute x28, waiting for transfers between devices, shift(): lax.ppermute(part, 'grp', way)  102 us
    all_to_all x4, starting transfers between devices, send_back(): lax.all_to_all(answer.reshape(ep_count, CAP, part), 'ep', split_axis=0, c...  44.8 us
    all_to_all x4, waiting for transfers between devices, send_back(): lax.all_to_all(answer.reshape(ep_count, CAP, part), 'ep', split_axis=0, c...  42.1 us
    ppermute x28, starting transfers between devices, shift(): lax.ppermute(part, 'grp', way)  41.4 us
    pallas_call x3, Pallas kernels, up_step(): pl.pallas_call(lambda *refs: up_kernel(steps, size, *refs), grid_spec=plt...  25.3 us
    pallas_call x5, Pallas kernels, down_step(): pl.pallas_call(lambda *refs: down_kernel(len(parts), *refs), grid=(1,), i...  23.5 us
    pallas_call x2, Pallas kernels, requantize(): pl.pallas_call(requantize_kernel, grid=(height // step,), in_specs=cuts +...  8.64 us
    all_to_all x1, starting transfers between devices, local(): lax.all_to_all(send, 'ep', split_axis=0, concat_axis=0, tiled=True)  8.64 us
  transfers between devices with their start and end apart: 33, of which 15 were waited for; matrix products, arithmetic and copies ran while one was open for 1% of the time, Pallas kernels for 18%

profile of v4, /device:TPU:1, one launch (start us, length us, event | category | flops | bytes accessed | tf_op | source)
XLA Modules:
  0.0 305.7 jit_solution(12915251748474886215)
XLA Ops:
  0.0 0.8 fusion.28
  0.9 0.1 fusion.8
  1.0 0.2 fusion
  1.3 3.2 %convolution_convert_fusion = bf16[512,4096]{1,0:T(8,128)(2,1)} fusion(pred[32,512]{0,1:T(8,128)(4,1)S(1)} %bitcast.121, bf16[1,1,32,4096]{3,2,1,0:T(8,128)(2,1)S(1)} %copy-done), kind=kOutput, calls=%fused_computation | convolution fusion | flops 136314880 | bytes 4472832 | tf_op jit(solution)/shard_map/dot_general | solution.py:186
  4.5 8.6 %all-to-all-start = ((bf16[32,16,4096]{2,1,0:T(8,128)(2,1)}), bf16[32,16,4096]{2,1,0:T(8,128)(2,1)}, u32[]{:S(2)}, u32[]{:S(2)}) async-start(bf16[32,16,4096]{2,1,0:T(8,128)(2,1)} %bitcast.112), calls=%async_computation | async-start | bytes 8388608 | tf_op jit(solution)/shard_map/all_to_all | solution.py:189
  13.2 4.3 %requantize_up.1 = (bf16[512,768]{1,0:T(8,128)(2,1)}, bf16[512,768]{1,0:T(8,128)(2,1)}) custom-call(f32[512,1536]{1,0:T(8,128)} %bitcast.104, f32[512,1536]{1,0:T(8,128)} %bitcast.105, f32[512,1536]{1,0:T(8,128)} %bitcast.106, f32[512,1536]{1,0:T(8,128)} %bitcast.107), custom_call_target="tpu_custom_call" | custom-call | flops 2000000000 | bytes 4000000 | tf_op jit(solution)/shard_map/requantize_up/pallas_call | solution.py:46
  17.5 1.6 collective-permute-start
  19.1 4.0 %collective-permute-start.1 = (bf16[512,768]{1,0:T(8,128)(2,1)}, bf16[512,768]{1,0:T(8,128)(2,1)S(1)}, u32[]{:S(2)}, u32[]{:S(2)}) collective-permute-start(bf16[512,768]{1,0:T(8,128)(2,1)} %get-tuple-element.51.refs_10_), channel_id=1, source_target_pairs={{0,224},{32,0},{64,32},{96,64},{128,96},{160,128},{192,160},{224,1... | collective-permute-start | bytes 2359304 | tf_op jit(solution)/shard_map/ppermute | solution.py:147
  23.1 17.9 %collective-permute-done.refs_11_ = bf16[512,768]{1,0:T(8,128)(2,1)S(1)} collective-permute-done((bf16[512,768]{1,0:T(8,128)(2,1)}, bf16[512,768]{1,0:T(8,128)(2,1)S(1)}, u32[]{:S(2)}, u32[]{:S(2)}) %collective-permute-start) | collective-permute-done | bytes 786464 | tf_op jit(solution)/shard_map/ppermute | solution.py:147
  41.1 2.7 collective-permute-start.3
  43.8 17.0 %collective-permute-done.2.refs_4_.refs_13_ = bf16[512,768]{1,0:T(8,128)(2,1)S(1)} collective-permute-done((bf16[512,768]{1,0:T(8,128)(2,1)S(1)}, bf16[512,768]{1,0:T(8,128)(2,1)S(1)}, u32[]{:S(2)}, u32[]{:S(2)}) %collective-permute-start.2) | collective-permute-done | bytes 786464 | tf_op jit(solution)/shard_map/ppermute | solution.py:147
  60.8 0.8 collective-permute-start.4
  61.6 2.0 collective-permute-start.5
  63.6 4.3 %requantize_down.1 = (bf16[1536,256]{1,0:T(8,128)(2,1)}, bf16[1536,256]{1,0:T(8,128)(2,1)}) custom-call(f32[1536,512]{1,0:T(8,128)} %bitcast.108, f32[1536,512]{1,0:T(8,128)} %bitcast.109, f32[1536,512]{1,0:T(8,128)} %bitcast.110, f32[1536,512]{1,0:T(8,128)} %bitcast.111, bf16[512,768]{1,0:T(8,128)(2,1)} %copy-done.1), custom_call_target="tpu_custom_call" | custom-call | flops 2000000000 | bytes 4000000 | tf_op jit(solution)/shard_map/requantize_down/pallas_call | solution.py:46
  67.9 11.8 %collective-permute-done.4.refs_15_ = bf16[512,768]{1,0:T(8,128)(2,1)S(1)} collective-permute-done((bf16[512,768]{1,0:T(8,128)(2,1)S(1)}, bf16[512,768]{1,0:T(8,128)(2,1)S(1)}, u32[]{:S(2)}, u32[]{:S(2)}) %collective-permute-start.4) | collective-permute-done | bytes 786464 | tf_op jit(solution)/shard_map/ppermute | solution.py:147
  79.7 0.4 collective-permute-start.6
  80.1 2.2 collective-permute-start.7
  82.4 15.2 %collective-permute-done.6.refs_5_ = bf16[512,768]{1,0:T(8,128)(2,1)S(1)} collective-permute-done((bf16[512,768]{1,0:T(8,128)(2,1)S(1)}, bf16[512,768]{1,0:T(8,128)(2,1)S(1)}, u32[]{:S(2)}, u32[]{:S(2)}) %collective-permute-start.6) | collective-permute-done | bytes 786464 | tf_op jit(solution)/shard_map/ppermute | solution.py:147
  97.5 0.4 collective-permute-start.8
  97.9 2.4 collective-permute-start.9
  100.3 14.2 %collective-permute-done.8.refs_7_ = bf16[512,768]{1,0:T(8,128)(2,1)S(1)} collective-permute-done((bf16[512,768]{1,0:T(8,128)(2,1)S(1)}, bf16[512,768]{1,0:T(8,128)(2,1)S(1)}, u32[]{:S(2)}, u32[]{:S(2)}) %collective-permute-start.8) | collective-permute-done | bytes 786464 | tf_op jit(solution)/shard_map/ppermute | solution.py:147
  114.5 0.1 collective-permute-start.10
  114.6 2.7 collective-permute-start.11
  117.3 9.9 %up_step.3.refs_9_ = f32[512,1536]{1,0:T(8,128)} custom-call(s32[1]{0:T(128)} %bitcast.11.refs_0_, bf16[512,4096]{1,0:T(8,128)(2,1)} %bitcast.10.refs_1_.refs_2_.refs_3_.refs_4_.refs_5_.refs_6_.refs_7_.refs_8_, bf16[512,4096]{1,0:T(8,128)(2,1)} %bitcast.10.refs_1_.refs_2_.refs_3_.refs_4_.refs_5_.refs_6_.refs_7_.refs_8_, ...), custom_call_target="tpu_custom_call" | custom-call | flops 2000000000 | bytes 4000000 | tf_op jit(solution)/shard_map/up_step/pallas_call | solution.py:95
  127.3 3.4 %collective-permute-done.10.refs_5_ = bf16[512,768]{1,0:T(8,128)(2,1)} collective-permute-done((bf16[512,768]{1,0:T(8,128)(2,1)S(1)}, bf16[512,768]{1,0:T(8,128)(2,1)}, u32[]{:S(2)}, u32[]{:S(2)}) %collective-permute-start.10) | collective-permute-done | bytes 786464 | tf_op jit(solution)/shard_map/ppermute | solution.py:147
  130.7 2.7 collective-permute-start.13
  133.4 7.8 %up_step.4.refs_9_ = f32[512,1536]{1,0:T(8,128)} custom-call(s32[1]{0:T(128)} %bitcast.11.refs_0_, bf16[512,4096]{1,0:T(8,128)(2,1)} %bitcast.10.refs_1_.refs_2_.refs_3_.refs_4_.refs_5_.refs_6_.refs_7_.refs_8_, bf16[512,4096]{1,0:T(8,128)(2,1)} %bitcast.10.refs_1_.refs_2_.refs_3_.refs_4_.refs_5_.refs_6_.refs_7_.refs_8_, ...), custom_call_target="tpu_custom_call" | custom-call | flops 2000000000 | bytes 4000000 | tf_op jit(solution)/shard_map/up_step/pallas_call | solution.py:95
  141.2 5.2 %collective-permute-done.12.refs_7_ = bf16[512,768]{1,0:T(8,128)(2,1)S(1)} collective-permute-done((bf16[512,768]{1,0:T(8,128)(2,1)}, bf16[512,768]{1,0:T(8,128)(2,1)S(1)}, u32[]{:S(2)}, u32[]{:S(2)}) %collective-permute-start.12) | collective-permute-done | bytes 786464 | tf_op jit(solution)/shard_map/ppermute | solution.py:147
  146.6 2.8 collective-permute-start.15
  149.4 7.5 %up_step.5.refs_0_ = bf16[512,1536]{1,0:T(8,128)(2,1)} custom-call(s32[1]{0:T(128)} %bitcast.11.refs_0_, bf16[512,4096]{1,0:T(8,128)(2,1)} %bitcast.10.refs_1_.refs_2_.refs_3_.refs_4_.refs_5_.refs_6_.refs_7_.refs_8_, bf16[512,4096]{1,0:T(8,128)(2,1)} %bitcast.10.refs_1_.refs_2_.refs_3_.refs_4_.refs_5_.refs_6_.refs_7_.refs_8_, ...), custom_call_target="tpu_custom_call" | custom-call | flops 2000000000 | bytes 4000000 | tf_op jit(solution)/shard_map/up_step/pallas_call | solution.py:95
  156.9 5.6 %collective-permute-done.14.refs_3_ = bf16[1536,256]{1,0:T(8,128)(2,1)S(1)} collective-permute-done((bf16[1536,256]{1,0:T(8,128)(2,1)S(1)}, bf16[1536,256]{1,0:T(8,128)(2,1)S(1)}, u32[]{:S(2)}, u32[]{:S(2)}) %collective-permute-start.14) | collective-permute-done | bytes 786464 | tf_op jit(solution)/shard_map/ppermute | solution.py:147
  162.6 2.7 collective-permute-start.17
  165.3 5.3 %down_step.5 = bf16[512,1024]{1,0:T(8,128)(2,1)} custom-call(bf16[512,1536]{1,0:T(8,128)(2,1)} %up_step.5.refs_0_, bf16[1536,256]{1,0:T(8,128)(2,1)} %get-tuple-element.70.refs_1_, bf16[1536,256]{1,0:T(8,128)(2,1)} %get-tuple-element.71.refs_2_, bf16[1536,256]{1,0:T(8,128)(2,1)} %copy-done.18, bf16[1536,256]{1,0:T(8,128)(2,1)} %copy-done.19), custom_call_target="tpu_custom_call" | custom-call | flops 2000000000 | bytes 4000000 | tf_op jit(solution)/shard_map/down_step/pallas_call | solution.py:130
  170.6 7.9 %collective-permute-done.16.refs_1_ = bf16[1536,256]{1,0:T(8,128)(2,1)S(1)} collective-permute-done((bf16[1536,256]{1,0:T(8,128)(2,1)S(1)}, bf16[1536,256]{1,0:T(8,128)(2,1)S(1)}, u32[]{:S(2)}, u32[]{:S(2)}) %collective-permute-start.16) | collective-permute-done | bytes 786464 | tf_op jit(solution)/shard_map/ppermute | solution.py:147
  178.5 2.9 collective-permute-start.19
  181.4 18.0 %all-to-all-start.1 = ((bf16[32,16,1024]{2,1,0:T(8,128)(2,1)}), bf16[32,16,1024]{2,1,0:T(8,128)(2,1)S(1)}, u32[]{:S(2)}, u32[]{:S(2)}) async-start(bf16[32,16,1024]{2,1,0:T(8,128)(2,1)} %bitcast.117), calls=%async_computation.1 | async-start | bytes 2097152 | tf_op jit(solution)/shard_map/all_to_all | solution.py:198
  199.5 2.7 collective-permute-start.21
  202.2 0.1 select_reduce_fusion
  202.6 0.1 eq.57
  202.7 0.1 fusion.3
  202.8 5.3 %down_step.6 = bf16[512,1024]{1,0:T(8,128)(2,1)} custom-call(bf16[512,1536]{1,0:T(8,128)(2,1)} %up_step.5.refs_0_, bf16[1536,256]{1,0:T(8,128)(2,1)} %copy-done.13, bf16[1536,256]{1,0:T(8,128)(2,1)} %collective-permute-done.17.refs_2_, bf16[1536,256]{1,0:T(8,128)(2,1)} %collective-permute-done.18.refs_3_, bf16[1536,256]{1,0:T(8,128)(2,1)} %collective-permute-done.19.refs_4_), custom_call_target="tpu_custom_call" | custom-call | flops 2000000000 | bytes 4000000 | tf_op jit(solution)/shard_map/down_step/pallas_call | solution.py:130
  208.1 8.2 %all-to-all-done.1 = bf16[32,16,1024]{2,1,0:T(8,128)(2,1)S(1)} async-done(((bf16[32,16,1024]{2,1,0:T(8,128)(2,1)}), bf16[32,16,1024]{2,1,0:T(8,128)(2,1)S(1)}, u32[]{:S(2)}, u32[]{:S(2)}) %all-to-all-start.1) | async-done | bytes 1048608 | tf_op jit(solution)/shard_map/all_to_all | solution.py:198
  216.3 2.7 collective-permute-start.23
  219.0 0.1 pad_maximum_fusion
  219.1 12.3 %all-to-all-start.2 = ((bf16[32,16,1024]{2,1,0:T(8,128)(2,1)}), bf16[32,16,1024]{2,1,0:T(8,128)(2,1)S(1)}, u32[]{:S(2)}, u32[]{:S(2)}) async-start(bf16[32,16,1024]{2,1,0:T(8,128)(2,1)} %bitcast.118), calls=%async_computation.2 | async-start | bytes 2097152 | tf_op jit(solution)/shard_map/all_to_all | solution.py:198
  231.4 0.3 fusion.33
  231.7 0.4 collective-permute-done.22.refs_3_
  232.2 0.9 copy-done.17
  233.1 2.7 collective-permute-start.25
  235.8 5.3 %down_step.7 = bf16[512,1024]{1,0:T(8,128)(2,1)} custom-call(bf16[512,1536]{1,0:T(8,128)(2,1)} %up_step.5.refs_0_, bf16[1536,256]{1,0:T(8,128)(2,1)} %collective-permute-done.20.refs_1_, bf16[1536,256]{1,0:T(8,128)(2,1)} %collective-permute-done.21.refs_2_, bf16[1536,256]{1,0:T(8,128)(2,1)} %copy-done.17, bf16[1536,256]{1,0:T(8,128)(2,1)} %collective-permute-done.23.refs_4_), custom_call_target="tpu_custom_call" | custom-call | flops 2000000000 | bytes 4000000 | tf_op jit(solution)/shard_map/down_step/pallas_call | solution.py:130
  241.1 7.2 %all-to-all-done.2 = bf16[32,16,1024]{2,1,0:T(8,128)(2,1)S(1)} async-done(((bf16[32,16,1024]{2,1,0:T(8,128)(2,1)}), bf16[32,16,1024]{2,1,0:T(8,128)(2,1)S(1)}, u32[]{:S(2)}, u32[]{:S(2)}) %all-to-all-start.2) | async-done | bytes 1048608 | tf_op jit(solution)/shard_map/all_to_all | solution.py:198
  248.3 6.5 %all-to-all-start.3 = ((bf16[32,16,1024]{2,1,0:T(8,128)(2,1)}), bf16[32,16,1024]{2,1,0:T(8,128)(2,1)S(1)}, u32[]{:S(2)}, u32[]{:S(2)}) async-start(bf16[32,16,1024]{2,1,0:T(8,128)(2,1)} %bitcast.119), calls=%async_computation.3 | async-start | bytes 2097152 | tf_op jit(solution)/shard_map/all_to_all | solution.py:198
  254.9 2.7 collective-permute-start.27
  257.6 0.3 fusion.34
  258.0 3.9 %down_step.8.refs_3_ = bf16[512,1024]{1,0:T(8,128)(2,1)} custom-call(bf16[512,1536]{1,0:T(8,128)(2,1)} %up_step.5.refs_0_, bf16[1536,256]{1,0:T(8,128)(2,1)} %copy-done.16, bf16[1536,256]{1,0:T(8,128)(2,1)} %collective-permute-done.25.refs_2_), custom_call_target="tpu_custom_call" | custom-call | flops 2000000000 | bytes 4000000 | tf_op jit(solution)/shard_map/down_step/pallas_call | solution.py:130
  261.8 9.9 %all-to-all-done.3 = bf16[32,16,1024]{2,1,0:T(8,128)(2,1)S(1)} async-done(((bf16[32,16,1024]{2,1,0:T(8,128)(2,1)}), bf16[32,16,1024]{2,1,0:T(8,128)(2,1)S(1)}, u32[]{:S(2)}, u32[]{:S(2)}) %all-to-all-start.3) | async-done | bytes 1048608 | tf_op jit(solution)/shard_map/all_to_all | solution.py:198
  271.7 0.3 fusion.35
  272.0 3.1 %collective-permute-done.26.refs_1_ = bf16[1536,256]{1,0:T(8,128)(2,1)} collective-permute-done((bf16[1536,256]{1,0:T(8,128)(2,1)S(1)}, bf16[1536,256]{1,0:T(8,128)(2,1)}, u32[]{:S(2)}, u32[]{:S(2)}) %collective-permute-start.26) | collective-permute-done | bytes 786464 | tf_op jit(solution)/shard_map/ppermute | solution.py:147
  275.1 3.8 %down_step.9 = bf16[512,1024]{1,0:T(8,128)(2,1)} custom-call(bf16[512,1536]{1,0:T(8,128)(2,1)} %up_step.5.refs_0_, bf16[1536,256]{1,0:T(8,128)(2,1)} %collective-permute-done.26.refs_1_, bf16[1536,256]{1,0:T(8,128)(2,1)} %collective-permute-done.27.refs_2_, bf16[512,1024]{1,0:T(8,128)(2,1)} %down_step.8.refs_3_), custom_call_target="tpu_custom_call", output_to_operand_aliasing={{}: (3, {})} | custom-call | flops 2000000000 | bytes 4000000 | tf_op jit(solution)/shard_map/down_step/pallas_call | solution.py:130
  279.0 8.1 %all-to-all-start.4 = ((bf16[32,16,1024]{2,1,0:T(8,128)(2,1)}), bf16[32,16,1024]{2,1,0:T(8,128)(2,1)S(1)}, u32[]{:S(2)}, u32[]{:S(2)}) async-start(bf16[32,16,1024]{2,1,0:T(8,128)(2,1)} %bitcast.120), calls=%async_computation.4 | async-start | bytes 2097152 | tf_op jit(solution)/shard_map/all_to_all | solution.py:198
  287.1 16.8 %all-to-all-done.4 = bf16[32,16,1024]{2,1,0:T(8,128)(2,1)S(1)} async-done(((bf16[32,16,1024]{2,1,0:T(8,128)(2,1)}), bf16[32,16,1024]{2,1,0:T(8,128)(2,1)S(1)}, u32[]{:S(2)}, u32[]{:S(2)}) %all-to-all-start.4) | async-done | bytes 1048608 | tf_op jit(solution)/shard_map/all_to_all | solution.py:198
  304.0 0.3 fusion.36
  304.4 0.7 copy-done.11
  305.1 0.6 fusion.9
  (94 shorter events, 1.2 us)
Async XLA Ops:
  0.0 1.3 copy-start
  4.5 110.0 %all-to-all-start = ((bf16[32,16,4096]{2,1,0:T(8,128)(2,1)}), bf16[32,16,4096]{2,1,0:T(8,128)(2,1)}, u32[]{:S(2)}, u32[]{:S(2)}) async-start(bf16[32,16,4096]{2,1,0:T(8,128)(2,1)} %bitcast.112), calls=%async_computation | async-start | bytes 8388608 | tf_op jit(solution)/shard_map/all_to_all | solution.py:189
  17.5 23.6 %collective-permute-start = (bf16[512,768]{1,0:T(8,128)(2,1)}, bf16[512,768]{1,0:T(8,128)(2,1)S(1)}, u32[]{:S(2)}, u32[]{:S(2)}) collective-permute-start(bf16[512,768]{1,0:T(8,128)(2,1)} %get-tuple-element.50.refs_9_), channel_id=1, source_target_pairs={{0,32},{32,64},{64,96},{96,128},{128,160},{160,192},{192,224},{224... | collective-permute-start | bytes 2359304 | tf_op jit(solution)/shard_map/ppermute | solution.py:147
  19.1 21.9 %collective-permute-start.1 = (bf16[512,768]{1,0:T(8,128)(2,1)}, bf16[512,768]{1,0:T(8,128)(2,1)S(1)}, u32[]{:S(2)}, u32[]{:S(2)}) collective-permute-start(bf16[512,768]{1,0:T(8,128)(2,1)} %get-tuple-element.51.refs_10_), channel_id=1, source_target_pairs={{0,224},{32,0},{64,32},{96,64},{128,96},{160,128},{192,160},{224,1... | collective-permute-start | bytes 2359304 | tf_op jit(solution)/shard_map/ppermute | solution.py:147
  41.0 19.8 %copy-start.5 = (bf16[512,768]{1,0:T(8,128)(2,1)}, bf16[512,768]{1,0:T(8,128)(2,1)S(1)}, u32[]{:S(2)}) copy-start(bf16[512,768]{1,0:T(8,128)(2,1)S(1)} %collective-permute-done.refs_11_) | copy-start | bytes 2359300
  41.1 19.8 %copy-start.6 = (bf16[512,768]{1,0:T(8,128)(2,1)}, bf16[512,768]{1,0:T(8,128)(2,1)S(1)}, u32[]{:S(2)}) copy-start(bf16[512,768]{1,0:T(8,128)(2,1)S(1)} %collective-permute-done.1.refs_12_) | copy-start | bytes 2359300
  41.1 19.8 %collective-permute-start.2 = (bf16[512,768]{1,0:T(8,128)(2,1)S(1)}, bf16[512,768]{1,0:T(8,128)(2,1)S(1)}, u32[]{:S(2)}, u32[]{:S(2)}) collective-permute-start(bf16[512,768]{1,0:T(8,128)(2,1)S(1)} %collective-permute-done.refs_11_), channel_id=1, source_target_pairs={{0,32},{32,64},{64,96},{96,128},{128,160},{160,192},{192,224},{224... | collective-permute-start | bytes 2359304 | tf_op jit(solution)/shard_map/ppermute | solution.py:147
  41.1 19.7 %collective-permute-start.3 = (bf16[512,768]{1,0:T(8,128)(2,1)S(1)}, bf16[512,768]{1,0:T(8,128)(2,1)S(1)}, u32[]{:S(2)}, u32[]{:S(2)}) collective-permute-start(bf16[512,768]{1,0:T(8,128)(2,1)S(1)} %collective-permute-done.1.refs_12_), channel_id=1, source_target_pairs={{0,224},{32,0},{64,32},{96,64},{128,96},{160,128},{192,160},{224,1... | collective-permute-start | bytes 2359304 | tf_op jit(solution)/shard_map/ppermute | solution.py:147
  60.8 2.8 copy-start.1
  60.8 7.1 %copy-start.7 = (bf16[512,768]{1,0:T(8,128)(2,1)}, bf16[512,768]{1,0:T(8,128)(2,1)S(1)}, u32[]{:S(2)}) copy-start(bf16[512,768]{1,0:T(8,128)(2,1)S(1)} %collective-permute-done.3.refs_14_) | copy-start | bytes 2359300
  60.8 18.8 %collective-permute-start.4 = (bf16[512,768]{1,0:T(8,128)(2,1)S(1)}, bf16[512,768]{1,0:T(8,128)(2,1)S(1)}, u32[]{:S(2)}, u32[]{:S(2)}) collective-permute-start(bf16[512,768]{1,0:T(8,128)(2,1)S(1)} %collective-permute-done.2.refs_4_.refs_13_), channel_id=1, source_target_pairs={{0,32},{32,64},{64,96},{96,128},{128,160},{160,192},{192,224},{224... | collective-permute-start | bytes 2359304 | tf_op jit(solution)/shard_map/ppermute | solution.py:147
  61.6 18.1 %collective-permute-start.5 = (bf16[512,768]{1,0:T(8,128)(2,1)S(1)}, bf16[512,768]{1,0:T(8,128)(2,1)}, u32[]{:S(2)}, u32[]{:S(2)}) collective-permute-start(bf16[512,768]{1,0:T(8,128)(2,1)S(1)} %collective-permute-done.3.refs_14_), channel_id=1, source_target_pairs={{0,224},{32,0},{64,32},{96,64},{128,96},{160,128},{192,160},{224,1... | collective-permute-start | bytes 2359304 | tf_op jit(solution)/shard_map/ppermute | solution.py:147
  79.7 17.8 %copy-start.8 = (bf16[512,768]{1,0:T(8,128)(2,1)}, bf16[512,768]{1,0:T(8,128)(2,1)S(1)}, u32[]{:S(2)}) copy-start(bf16[512,768]{1,0:T(8,128)(2,1)S(1)} %collective-permute-done.4.refs_15_) | copy-start | bytes 2359300
  79.7 17.8 %collective-permute-start.6 = (bf16[512,768]{1,0:T(8,128)(2,1)S(1)}, bf16[512,768]{1,0:T(8,128)(2,1)S(1)}, u32[]{:S(2)}, u32[]{:S(2)}) collective-permute-start(bf16[512,768]{1,0:T(8,128)(2,1)S(1)} %collective-permute-done.4.refs_15_), channel_id=1, source_target_pairs={{0,32},{32,64},{64,96},{96,128},{128,160},{160,192},{192,224},{224... | collective-permute-start | bytes 2359304 | tf_op jit(solution)/shard_map/ppermute | solution.py:147
  80.1 17.4 %collective-permute-start.7 = (bf16[512,768]{1,0:T(8,128)(2,1)}, bf16[512,768]{1,0:T(8,128)(2,1)S(1)}, u32[]{:S(2)}, u32[]{:S(2)}) collective-permute-start(bf16[512,768]{1,0:T(8,128)(2,1)} %collective-permute-done.5.refs_16_), channel_id=1, source_target_pairs={{0,224},{32,0},{64,32},{96,64},{128,96},{160,128},{192,160},{224,1... | collective-permute-start | bytes 2359304 | tf_op jit(solution)/shard_map/ppermute | solution.py:147
  97.5 29.7 %copy-start.2 = (bf16[512,768]{1,0:T(8,128)(2,1)}, bf16[512,768]{1,0:T(8,128)(2,1)S(1)}, u32[]{:S(2)}) copy-start(bf16[512,768]{1,0:T(8,128)(2,1)S(1)} %collective-permute-done.6.refs_5_) | copy-start | bytes 2359300
  97.5 29.7 %copy-start.3 = (bf16[512,768]{1,0:T(8,128)(2,1)}, bf16[512,768]{1,0:T(8,128)(2,1)S(1)}, u32[]{:S(2)}) copy-start(bf16[512,768]{1,0:T(8,128)(2,1)S(1)} %collective-permute-done.7.refs_6_) | copy-start | bytes 2359300
  97.5 17.0 %collective-permute-start.8 = (bf16[512,768]{1,0:T(8,128)(2,1)S(1)}, bf16[512,768]{1,0:T(8,128)(2,1)S(1)}, u32[]{:S(2)}, u32[]{:S(2)}) collective-permute-start(bf16[512,768]{1,0:T(8,128)(2,1)S(1)} %collective-permute-done.6.refs_5_), channel_id=1, source_target_pairs={{0,32},{32,64},{64,96},{96,128},{128,160},{160,192},{192,224},{224... | collective-permute-start | bytes 2359304 | tf_op jit(solution)/shard_map/ppermute | solution.py:147
  97.9 16.6 %collective-permute-start.9 = (bf16[512,768]{1,0:T(8,128)(2,1)S(1)}, bf16[512,768]{1,0:T(8,128)(2,1)}, u32[]{:S(2)}, u32[]{:S(2)}) collective-permute-start(bf16[512,768]{1,0:T(8,128)(2,1)S(1)} %collective-permute-done.7.refs_6_), channel_id=1, source_target_pairs={{0,224},{32,0},{64,32},{96,64},{128,96},{160,128},{192,160},{224,1... | collective-permute-start | bytes 2359304 | tf_op jit(solution)/shard_map/ppermute | solution.py:147
  114.5 12.7 %copy-start.4 = (bf16[512,768]{1,0:T(8,128)(2,1)}, bf16[512,768]{1,0:T(8,128)(2,1)S(1)}, u32[]{:S(2)}) copy-start(bf16[512,768]{1,0:T(8,128)(2,1)S(1)} %collective-permute-done.8.refs_7_) | copy-start | bytes 2359300
  114.5 16.2 %collective-permute-start.10 = (bf16[512,768]{1,0:T(8,128)(2,1)S(1)}, bf16[512,768]{1,0:T(8,128)(2,1)}, u32[]{:S(2)}, u32[]{:S(2)}) collective-permute-start(bf16[512,768]{1,0:T(8,128)(2,1)S(1)} %collective-permute-done.8.refs_7_), channel_id=1, source_target_pairs={{0,32},{32,64},{64,96},{96,128},{128,160},{160,192},{192,224},{224... | collective-permute-start | bytes 2359304 | tf_op jit(solution)/shard_map/ppermute | solution.py:147
  114.6 16.1 %collective-permute-start.11 = (bf16[512,768]{1,0:T(8,128)(2,1)}, bf16[512,768]{1,0:T(8,128)(2,1)}, u32[]{:S(2)}, u32[]{:S(2)}) collective-permute-start(bf16[512,768]{1,0:T(8,128)(2,1)} %collective-permute-done.9.refs_8_), channel_id=1, source_target_pairs={{0,224},{32,0},{64,32},{96,64},{128,96},{160,128},{192,160},{224,1... | collective-permute-start | bytes 2359304 | tf_op jit(solution)/shard_map/ppermute | solution.py:147
  127.3 19.2 %copy-start.14 = (bf16[1536,256]{1,0:T(8,128)(2,1)S(1)}, bf16[1536,256]{1,0:T(8,128)(2,1)}, u32[]{:S(2)}) copy-start(bf16[1536,256]{1,0:T(8,128)(2,1)} %get-tuple-element.70.refs_1_) | copy-start | bytes 2359300
  127.3 19.3 %copy-start.15 = (bf16[1536,256]{1,0:T(8,128)(2,1)S(1)}, bf16[1536,256]{1,0:T(8,128)(2,1)}, u32[]{:S(2)}) copy-start(bf16[1536,256]{1,0:T(8,128)(2,1)} %get-tuple-element.71.refs_2_) | copy-start | bytes 2359300
  130.7 15.8 %collective-permute-start.12 = (bf16[512,768]{1,0:T(8,128)(2,1)}, bf16[512,768]{1,0:T(8,128)(2,1)S(1)}, u32[]{:S(2)}, u32[]{:S(2)}) collective-permute-start(bf16[512,768]{1,0:T(8,128)(2,1)} %collective-permute-done.10.refs_5_), channel_id=1, source_target_pairs={{0,32},{32,64},{64,96},{96,128},{128,160},{160,192},{192,224},{224... | collective-permute-start | bytes 2359304 | tf_op jit(solution)/shard_map/ppermute | solution.py:147
  130.7 15.8 %collective-permute-start.13 = (bf16[512,768]{1,0:T(8,128)(2,1)}, bf16[512,768]{1,0:T(8,128)(2,1)S(1)}, u32[]{:S(2)}, u32[]{:S(2)}) collective-permute-start(bf16[512,768]{1,0:T(8,128)(2,1)} %collective-permute-done.11.refs_6_), channel_id=1, source_target_pairs={{0,224},{32,0},{64,32},{96,64},{128,96},{160,128},{192,160},{224,1... | collective-permute-start | bytes 2359304 | tf_op jit(solution)/shard_map/ppermute | solution.py:147
  146.5 2.9 copy-start.9
  146.5 2.9 copy-start.10
  146.5 16.0 %collective-permute-start.14 = (bf16[1536,256]{1,0:T(8,128)(2,1)S(1)}, bf16[1536,256]{1,0:T(8,128)(2,1)S(1)}, u32[]{:S(2)}, u32[]{:S(2)}) collective-permute-start(bf16[1536,256]{1,0:T(8,128)(2,1)S(1)} %copy-done.14), channel_id=1, source_target_pairs={{0,32},{32,64},{64,96},{96,128},{128,160},{160,192},{192,224},{224... | collective-permute-start | bytes 2359304 | tf_op jit(solution)/shard_map/ppermute | solution.py:147
  146.6 15.9 %collective-permute-start.15 = (bf16[1536,256]{1,0:T(8,128)(2,1)S(1)}, bf16[1536,256]{1,0:T(8,128)(2,1)S(1)}, u32[]{:S(2)}, u32[]{:S(2)}) collective-permute-start(bf16[1536,256]{1,0:T(8,128)(2,1)S(1)} %copy-done.15), channel_id=1, source_target_pairs={{0,224},{32,0},{64,32},{96,64},{128,96},{160,128},{192,160},{224,1... | collective-permute-start | bytes 2359304 | tf_op jit(solution)/shard_map/ppermute | solution.py:147
  156.9 45.2 %copy-start.12 = (f32[1,1,32,8]{2,3,1,0:T(8,128)S(1)}, f32[1,1,32,8]{2,3,1,0:T(8,128)}, u32[]{:S(2)}) copy-start(f32[1,1,32,8]{2,3,1,0:T(8,128)} %param.6) | copy-start | bytes 3076
  162.5 2.8 copy-start.18
  162.5 2.8 copy-start.19
  162.5 15.9 %collective-permute-start.16 = (bf16[1536,256]{1,0:T(8,128)(2,1)S(1)}, bf16[1536,256]{1,0:T(8,128)(2,1)S(1)}, u32[]{:S(2)}, u32[]{:S(2)}) collective-permute-start(bf16[1536,256]{1,0:T(8,128)(2,1)S(1)} %collective-permute-done.14.refs_3_), channel_id=1, source_target_pairs={{0,32},{32,64},{64,96},{96,128},{128,160},{160,192},{192,224},{224... | collective-permute-start | bytes 2359304 | tf_op jit(solution)/shard_map/ppermute | solution.py:147
  162.6 15.9 %collective-permute-start.17 = (bf16[1536,256]{1,0:T(8,128)(2,1)S(1)}, bf16[1536,256]{1,0:T(8,128)(2,1)}, u32[]{:S(2)}, u32[]{:S(2)}) collective-permute-start(bf16[1536,256]{1,0:T(8,128)(2,1)S(1)} %collective-permute-done.15.refs_4_), channel_id=1, source_target_pairs={{0,224},{32,0},{64,32},{96,64},{128,96},{160,128},{192,160},{224,1... | collective-permute-start | bytes 2359304 | tf_op jit(solution)/shard_map/ppermute | solution.py:147
  178.5 24.4 %copy-start.13 = (bf16[1536,256]{1,0:T(8,128)(2,1)}, bf16[1536,256]{1,0:T(8,128)(2,1)S(1)}, u32[]{:S(2)}) copy-start(bf16[1536,256]{1,0:T(8,128)(2,1)S(1)} %collective-permute-done.16.refs_1_) | copy-start | bytes 2359300
  178.5 20.9 %collective-permute-start.18 = (bf16[1536,256]{1,0:T(8,128)(2,1)S(1)}, bf16[1536,256]{1,0:T(8,128)(2,1)}, u32[]{:S(2)}, u32[]{:S(2)}) collective-permute-start(bf16[1536,256]{1,0:T(8,128)(2,1)S(1)} %collective-permute-done.16.refs_1_), channel_id=1, source_target_pairs={{0,32},{32,64},{64,96},{96,128},{128,160},{160,192},{192,224},{224... | collective-permute-start | bytes 2359304 | tf_op jit(solution)/shard_map/ppermute | solution.py:147
  178.5 20.9 %collective-permute-start.19 = (bf16[1536,256]{1,0:T(8,128)(2,1)}, bf16[1536,256]{1,0:T(8,128)(2,1)}, u32[]{:S(2)}, u32[]{:S(2)}) collective-permute-start(bf16[1536,256]{1,0:T(8,128)(2,1)} %collective-permute-done.17.refs_2_), channel_id=1, source_target_pairs={{0,224},{32,0},{64,32},{96,64},{128,96},{160,128},{192,160},{224,1... | collective-permute-start | bytes 2359304 | tf_op jit(solution)/shard_map/ppermute | solution.py:147
  181.4 34.9 %all-to-all-start.1 = ((bf16[32,16,1024]{2,1,0:T(8,128)(2,1)}), bf16[32,16,1024]{2,1,0:T(8,128)(2,1)S(1)}, u32[]{:S(2)}, u32[]{:S(2)}) async-start(bf16[32,16,1024]{2,1,0:T(8,128)(2,1)} %bitcast.117), calls=%async_computation.1 | async-start | bytes 2097152 | tf_op jit(solution)/shard_map/all_to_all | solution.py:198
  199.4 16.9 %collective-permute-start.20 = (bf16[1536,256]{1,0:T(8,128)(2,1)}, bf16[1536,256]{1,0:T(8,128)(2,1)}, u32[]{:S(2)}, u32[]{:S(2)}) collective-permute-start(bf16[1536,256]{1,0:T(8,128)(2,1)} %collective-permute-done.18.refs_3_), channel_id=1, source_target_pairs={{0,32},{32,64},{64,96},{96,128},{128,160},{160,192},{192,224},{224... | collective-permute-start | bytes 2359304 | tf_op jit(solution)/shard_map/ppermute | solution.py:147
  199.5 16.8 %collective-permute-start.21 = (bf16[1536,256]{1,0:T(8,128)(2,1)}, bf16[1536,256]{1,0:T(8,128)(2,1)}, u32[]{:S(2)}, u32[]{:S(2)}) collective-permute-start(bf16[1536,256]{1,0:T(8,128)(2,1)} %collective-permute-done.19.refs_4_), channel_id=1, source_target_pairs={{0,224},{32,0},{64,32},{96,64},{128,96},{160,128},{192,160},{224,1... | collective-permute-start | bytes 2359304 | tf_op jit(solution)/shard_map/ppermute | solution.py:147
  216.3 15.9 %collective-permute-start.22 = (bf16[1536,256]{1,0:T(8,128)(2,1)}, bf16[1536,256]{1,0:T(8,128)(2,1)S(1)}, u32[]{:S(2)}, u32[]{:S(2)}) collective-permute-start(bf16[1536,256]{1,0:T(8,128)(2,1)} %collective-permute-done.20.refs_1_), channel_id=1, source_target_pairs={{0,32},{32,64},{64,96},{96,128},{128,160},{160,192},{192,224},{224... | collective-permute-start | bytes 2359304 | tf_op jit(solution)/shard_map/ppermute | solution.py:147
  216.3 16.8 %collective-permute-start.23 = (bf16[1536,256]{1,0:T(8,128)(2,1)}, bf16[1536,256]{1,0:T(8,128)(2,1)}, u32[]{:S(2)}, u32[]{:S(2)}) collective-permute-start(bf16[1536,256]{1,0:T(8,128)(2,1)} %collective-permute-done.21.refs_2_), channel_id=1, source_target_pairs={{0,224},{32,0},{64,32},{96,64},{128,96},{160,128},{192,160},{224,1... | collective-permute-start | bytes 2359304 | tf_op jit(solution)/shard_map/ppermute | solution.py:147
  219.1 29.2 %all-to-all-start.2 = ((bf16[32,16,1024]{2,1,0:T(8,128)(2,1)}), bf16[32,16,1024]{2,1,0:T(8,128)(2,1)S(1)}, u32[]{:S(2)}, u32[]{:S(2)}) async-start(bf16[32,16,1024]{2,1,0:T(8,128)(2,1)} %bitcast.118), calls=%async_computation.2 | async-start | bytes 2097152 | tf_op jit(solution)/shard_map/all_to_all | solution.py:198
  232.2 0.9 copy-start.17
  233.1 21.7 %collective-permute-start.24 = (bf16[1536,256]{1,0:T(8,128)(2,1)}, bf16[1536,256]{1,0:T(8,128)(2,1)S(1)}, u32[]{:S(2)}, u32[]{:S(2)}) collective-permute-start(bf16[1536,256]{1,0:T(8,128)(2,1)} %copy-done.17), channel_id=1, source_target_pairs={{0,32},{32,64},{64,96},{96,128},{128,160},{160,192},{192,224},{224... | collective-permute-start | bytes 2359304 | tf_op jit(solution)/shard_map/ppermute | solution.py:147
  233.1 21.7 %collective-permute-start.25 = (bf16[1536,256]{1,0:T(8,128)(2,1)}, bf16[1536,256]{1,0:T(8,128)(2,1)}, u32[]{:S(2)}, u32[]{:S(2)}) collective-permute-start(bf16[1536,256]{1,0:T(8,128)(2,1)} %collective-permute-done.23.refs_4_), channel_id=1, source_target_pairs={{0,224},{32,0},{64,32},{96,64},{128,96},{160,128},{192,160},{224,1... | collective-permute-start | bytes 2359304 | tf_op jit(solution)/shard_map/ppermute | solution.py:147
  248.3 23.4 %all-to-all-start.3 = ((bf16[32,16,1024]{2,1,0:T(8,128)(2,1)}), bf16[32,16,1024]{2,1,0:T(8,128)(2,1)S(1)}, u32[]{:S(2)}, u32[]{:S(2)}) async-start(bf16[32,16,1024]{2,1,0:T(8,128)(2,1)} %bitcast.119), calls=%async_computation.3 | async-start | bytes 2097152 | tf_op jit(solution)/shard_map/all_to_all | solution.py:198
  254.8 3.2 %copy-start.16 = (bf16[1536,256]{1,0:T(8,128)(2,1)}, bf16[1536,256]{1,0:T(8,128)(2,1)S(1)}, u32[]{:S(2)}) copy-start(bf16[1536,256]{1,0:T(8,128)(2,1)S(1)} %collective-permute-done.24.refs_1_) | copy-start | bytes 2359300
  254.8 20.3 %collective-permute-start.26 = (bf16[1536,256]{1,0:T(8,128)(2,1)S(1)}, bf16[1536,256]{1,0:T(8,128)(2,1)}, u32[]{:S(2)}, u32[]{:S(2)}) collective-permute-start(bf16[1536,256]{1,0:T(8,128)(2,1)S(1)} %collective-permute-done.24.refs_1_), channel_id=1, source_target_pairs={{0,32},{32,64},{64,96},{96,128},{128,160},{160,192},{192,224},{224... | collective-permute-start | bytes 2359304 | tf_op jit(solution)/shard_map/ppermute | solution.py:147
  254.9 20.2 %collective-permute-start.27 = (bf16[1536,256]{1,0:T(8,128)(2,1)}, bf16[1536,256]{1,0:T(8,128)(2,1)}, u32[]{:S(2)}, u32[]{:S(2)}) collective-permute-start(bf16[1536,256]{1,0:T(8,128)(2,1)} %collective-permute-done.25.refs_2_), channel_id=1, source_target_pairs={{0,224},{32,0},{64,32},{96,64},{128,96},{160,128},{192,160},{224,1... | collective-permute-start | bytes 2359304 | tf_op jit(solution)/shard_map/ppermute | solution.py:147
  279.0 25.0 %all-to-all-start.4 = ((bf16[32,16,1024]{2,1,0:T(8,128)(2,1)}), bf16[32,16,1024]{2,1,0:T(8,128)(2,1)S(1)}, u32[]{:S(2)}, u32[]{:S(2)}) async-start(bf16[32,16,1024]{2,1,0:T(8,128)(2,1)} %bitcast.120), calls=%async_computation.4 | async-start | bytes 2097152 | tf_op jit(solution)/shard_map/all_to_all | solution.py:198
  304.4 0.7 copy-start.11

commit v5 on v4

--- a/solution.py
+++ b/solution.py
@@ -182,13 +182,13 @@
         axis=0,
     )
 
-    up = [requantize(master_up[0], BLK, "requantize_up")]
+    up = [requantize(master_up[0], 2 * BLK, "requantize_up")]
     send = lax.dot_general(place, tokens, (((0,), (0,)), ((), ())), preferred_element_type=jnp.float32)
     send = send.astype(jnp.bfloat16).reshape(ep_count, CAP, width)
     advance(up)
     rows = lax.all_to_all(send, "ep", split_axis=0, concat_axis=0, tiled=True).reshape(slot_total, width)
     advance(up)
-    down = [requantize(master_down[0], 3 * BLK, "requantize_down", up[2][:1])]
+    down = [requantize(master_down[0], 6 * BLK, "requantize_down", up[2][:1])]
     (down[0],) = advance(up, down[0])
     advance(up)
     (rows,) = advance(up, rows)

time: 306 us -> 305 us (level)
  transfers between devices with their start and end apart: 33 -> 33, of which waited for: 15 -> 15; matrix products, arithmetic and copies ran while one was open for 1% -> 1% of each run, Pallas kernels for 18% -> 17%
where the time goes in v5:
time: 305 us; the launch traced here: 304 us
  waiting for transfers between devices  145 us (48%)
  starting transfers between devices  94.8 us (31%)
  Pallas kernels  54.9 us (18%)
  matrix products  4.61 us (2%)
  local copies, waits for them, and re-layouts  3.73 us (1%)
    ppermute x28, waiting for transfers between devices, shift(): lax.ppermute(part, 'grp', way)  103 us
    all_to_all x4, starting transfers between devices, send_back(): lax.all_to_all(answer.reshape(ep_count, CAP, part), 'ep', split_axis=0, c...  44.8 us
    all_to_all x4, waiting for transfers between devices, send_back(): lax.all_to_all(answer.reshape(ep_count, CAP, part), 'ep', split_axis=0, c...  42.1 us
    ppermute x28, starting transfers between devices, shift(): lax.ppermute(part, 'grp', way)  41.4 us
    pallas_call x3, Pallas kernels, up_step(): pl.pallas_call(lambda *refs: up_kernel(steps, size, *refs), grid_spec=plt...  25.3 us
    pallas_call x5, Pallas kernels, down_step(): pl.pallas_call(lambda *refs: down_kernel(len(parts), *refs), grid=(1,), i...  23.5 us
    all_to_all x1, starting transfers between devices, local(): lax.all_to_all(send, 'ep', split_axis=0, concat_axis=0, tiled=True)  8.64 us
  transfers between devices with their start and end apart: 33, of which 15 were waited for; matrix products, arithmetic and copies ran while one was open for 1% of the time, Pallas kernels for 17%

profile of v5, /device:TPU:1, one launch (start us, length us, event | category | flops | bytes accessed | tf_op | source)
XLA Modules:
  0.0 304.4 jit_solution(449904314223940654)
XLA Ops:
  0.0 0.8 fusion.28
  0.9 0.1 fusion.8
  1.0 0.2 fusion
  1.3 3.2 %convolution_convert_fusion = bf16[512,4096]{1,0:T(8,128)(2,1)} fusion(pred[32,512]{0,1:T(8,128)(4,1)S(1)} %bitcast.121, bf16[1,1,32,4096]{3,2,1,0:T(8,128)(2,1)S(1)} %copy-done), kind=kOutput, calls=%fused_computation | convolution fusion | flops 136314880 | bytes 4472832 | tf_op jit(solution)/shard_map/dot_general | solution.py:186
  4.5 8.6 %all-to-all-start = ((bf16[32,16,4096]{2,1,0:T(8,128)(2,1)}), bf16[32,16,4096]{2,1,0:T(8,128)(2,1)}, u32[]{:S(2)}, u32[]{:S(2)}) async-start(bf16[32,16,4096]{2,1,0:T(8,128)(2,1)} %bitcast.112), calls=%async_computation | async-start | bytes 8388608 | tf_op jit(solution)/shard_map/all_to_all | solution.py:189
  13.2 3.0 requantize_up.1
  16.2 1.6 collective-permute-start
  17.8 4.0 %collective-permute-start.1 = (bf16[512,768]{1,0:T(8,128)(2,1)}, bf16[512,768]{1,0:T(8,128)(2,1)S(1)}, u32[]{:S(2)}, u32[]{:S(2)}) collective-permute-start(bf16[512,768]{1,0:T(8,128)(2,1)} %get-tuple-element.51.refs_10_), channel_id=1, source_target_pairs={{0,224},{32,0},{64,32},{96,64},{128,96},{160,128},{192,160},{224,1... | collective-permute-start | bytes 2359304 | tf_op jit(solution)/shard_map/ppermute | solution.py:147
  21.9 17.9 %collective-permute-done.refs_11_ = bf16[512,768]{1,0:T(8,128)(2,1)S(1)} collective-permute-done((bf16[512,768]{1,0:T(8,128)(2,1)}, bf16[512,768]{1,0:T(8,128)(2,1)S(1)}, u32[]{:S(2)}, u32[]{:S(2)}) %collective-permute-start) | collective-permute-done | bytes 786464 | tf_op jit(solution)/shard_map/ppermute | solution.py:147
  39.9 2.7 collective-permute-start.3
  42.5 17.0 %collective-permute-done.2.refs_4_.refs_13_ = bf16[512,768]{1,0:T(8,128)(2,1)S(1)} collective-permute-done((bf16[512,768]{1,0:T(8,128)(2,1)S(1)}, bf16[512,768]{1,0:T(8,128)(2,1)S(1)}, u32[]{:S(2)}, u32[]{:S(2)}) %collective-permute-start.2) | collective-permute-done | bytes 786464 | tf_op jit(solution)/shard_map/ppermute | solution.py:147
  59.6 0.8 collective-permute-start.4
  60.3 2.0 collective-permute-start.5
  62.3 3.1 %requantize_down.1 = (bf16[1536,256]{1,0:T(8,128)(2,1)}, bf16[1536,256]{1,0:T(8,128)(2,1)}) custom-call(f32[1536,512]{1,0:T(8,128)} %bitcast.108, f32[1536,512]{1,0:T(8,128)} %bitcast.109, f32[1536,512]{1,0:T(8,128)} %bitcast.110, f32[1536,512]{1,0:T(8,128)} %bitcast.111, bf16[512,768]{1,0:T(8,128)(2,1)} %copy-done.1), custom_call_target="tpu_custom_call" | custom-call | flops 2000000000 | bytes 4000000 | tf_op jit(solution)/shard_map/requantize_down/pallas_call | solution.py:46
  65.4 13.0 %collective-permute-done.4.refs_15_ = bf16[512,768]{1,0:T(8,128)(2,1)S(1)} collective-permute-done((bf16[512,768]{1,0:T(8,128)(2,1)S(1)}, bf16[512,768]{1,0:T(8,128)(2,1)S(1)}, u32[]{:S(2)}, u32[]{:S(2)}) %collective-permute-start.4) | collective-permute-done | bytes 786464 | tf_op jit(solution)/shard_map/ppermute | solution.py:147
  78.4 0.4 collective-permute-start.6
  78.8 2.2 collective-permute-start.7
  81.1 15.2 %collective-permute-done.6.refs_5_ = bf16[512,768]{1,0:T(8,128)(2,1)S(1)} collective-permute-done((bf16[512,768]{1,0:T(8,128)(2,1)S(1)}, bf16[512,768]{1,0:T(8,128)(2,1)S(1)}, u32[]{:S(2)}, u32[]{:S(2)}) %collective-permute-start.6) | collective-permute-done | bytes 786464 | tf_op jit(solution)/shard_map/ppermute | solution.py:147
  96.3 0.4 collective-permute-start.8
  96.6 2.4 collective-permute-start.9
  99.0 14.2 %collective-permute-done.8.refs_7_ = bf16[512,768]{1,0:T(8,128)(2,1)S(1)} collective-permute-done((bf16[512,768]{1,0:T(8,128)(2,1)S(1)}, bf16[512,768]{1,0:T(8,128)(2,1)S(1)}, u32[]{:S(2)}, u32[]{:S(2)}) %collective-permute-start.8) | collective-permute-done | bytes 786464 | tf_op jit(solution)/shard_map/ppermute | solution.py:147
  113.3 0.1 collective-permute-start.10
  113.4 2.7 collective-permute-start.11
  116.0 9.9 %up_step.3.refs_9_ = f32[512,1536]{1,0:T(8,128)} custom-call(s32[1]{0:T(128)} %bitcast.11.refs_0_, bf16[512,4096]{1,0:T(8,128)(2,1)} %bitcast.10.refs_1_.refs_2_.refs_3_.refs_4_.refs_5_.refs_6_.refs_7_.refs_8_, bf16[512,4096]{1,0:T(8,128)(2,1)} %bitcast.10.refs_1_.refs_2_.refs_3_.refs_4_.refs_5_.refs_6_.refs_7_.refs_8_, ...), custom_call_target="tpu_custom_call" | custom-call | flops 2000000000 | bytes 4000000 | tf_op jit(solution)/shard_map/up_step/pallas_call | solution.py:95
  126.0 3.4 %collective-permute-done.10.refs_5_ = bf16[512,768]{1,0:T(8,128)(2,1)} collective-permute-done((bf16[512,768]{1,0:T(8,128)(2,1)S(1)}, bf16[512,768]{1,0:T(8,128)(2,1)}, u32[]{:S(2)}, u32[]{:S(2)}) %collective-permute-start.10) | collective-permute-done | bytes 786464 | tf_op jit(solution)/shard_map/ppermute | solution.py:147
  129.5 2.7 collective-permute-start.13
  132.1 7.8 %up_step.4.refs_9_ = f32[512,1536]{1,0:T(8,128)} custom-call(s32[1]{0:T(128)} %bitcast.11.refs_0_, bf16[512,4096]{1,0:T(8,128)(2,1)} %bitcast.10.refs_1_.refs_2_.refs_3_.refs_4_.refs_5_.refs_6_.refs_7_.refs_8_, bf16[512,4096]{1,0:T(8,128)(2,1)} %bitcast.10.refs_1_.refs_2_.refs_3_.refs_4_.refs_5_.refs_6_.refs_7_.refs_8_, ...), custom_call_target="tpu_custom_call" | custom-call | flops 2000000000 | bytes 4000000 | tf_op jit(solution)/shard_map/up_step/pallas_call | solution.py:95
  140.0 5.2 %collective-permute-done.12.refs_7_ = bf16[512,768]{1,0:T(8,128)(2,1)S(1)} collective-permute-done((bf16[512,768]{1,0:T(8,128)(2,1)}, bf16[512,768]{1,0:T(8,128)(2,1)S(1)}, u32[]{:S(2)}, u32[]{:S(2)}) %collective-permute-start.12) | collective-permute-done | bytes 786464 | tf_op jit(solution)/shard_map/ppermute | solution.py:147
  145.3 2.8 collective-permute-start.15
  148.1 7.5 %up_step.5.refs_0_ = bf16[512,1536]{1,0:T(8,128)(2,1)} custom-call(s32[1]{0:T(128)} %bitcast.11.refs_0_, bf16[512,4096]{1,0:T(8,128)(2,1)} %bitcast.10.refs_1_.refs_2_.refs_3_.refs_4_.refs_5_.refs_6_.refs_7_.refs_8_, bf16[512,4096]{1,0:T(8,128)(2,1)} %bitcast.10.refs_1_.refs_2_.refs_3_.refs_4_.refs_5_.refs_6_.refs_7_.refs_8_, ...), custom_call_target="tpu_custom_call" | custom-call | flops 2000000000 | bytes 4000000 | tf_op jit(solution)/shard_map/up_step/pallas_call | solution.py:95
  155.6 5.6 %collective-permute-done.14.refs_3_ = bf16[1536,256]{1,0:T(8,128)(2,1)S(1)} collective-permute-done((bf16[1536,256]{1,0:T(8,128)(2,1)S(1)}, bf16[1536,256]{1,0:T(8,128)(2,1)S(1)}, u32[]{:S(2)}, u32[]{:S(2)}) %collective-permute-start.14) | collective-permute-done | bytes 786464 | tf_op jit(solution)/shard_map/ppermute | solution.py:147
  161.3 2.7 collective-permute-start.17
  164.0 5.3 %down_step.5 = bf16[512,1024]{1,0:T(8,128)(2,1)} custom-call(bf16[512,1536]{1,0:T(8,128)(2,1)} %up_step.5.refs_0_, bf16[1536,256]{1,0:T(8,128)(2,1)} %get-tuple-element.70.refs_1_, bf16[1536,256]{1,0:T(8,128)(2,1)} %get-tuple-element.71.refs_2_, bf16[1536,256]{1,0:T(8,128)(2,1)} %copy-done.18, bf16[1536,256]{1,0:T(8,128)(2,1)} %copy-done.19), custom_call_target="tpu_custom_call" | custom-call | flops 2000000000 | bytes 4000000 | tf_op jit(solution)/shard_map/down_step/pallas_call | solution.py:130
  169.3 7.9 %collective-permute-done.16.refs_1_ = bf16[1536,256]{1,0:T(8,128)(2,1)S(1)} collective-permute-done((bf16[1536,256]{1,0:T(8,128)(2,1)S(1)}, bf16[1536,256]{1,0:T(8,128)(2,1)S(1)}, u32[]{:S(2)}, u32[]{:S(2)}) %collective-permute-start.16) | collective-permute-done | bytes 786464 | tf_op jit(solution)/shard_map/ppermute | solution.py:147
  177.2 2.9 collective-permute-start.19
  180.1 18.0 %all-to-all-start.1 = ((bf16[32,16,1024]{2,1,0:T(8,128)(2,1)}), bf16[32,16,1024]{2,1,0:T(8,128)(2,1)S(1)}, u32[]{:S(2)}, u32[]{:S(2)}) async-start(bf16[32,16,1024]{2,1,0:T(8,128)(2,1)} %bitcast.117), calls=%async_computation.1 | async-start | bytes 2097152 | tf_op jit(solution)/shard_map/all_to_all | solution.py:198
  198.2 2.7 collective-permute-start.21
  201.0 0.1 select_reduce_fusion
  201.3 0.1 eq.57
  201.4 0.1 fusion.3
  201.6 5.3 %down_step.6 = bf16[512,1024]{1,0:T(8,128)(2,1)} custom-call(bf16[512,1536]{1,0:T(8,128)(2,1)} %up_step.5.refs_0_, bf16[1536,256]{1,0:T(8,128)(2,1)} %copy-done.13, bf16[1536,256]{1,0:T(8,128)(2,1)} %collective-permute-done.17.refs_2_, bf16[1536,256]{1,0:T(8,128)(2,1)} %collective-permute-done.18.refs_3_, bf16[1536,256]{1,0:T(8,128)(2,1)} %collective-permute-done.19.refs_4_), custom_call_target="tpu_custom_call" | custom-call | flops 2000000000 | bytes 4000000 | tf_op jit(solution)/shard_map/down_step/pallas_call | solution.py:130
  206.8 8.2 %all-to-all-done.1 = bf16[32,16,1024]{2,1,0:T(8,128)(2,1)S(1)} async-done(((bf16[32,16,1024]{2,1,0:T(8,128)(2,1)}), bf16[32,16,1024]{2,1,0:T(8,128)(2,1)S(1)}, u32[]{:S(2)}, u32[]{:S(2)}) %all-to-all-start.1) | async-done | bytes 1048608 | tf_op jit(solution)/shard_map/all_to_all | solution.py:198
  215.0 2.7 collective-permute-start.23
  217.7 0.1 pad_maximum_fusion
  217.8 12.3 %all-to-all-start.2 = ((bf16[32,16,1024]{2,1,0:T(8,128)(2,1)}), bf16[32,16,1024]{2,1,0:T(8,128)(2,1)S(1)}, u32[]{:S(2)}, u32[]{:S(2)}) async-start(bf16[32,16,1024]{2,1,0:T(8,128)(2,1)} %bitcast.118), calls=%async_computation.2 | async-start | bytes 2097152 | tf_op jit(solution)/shard_map/all_to_all | solution.py:198
  230.1 0.3 fusion.33
  230.5 0.4 collective-permute-done.22.refs_3_
  230.9 0.9 copy-done.17
  231.8 2.7 collective-permute-start.25
  234.5 5.3 %down_step.7 = bf16[512,1024]{1,0:T(8,128)(2,1)} custom-call(bf16[512,1536]{1,0:T(8,128)(2,1)} %up_step.5.refs_0_, bf16[1536,256]{1,0:T(8,128)(2,1)} %collective-permute-done.20.refs_1_, bf16[1536,256]{1,0:T(8,128)(2,1)} %collective-permute-done.21.refs_2_, bf16[1536,256]{1,0:T(8,128)(2,1)} %copy-done.17, bf16[1536,256]{1,0:T(8,128)(2,1)} %collective-permute-done.23.refs_4_), custom_call_target="tpu_custom_call" | custom-call | flops 2000000000 | bytes 4000000 | tf_op jit(solution)/shard_map/down_step/pallas_call | solution.py:130
  239.8 7.2 %all-to-all-done.2 = bf16[32,16,1024]{2,1,0:T(8,128)(2,1)S(1)} async-done(((bf16[32,16,1024]{2,1,0:T(8,128)(2,1)}), bf16[32,16,1024]{2,1,0:T(8,128)(2,1)S(1)}, u32[]{:S(2)}, u32[]{:S(2)}) %all-to-all-start.2) | async-done | bytes 1048608 | tf_op jit(solution)/shard_map/all_to_all | solution.py:198
  247.0 6.5 %all-to-all-start.3 = ((bf16[32,16,1024]{2,1,0:T(8,128)(2,1)}), bf16[32,16,1024]{2,1,0:T(8,128)(2,1)S(1)}, u32[]{:S(2)}, u32[]{:S(2)}) async-start(bf16[32,16,1024]{2,1,0:T(8,128)(2,1)} %bitcast.119), calls=%async_computation.3 | async-start | bytes 2097152 | tf_op jit(solution)/shard_map/all_to_all | solution.py:198
  253.6 2.7 collective-permute-start.27
  256.3 0.3 fusion.34
  256.7 3.9 %down_step.8.refs_3_ = bf16[512,1024]{1,0:T(8,128)(2,1)} custom-call(bf16[512,1536]{1,0:T(8,128)(2,1)} %up_step.5.refs_0_, bf16[1536,256]{1,0:T(8,128)(2,1)} %copy-done.16, bf16[1536,256]{1,0:T(8,128)(2,1)} %collective-permute-done.25.refs_2_), custom_call_target="tpu_custom_call" | custom-call | flops 2000000000 | bytes 4000000 | tf_op jit(solution)/shard_map/down_step/pallas_call | solution.py:130
  260.6 9.9 %all-to-all-done.3 = bf16[32,16,1024]{2,1,0:T(8,128)(2,1)S(1)} async-done(((bf16[32,16,1024]{2,1,0:T(8,128)(2,1)}), bf16[32,16,1024]{2,1,0:T(8,128)(2,1)S(1)}, u32[]{:S(2)}, u32[]{:S(2)}) %all-to-all-start.3) | async-done | bytes 1048608 | tf_op jit(solution)/shard_map/all_to_all | solution.py:198
  270.4 0.3 fusion.35
  270.7 3.1 %collective-permute-done.26.refs_1_ = bf16[1536,256]{1,0:T(8,128)(2,1)} collective-permute-done((bf16[1536,256]{1,0:T(8,128)(2,1)S(1)}, bf16[1536,256]{1,0:T(8,128)(2,1)}, u32[]{:S(2)}, u32[]{:S(2)}) %collective-permute-start.26) | collective-permute-done | bytes 786464 | tf_op jit(solution)/shard_map/ppermute | solution.py:147
  273.8 3.8 %down_step.9 = bf16[512,1024]{1,0:T(8,128)(2,1)} custom-call(bf16[512,1536]{1,0:T(8,128)(2,1)} %up_step.5.refs_0_, bf16[1536,256]{1,0:T(8,128)(2,1)} %collective-permute-done.26.refs_1_, bf16[1536,256]{1,0:T(8,128)(2,1)} %collective-permute-done.27.refs_2_, bf16[512,1024]{1,0:T(8,128)(2,1)} %down_step.8.refs_3_), custom_call_target="tpu_custom_call", output_to_operand_aliasing={{}: (3, {})} | custom-call | flops 2000000000 | bytes 4000000 | tf_op jit(solution)/shard_map/down_step/pallas_call | solution.py:130
  277.7 8.1 %all-to-all-start.4 = ((bf16[32,16,1024]{2,1,0:T(8,128)(2,1)}), bf16[32,16,1024]{2,1,0:T(8,128)(2,1)S(1)}, u32[]{:S(2)}, u32[]{:S(2)}) async-start(bf16[32,16,1024]{2,1,0:T(8,128)(2,1)} %bitcast.120), calls=%async_computation.4 | async-start | bytes 2097152 | tf_op jit(solution)/shard_map/all_to_all | solution.py:198
  285.9 16.8 %all-to-all-done.4 = bf16[32,16,1024]{2,1,0:T(8,128)(2,1)S(1)} async-done(((bf16[32,16,1024]{2,1,0:T(8,128)(2,1)}), bf16[32,16,1024]{2,1,0:T(8,128)(2,1)S(1)}, u32[]{:S(2)}, u32[]{:S(2)}) %all-to-all-start.4) | async-done | bytes 1048608 | tf_op jit(solution)/shard_map/all_to_all | solution.py:198
  302.7 0.3 fusion.36
  303.1 0.7 copy-done.11
  303.8 0.6 fusion.9
  (94 shorter events, 1.2 us)
Async XLA Ops:
  0.0 1.3 copy-start
  4.5 108.8 %all-to-all-start = ((bf16[32,16,4096]{2,1,0:T(8,128)(2,1)}), bf16[32,16,4096]{2,1,0:T(8,128)(2,1)}, u32[]{:S(2)}, u32[]{:S(2)}) async-start(bf16[32,16,4096]{2,1,0:T(8,128)(2,1)} %bitcast.112), calls=%async_computation | async-start | bytes 8388608 | tf_op jit(solution)/shard_map/all_to_all | solution.py:189
  16.2 23.6 %collective-permute-start = (bf16[512,768]{1,0:T(8,128)(2,1)}, bf16[512,768]{1,0:T(8,128)(2,1)S(1)}, u32[]{:S(2)}, u32[]{:S(2)}) collective-permute-start(bf16[512,768]{1,0:T(8,128)(2,1)} %get-tuple-element.50.refs_9_), channel_id=1, source_target_pairs={{0,32},{32,64},{64,96},{96,128},{128,160},{160,192},{192,224},{224... | collective-permute-start | bytes 2359304 | tf_op jit(solution)/shard_map/ppermute | solution.py:147
  17.8 21.9 %collective-permute-start.1 = (bf16[512,768]{1,0:T(8,128)(2,1)}, bf16[512,768]{1,0:T(8,128)(2,1)S(1)}, u32[]{:S(2)}, u32[]{:S(2)}) collective-permute-start(bf16[512,768]{1,0:T(8,128)(2,1)} %get-tuple-element.51.refs_10_), channel_id=1, source_target_pairs={{0,224},{32,0},{64,32},{96,64},{128,96},{160,128},{192,160},{224,1... | collective-permute-start | bytes 2359304 | tf_op jit(solution)/shard_map/ppermute | solution.py:147
  39.8 19.8 %copy-start.5 = (bf16[512,768]{1,0:T(8,128)(2,1)}, bf16[512,768]{1,0:T(8,128)(2,1)S(1)}, u32[]{:S(2)}) copy-start(bf16[512,768]{1,0:T(8,128)(2,1)S(1)} %collective-permute-done.refs_11_) | copy-start | bytes 2359300
  39.8 19.8 %copy-start.6 = (bf16[512,768]{1,0:T(8,128)(2,1)}, bf16[512,768]{1,0:T(8,128)(2,1)S(1)}, u32[]{:S(2)}) copy-start(bf16[512,768]{1,0:T(8,128)(2,1)S(1)} %collective-permute-done.1.refs_12_) | copy-start | bytes 2359300
  39.8 19.8 %collective-permute-start.2 = (bf16[512,768]{1,0:T(8,128)(2,1)S(1)}, bf16[512,768]{1,0:T(8,128)(2,1)S(1)}, u32[]{:S(2)}, u32[]{:S(2)}) collective-permute-start(bf16[512,768]{1,0:T(8,128)(2,1)S(1)} %collective-permute-done.refs_11_), channel_id=1, source_target_pairs={{0,32},{32,64},{64,96},{96,128},{128,160},{160,192},{192,224},{224... | collective-permute-start | bytes 2359304 | tf_op jit(solution)/shard_map/ppermute | solution.py:147
  39.9 19.7 %collective-permute-start.3 = (bf16[512,768]{1,0:T(8,128)(2,1)S(1)}, bf16[512,768]{1,0:T(8,128)(2,1)S(1)}, u32[]{:S(2)}, u32[]{:S(2)}) collective-permute-start(bf16[512,768]{1,0:T(8,128)(2,1)S(1)} %collective-permute-done.1.refs_12_), channel_id=1, source_target_pairs={{0,224},{32,0},{64,32},{96,64},{128,96},{160,128},{192,160},{224,1... | collective-permute-start | bytes 2359304 | tf_op jit(solution)/shard_map/ppermute | solution.py:147
  59.5 2.8 copy-start.1
  59.6 5.8 %copy-start.7 = (bf16[512,768]{1,0:T(8,128)(2,1)}, bf16[512,768]{1,0:T(8,128)(2,1)S(1)}, u32[]{:S(2)}) copy-start(bf16[512,768]{1,0:T(8,128)(2,1)S(1)} %collective-permute-done.3.refs_14_) | copy-start | bytes 2359300
  59.6 18.8 %collective-permute-start.4 = (bf16[512,768]{1,0:T(8,128)(2,1)S(1)}, bf16[512,768]{1,0:T(8,128)(2,1)S(1)}, u32[]{:S(2)}, u32[]{:S(2)}) collective-permute-start(bf16[512,768]{1,0:T(8,128)(2,1)S(1)} %collective-permute-done.2.refs_4_.refs_13_), channel_id=1, source_target_pairs={{0,32},{32,64},{64,96},{96,128},{128,160},{160,192},{192,224},{224... | collective-permute-start | bytes 2359304 | tf_op jit(solution)/shard_map/ppermute | solution.py:147
  60.3 18.1 %collective-permute-start.5 = (bf16[512,768]{1,0:T(8,128)(2,1)S(1)}, bf16[512,768]{1,0:T(8,128)(2,1)}, u32[]{:S(2)}, u32[]{:S(2)}) collective-permute-start(bf16[512,768]{1,0:T(8,128)(2,1)S(1)} %collective-permute-done.3.refs_14_), channel_id=1, source_target_pairs={{0,224},{32,0},{64,32},{96,64},{128,96},{160,128},{192,160},{224,1... | collective-permute-start | bytes 2359304 | tf_op jit(solution)/shard_map/ppermute | solution.py:147
  78.4 17.8 %copy-start.8 = (bf16[512,768]{1,0:T(8,128)(2,1)}, bf16[512,768]{1,0:T(8,128)(2,1)S(1)}, u32[]{:S(2)}) copy-start(bf16[512,768]{1,0:T(8,128)(2,1)S(1)} %collective-permute-done.4.refs_15_) | copy-start | bytes 2359300
  78.4 17.8 %collective-permute-start.6 = (bf16[512,768]{1,0:T(8,128)(2,1)S(1)}, bf16[512,768]{1,0:T(8,128)(2,1)S(1)}, u32[]{:S(2)}, u32[]{:S(2)}) collective-permute-start(bf16[512,768]{1,0:T(8,128)(2,1)S(1)} %collective-permute-done.4.refs_15_), channel_id=1, source_target_pairs={{0,32},{32,64},{64,96},{96,128},{128,160},{160,192},{192,224},{224... | collective-permute-start | bytes 2359304 | tf_op jit(solution)/shard_map/ppermute | solution.py:147
  78.8 17.4 %collective-permute-start.7 = (bf16[512,768]{1,0:T(8,128)(2,1)}, bf16[512,768]{1,0:T(8,128)(2,1)S(1)}, u32[]{:S(2)}, u32[]{:S(2)}) collective-permute-start(bf16[512,768]{1,0:T(8,128)(2,1)} %collective-permute-done.5.refs_16_), channel_id=1, source_target_pairs={{0,224},{32,0},{64,32},{96,64},{128,96},{160,128},{192,160},{224,1... | collective-permute-start | bytes 2359304 | tf_op jit(solution)/shard_map/ppermute | solution.py:147
  96.2 29.7 %copy-start.2 = (bf16[512,768]{1,0:T(8,128)(2,1)}, bf16[512,768]{1,0:T(8,128)(2,1)S(1)}, u32[]{:S(2)}) copy-start(bf16[512,768]{1,0:T(8,128)(2,1)S(1)} %collective-permute-done.6.refs_5_) | copy-start | bytes 2359300
  96.3 29.7 %copy-start.3 = (bf16[512,768]{1,0:T(8,128)(2,1)}, bf16[512,768]{1,0:T(8,128)(2,1)S(1)}, u32[]{:S(2)}) copy-start(bf16[512,768]{1,0:T(8,128)(2,1)S(1)} %collective-permute-done.7.refs_6_) | copy-start | bytes 2359300
  96.3 17.0 %collective-permute-start.8 = (bf16[512,768]{1,0:T(8,128)(2,1)S(1)}, bf16[512,768]{1,0:T(8,128)(2,1)S(1)}, u32[]{:S(2)}, u32[]{:S(2)}) collective-permute-start(bf16[512,768]{1,0:T(8,128)(2,1)S(1)} %collective-permute-done.6.refs_5_), channel_id=1, source_target_pairs={{0,32},{32,64},{64,96},{96,128},{128,160},{160,192},{192,224},{224... | collective-permute-start | bytes 2359304 | tf_op jit(solution)/shard_map/ppermute | solution.py:147
  96.6 16.6 %collective-permute-start.9 = (bf16[512,768]{1,0:T(8,128)(2,1)S(1)}, bf16[512,768]{1,0:T(8,128)(2,1)}, u32[]{:S(2)}, u32[]{:S(2)}) collective-permute-start(bf16[512,768]{1,0:T(8,128)(2,1)S(1)} %collective-permute-done.7.refs_6_), channel_id=1, source_target_pairs={{0,224},{32,0},{64,32},{96,64},{128,96},{160,128},{192,160},{224,1... | collective-permute-start | bytes 2359304 | tf_op jit(solution)/shard_map/ppermute | solution.py:147
  113.3 12.7 %copy-start.4 = (bf16[512,768]{1,0:T(8,128)(2,1)}, bf16[512,768]{1,0:T(8,128)(2,1)S(1)}, u32[]{:S(2)}) copy-start(bf16[512,768]{1,0:T(8,128)(2,1)S(1)} %collective-permute-done.8.refs_7_) | copy-start | bytes 2359300
  113.3 16.2 %collective-permute-start.10 = (bf16[512,768]{1,0:T(8,128)(2,1)S(1)}, bf16[512,768]{1,0:T(8,128)(2,1)}, u32[]{:S(2)}, u32[]{:S(2)}) collective-permute-start(bf16[512,768]{1,0:T(8,128)(2,1)S(1)} %collective-permute-done.8.refs_7_), channel_id=1, source_target_pairs={{0,32},{32,64},{64,96},{96,128},{128,160},{160,192},{192,224},{224... | collective-permute-start | bytes 2359304 | tf_op jit(solution)/shard_map/ppermute | solution.py:147
  113.4 16.1 %collective-permute-start.11 = (bf16[512,768]{1,0:T(8,128)(2,1)}, bf16[512,768]{1,0:T(8,128)(2,1)}, u32[]{:S(2)}, u32[]{:S(2)}) collective-permute-start(bf16[512,768]{1,0:T(8,128)(2,1)} %collective-permute-done.9.refs_8_), channel_id=1, source_target_pairs={{0,224},{32,0},{64,32},{96,64},{128,96},{160,128},{192,160},{224,1... | collective-permute-start | bytes 2359304 | tf_op jit(solution)/shard_map/ppermute | solution.py:147
  126.0 19.2 %copy-start.14 = (bf16[1536,256]{1,0:T(8,128)(2,1)S(1)}, bf16[1536,256]{1,0:T(8,128)(2,1)}, u32[]{:S(2)}) copy-start(bf16[1536,256]{1,0:T(8,128)(2,1)} %get-tuple-element.70.refs_1_) | copy-start | bytes 2359300
  126.0 19.3 %copy-start.15 = (bf16[1536,256]{1,0:T(8,128)(2,1)S(1)}, bf16[1536,256]{1,0:T(8,128)(2,1)}, u32[]{:S(2)}) copy-start(bf16[1536,256]{1,0:T(8,128)(2,1)} %get-tuple-element.71.refs_2_) | copy-start | bytes 2359300
  129.5 15.8 %collective-permute-start.12 = (bf16[512,768]{1,0:T(8,128)(2,1)}, bf16[512,768]{1,0:T(8,128)(2,1)S(1)}, u32[]{:S(2)}, u32[]{:S(2)}) collective-permute-start(bf16[512,768]{1,0:T(8,128)(2,1)} %collective-permute-done.10.refs_5_), channel_id=1, source_target_pairs={{0,32},{32,64},{64,96},{96,128},{128,160},{160,192},{192,224},{224... | collective-permute-start | bytes 2359304 | tf_op jit(solution)/shard_map/ppermute | solution.py:147
  129.5 15.8 %collective-permute-start.13 = (bf16[512,768]{1,0:T(8,128)(2,1)}, bf16[512,768]{1,0:T(8,128)(2,1)S(1)}, u32[]{:S(2)}, u32[]{:S(2)}) collective-permute-start(bf16[512,768]{1,0:T(8,128)(2,1)} %collective-permute-done.11.refs_6_), channel_id=1, source_target_pairs={{0,224},{32,0},{64,32},{96,64},{128,96},{160,128},{192,160},{224,1... | collective-permute-start | bytes 2359304 | tf_op jit(solution)/shard_map/ppermute | solution.py:147
  145.2 2.9 copy-start.9
  145.2 2.9 copy-start.10
  145.2 16.0 %collective-permute-start.14 = (bf16[1536,256]{1,0:T(8,128)(2,1)S(1)}, bf16[1536,256]{1,0:T(8,128)(2,1)S(1)}, u32[]{:S(2)}, u32[]{:S(2)}) collective-permute-start(bf16[1536,256]{1,0:T(8,128)(2,1)S(1)} %copy-done.14), channel_id=1, source_target_pairs={{0,32},{32,64},{64,96},{96,128},{128,160},{160,192},{192,224},{224... | collective-permute-start | bytes 2359304 | tf_op jit(solution)/shard_map/ppermute | solution.py:147
  145.3 15.9 %collective-permute-start.15 = (bf16[1536,256]{1,0:T(8,128)(2,1)S(1)}, bf16[1536,256]{1,0:T(8,128)(2,1)S(1)}, u32[]{:S(2)}, u32[]{:S(2)}) collective-permute-start(bf16[1536,256]{1,0:T(8,128)(2,1)S(1)} %copy-done.15), channel_id=1, source_target_pairs={{0,224},{32,0},{64,32},{96,64},{128,96},{160,128},{192,160},{224,1... | collective-permute-start | bytes 2359304 | tf_op jit(solution)/shard_map/ppermute | solution.py:147
  155.6 45.2 %copy-start.12 = (f32[1,1,32,8]{2,3,1,0:T(8,128)S(1)}, f32[1,1,32,8]{2,3,1,0:T(8,128)}, u32[]{:S(2)}) copy-start(f32[1,1,32,8]{2,3,1,0:T(8,128)} %param.6) | copy-start | bytes 3076
  161.2 2.8 copy-start.18
  161.3 2.8 copy-start.19
  161.3 15.9 %collective-permute-start.16 = (bf16[1536,256]{1,0:T(8,128)(2,1)S(1)}, bf16[1536,256]{1,0:T(8,128)(2,1)S(1)}, u32[]{:S(2)}, u32[]{:S(2)}) collective-permute-start(bf16[1536,256]{1,0:T(8,128)(2,1)S(1)} %collective-permute-done.14.refs_3_), channel_id=1, source_target_pairs={{0,32},{32,64},{64,96},{96,128},{128,160},{160,192},{192,224},{224... | collective-permute-start | bytes 2359304 | tf_op jit(solution)/shard_map/ppermute | solution.py:147
  161.3 15.9 %collective-permute-start.17 = (bf16[1536,256]{1,0:T(8,128)(2,1)S(1)}, bf16[1536,256]{1,0:T(8,128)(2,1)}, u32[]{:S(2)}, u32[]{:S(2)}) collective-permute-start(bf16[1536,256]{1,0:T(8,128)(2,1)S(1)} %collective-permute-done.15.refs_4_), channel_id=1, source_target_pairs={{0,224},{32,0},{64,32},{96,64},{128,96},{160,128},{192,160},{224,1... | collective-permute-start | bytes 2359304 | tf_op jit(solution)/shard_map/ppermute | solution.py:147
  177.2 24.4 %copy-start.13 = (bf16[1536,256]{1,0:T(8,128)(2,1)}, bf16[1536,256]{1,0:T(8,128)(2,1)S(1)}, u32[]{:S(2)}) copy-start(bf16[1536,256]{1,0:T(8,128)(2,1)S(1)} %collective-permute-done.16.refs_1_) | copy-start | bytes 2359300
  177.2 20.9 %collective-permute-start.18 = (bf16[1536,256]{1,0:T(8,128)(2,1)S(1)}, bf16[1536,256]{1,0:T(8,128)(2,1)}, u32[]{:S(2)}, u32[]{:S(2)}) collective-permute-start(bf16[1536,256]{1,0:T(8,128)(2,1)S(1)} %collective-permute-done.16.refs_1_), channel_id=1, source_target_pairs={{0,32},{32,64},{64,96},{96,128},{128,160},{160,192},{192,224},{224... | collective-permute-start | bytes 2359304 | tf_op jit(solution)/shard_map/ppermute | solution.py:147
  177.2 20.9 %collective-permute-start.19 = (bf16[1536,256]{1,0:T(8,128)(2,1)}, bf16[1536,256]{1,0:T(8,128)(2,1)}, u32[]{:S(2)}, u32[]{:S(2)}) collective-permute-start(bf16[1536,256]{1,0:T(8,128)(2,1)} %collective-permute-done.17.refs_2_), channel_id=1, source_target_pairs={{0,224},{32,0},{64,32},{96,64},{128,96},{160,128},{192,160},{224,1... | collective-permute-start | bytes 2359304 | tf_op jit(solution)/shard_map/ppermute | solution.py:147
  180.1 34.9 %all-to-all-start.1 = ((bf16[32,16,1024]{2,1,0:T(8,128)(2,1)}), bf16[32,16,1024]{2,1,0:T(8,128)(2,1)S(1)}, u32[]{:S(2)}, u32[]{:S(2)}) async-start(bf16[32,16,1024]{2,1,0:T(8,128)(2,1)} %bitcast.117), calls=%async_computation.1 | async-start | bytes 2097152 | tf_op jit(solution)/shard_map/all_to_all | solution.py:198
  198.1 16.9 %collective-permute-start.20 = (bf16[1536,256]{1,0:T(8,128)(2,1)}, bf16[1536,256]{1,0:T(8,128)(2,1)}, u32[]{:S(2)}, u32[]{:S(2)}) collective-permute-start(bf16[1536,256]{1,0:T(8,128)(2,1)} %collective-permute-done.18.refs_3_), channel_id=1, source_target_pairs={{0,32},{32,64},{64,96},{96,128},{128,160},{160,192},{192,224},{224... | collective-permute-start | bytes 2359304 | tf_op jit(solution)/shard_map/ppermute | solution.py:147
  198.2 16.8 %collective-permute-start.21 = (bf16[1536,256]{1,0:T(8,128)(2,1)}, bf16[1536,256]{1,0:T(8,128)(2,1)}, u32[]{:S(2)}, u32[]{:S(2)}) collective-permute-start(bf16[1536,256]{1,0:T(8,128)(2,1)} %collective-permute-done.19.refs_4_), channel_id=1, source_target_pairs={{0,224},{32,0},{64,32},{96,64},{128,96},{160,128},{192,160},{224,1... | collective-permute-start | bytes 2359304 | tf_op jit(solution)/shard_map/ppermute | solution.py:147
  215.0 15.9 %collective-permute-start.22 = (bf16[1536,256]{1,0:T(8,128)(2,1)}, bf16[1536,256]{1,0:T(8,128)(2,1)S(1)}, u32[]{:S(2)}, u32[]{:S(2)}) collective-permute-start(bf16[1536,256]{1,0:T(8,128)(2,1)} %collective-permute-done.20.refs_1_), channel_id=1, source_target_pairs={{0,32},{32,64},{64,96},{96,128},{128,160},{160,192},{192,224},{224... | collective-permute-start | bytes 2359304 | tf_op jit(solution)/shard_map/ppermute | solution.py:147
  215.0 16.8 %collective-permute-start.23 = (bf16[1536,256]{1,0:T(8,128)(2,1)}, bf16[1536,256]{1,0:T(8,128)(2,1)}, u32[]{:S(2)}, u32[]{:S(2)}) collective-permute-start(bf16[1536,256]{1,0:T(8,128)(2,1)} %collective-permute-done.21.refs_2_), channel_id=1, source_target_pairs={{0,224},{32,0},{64,32},{96,64},{128,96},{160,128},{192,160},{224,1... | collective-permute-start | bytes 2359304 | tf_op jit(solution)/shard_map/ppermute | solution.py:147
  217.8 29.2 %all-to-all-start.2 = ((bf16[32,16,1024]{2,1,0:T(8,128)(2,1)}), bf16[32,16,1024]{2,1,0:T(8,128)(2,1)S(1)}, u32[]{:S(2)}, u32[]{:S(2)}) async-start(bf16[32,16,1024]{2,1,0:T(8,128)(2,1)} %bitcast.118), calls=%async_computation.2 | async-start | bytes 2097152 | tf_op jit(solution)/shard_map/all_to_all | solution.py:198
  230.9 0.9 copy-start.17
  231.8 21.7 %collective-permute-start.24 = (bf16[1536,256]{1,0:T(8,128)(2,1)}, bf16[1536,256]{1,0:T(8,128)(2,1)S(1)}, u32[]{:S(2)}, u32[]{:S(2)}) collective-permute-start(bf16[1536,256]{1,0:T(8,128)(2,1)} %copy-done.17), channel_id=1, source_target_pairs={{0,32},{32,64},{64,96},{96,128},{128,160},{160,192},{192,224},{224... | collective-permute-start | bytes 2359304 | tf_op jit(solution)/shard_map/ppermute | solution.py:147
  231.8 21.7 %collective-permute-start.25 = (bf16[1536,256]{1,0:T(8,128)(2,1)}, bf16[1536,256]{1,0:T(8,128)(2,1)}, u32[]{:S(2)}, u32[]{:S(2)}) collective-permute-start(bf16[1536,256]{1,0:T(8,128)(2,1)} %collective-permute-done.23.refs_4_), channel_id=1, source_target_pairs={{0,224},{32,0},{64,32},{96,64},{128,96},{160,128},{192,160},{224,1... | collective-permute-start | bytes 2359304 | tf_op jit(solution)/shard_map/ppermute | solution.py:147
  247.0 23.4 %all-to-all-start.3 = ((bf16[32,16,1024]{2,1,0:T(8,128)(2,1)}), bf16[32,16,1024]{2,1,0:T(8,128)(2,1)S(1)}, u32[]{:S(2)}, u32[]{:S(2)}) async-start(bf16[32,16,1024]{2,1,0:T(8,128)(2,1)} %bitcast.119), calls=%async_computation.3 | async-start | bytes 2097152 | tf_op jit(solution)/shard_map/all_to_all | solution.py:198
  253.5 3.2 %copy-start.16 = (bf16[1536,256]{1,0:T(8,128)(2,1)}, bf16[1536,256]{1,0:T(8,128)(2,1)S(1)}, u32[]{:S(2)}) copy-start(bf16[1536,256]{1,0:T(8,128)(2,1)S(1)} %collective-permute-done.24.refs_1_) | copy-start | bytes 2359300
  253.5 20.3 %collective-permute-start.26 = (bf16[1536,256]{1,0:T(8,128)(2,1)S(1)}, bf16[1536,256]{1,0:T(8,128)(2,1)}, u32[]{:S(2)}, u32[]{:S(2)}) collective-permute-start(bf16[1536,256]{1,0:T(8,128)(2,1)S(1)} %collective-permute-done.24.refs_1_), channel_id=1, source_target_pairs={{0,32},{32,64},{64,96},{96,128},{128,160},{160,192},{192,224},{224... | collective-permute-start | bytes 2359304 | tf_op jit(solution)/shard_map/ppermute | solution.py:147
  253.6 20.2 %collective-permute-start.27 = (bf16[1536,256]{1,0:T(8,128)(2,1)}, bf16[1536,256]{1,0:T(8,128)(2,1)}, u32[]{:S(2)}, u32[]{:S(2)}) collective-permute-start(bf16[1536,256]{1,0:T(8,128)(2,1)} %collective-permute-done.25.refs_2_), channel_id=1, source_target_pairs={{0,224},{32,0},{64,32},{96,64},{128,96},{160,128},{192,160},{224,1... | collective-permute-start | bytes 2359304 | tf_op jit(solution)/shard_map/ppermute | solution.py:147
  277.7 25.0 %all-to-all-start.4 = ((bf16[32,16,1024]{2,1,0:T(8,128)(2,1)}), bf16[32,16,1024]{2,1,0:T(8,128)(2,1)S(1)}, u32[]{:S(2)}, u32[]{:S(2)}) async-start(bf16[32,16,1024]{2,1,0:T(8,128)(2,1)} %bitcast.120), calls=%async_computation.4 | async-start | bytes 2097152 | tf_op jit(solution)/shard_map/all_to_all | solution.py:198
  303.1 0.7 copy-start.11

commit v6 on v5

--- a/solution.py
+++ b/solution.py
@@ -111,9 +111,11 @@
     out_ref = refs[-1]
     part = refs[0].shape[1]
 
-    @pl.loop(0, hidden_ref.shape[0] // TILE)
+    height = TILE if count > 2 else hidden_ref.shape[0]
+
+    @pl.loop(0, hidden_ref.shape[0] // height)
     def _(tile):
-        rows = pl.ds(pl.multiple_of(tile * TILE, TILE), TILE)
+        rows = pl.ds(pl.multiple_of(tile * height, height), height)
         for index in range(count):
             out_ref[rows, index * part:(index + 1) * part] = jnp.dot(
                 hidden_ref[rows, :], refs[index][...], preferred_element_type=jnp.float32

time: 305 us -> 305 us (level)
  no operation moved by 1% of the time
where the time goes in v6:
time: 305 us; the launch traced here: 304 us
  waiting for transfers between devices  145 us (48%)
  starting transfers between devices  94.8 us (31%)
  Pallas kernels  54.6 us (18%)
  matrix products  4.61 us (2%)
  local copies, waits for them, and re-layouts  3.73 us (1%)
    ppermute x28, waiting for transfers between devices, shift(): lax.ppermute(part, 'grp', way)  103 us
    all_to_all x4, starting transfers between devices, send_back(): lax.all_to_all(answer.reshape(ep_count, CAP, part), 'ep', split_axis=0, c...  44.8 us
    all_to_all x4, waiting for transfers between devices, send_back(): lax.all_to_all(answer.reshape(ep_count, CAP, part), 'ep', split_axis=0, c...  42.2 us
    ppermute x28, starting transfers between devices, shift(): lax.ppermute(part, 'grp', way)  41.4 us
    pallas_call x3, Pallas kernels, up_step(): pl.pallas_call(lambda *refs: up_kernel(steps, size, *refs), grid_spec=plt...  25.3 us
    pallas_call x5, Pallas kernels, down_step(): pl.pallas_call(lambda *refs: down_kernel(len(parts), *refs), grid=(1,), i...  23.2 us
    all_to_all x1, starting transfers between devices, local(): lax.all_to_all(send, 'ep', split_axis=0, concat_axis=0, tiled=True)  8.64 us
  transfers between devices with their start and end apart: 33, of which 15 were waited for; matrix products, arithmetic and copies ran while one was open for 1% of the time, Pallas kernels for 17%

profile of v6, /device:TPU:1, one launch (start us, length us, event | category | flops | bytes accessed | tf_op | source)
XLA Modules:
  0.0 304.2 jit_solution(1997519238031706942)
XLA Ops:
  0.0 0.8 fusion.28
  0.9 0.1 fusion.8
  1.0 0.2 fusion
  1.3 3.2 %convolution_convert_fusion = bf16[512,4096]{1,0:T(8,128)(2,1)} fusion(pred[32,512]{0,1:T(8,128)(4,1)S(1)} %bitcast.121, bf16[1,1,32,4096]{3,2,1,0:T(8,128)(2,1)S(1)} %copy-done), kind=kOutput, calls=%fused_computation | convolution fusion | flops 136314880 | bytes 4472832 | tf_op jit(solution)/shard_map/dot_general | solution.py:188
  4.5 8.6 %all-to-all-start = ((bf16[32,16,4096]{2,1,0:T(8,128)(2,1)}), bf16[32,16,4096]{2,1,0:T(8,128)(2,1)}, u32[]{:S(2)}, u32[]{:S(2)}) async-start(bf16[32,16,4096]{2,1,0:T(8,128)(2,1)} %bitcast.112), calls=%async_computation | async-start | bytes 8388608 | tf_op jit(solution)/shard_map/all_to_all | solution.py:191
  13.2 3.0 %requantize_up.1 = (bf16[512,768]{1,0:T(8,128)(2,1)}, bf16[512,768]{1,0:T(8,128)(2,1)}) custom-call(f32[512,1536]{1,0:T(8,128)} %bitcast.104, f32[512,1536]{1,0:T(8,128)} %bitcast.105, f32[512,1536]{1,0:T(8,128)} %bitcast.106, f32[512,1536]{1,0:T(8,128)} %bitcast.107), custom_call_target="tpu_custom_call" | custom-call | flops 2000000000 | bytes 4000000 | tf_op jit(solution)/shard_map/requantize_up/pallas_call | solution.py:46
  16.2 1.6 collective-permute-start
  17.8 4.0 %collective-permute-start.1 = (bf16[512,768]{1,0:T(8,128)(2,1)}, bf16[512,768]{1,0:T(8,128)(2,1)S(1)}, u32[]{:S(2)}, u32[]{:S(2)}) collective-permute-start(bf16[512,768]{1,0:T(8,128)(2,1)} %get-tuple-element.51.refs_10_), channel_id=1, source_target_pairs={{0,224},{32,0},{64,32},{96,64},{128,96},{160,128},{192,160},{224,1... | collective-permute-start | bytes 2359304 | tf_op jit(solution)/shard_map/ppermute | solution.py:149
  21.9 17.9 %collective-permute-done.refs_11_ = bf16[512,768]{1,0:T(8,128)(2,1)S(1)} collective-permute-done((bf16[512,768]{1,0:T(8,128)(2,1)}, bf16[512,768]{1,0:T(8,128)(2,1)S(1)}, u32[]{:S(2)}, u32[]{:S(2)}) %collective-permute-start) | collective-permute-done | bytes 786464 | tf_op jit(solution)/shard_map/ppermute | solution.py:149
  39.9 2.7 collective-permute-start.3
  42.5 17.0 %collective-permute-done.2.refs_4_.refs_13_ = bf16[512,768]{1,0:T(8,128)(2,1)S(1)} collective-permute-done((bf16[512,768]{1,0:T(8,128)(2,1)S(1)}, bf16[512,768]{1,0:T(8,128)(2,1)S(1)}, u32[]{:S(2)}, u32[]{:S(2)}) %collective-permute-start.2) | collective-permute-done | bytes 786464 | tf_op jit(solution)/shard_map/ppermute | solution.py:149
  59.6 0.8 collective-permute-start.4
  60.3 2.0 collective-permute-start.5
  62.3 3.1 %requantize_down.1 = (bf16[1536,256]{1,0:T(8,128)(2,1)}, bf16[1536,256]{1,0:T(8,128)(2,1)}) custom-call(f32[1536,512]{1,0:T(8,128)} %bitcast.108, f32[1536,512]{1,0:T(8,128)} %bitcast.109, f32[1536,512]{1,0:T(8,128)} %bitcast.110, f32[1536,512]{1,0:T(8,128)} %bitcast.111, bf16[512,768]{1,0:T(8,128)(2,1)} %copy-done.1), custom_call_target="tpu_custom_call" | custom-call | flops 2000000000 | bytes 4000000 | tf_op jit(solution)/shard_map/requantize_down/pallas_call | solution.py:46
  65.4 13.0 %collective-permute-done.4.refs_15_ = bf16[512,768]{1,0:T(8,128)(2,1)S(1)} collective-permute-done((bf16[512,768]{1,0:T(8,128)(2,1)S(1)}, bf16[512,768]{1,0:T(8,128)(2,1)S(1)}, u32[]{:S(2)}, u32[]{:S(2)}) %collective-permute-start.4) | collective-permute-done | bytes 786464 | tf_op jit(solution)/shard_map/ppermute | solution.py:149
  78.4 0.4 collective-permute-start.6
  78.8 2.2 collective-permute-start.7
  81.1 15.2 %collective-permute-done.6.refs_5_ = bf16[512,768]{1,0:T(8,128)(2,1)S(1)} collective-permute-done((bf16[512,768]{1,0:T(8,128)(2,1)S(1)}, bf16[512,768]{1,0:T(8,128)(2,1)S(1)}, u32[]{:S(2)}, u32[]{:S(2)}) %collective-permute-start.6) | collective-permute-done | bytes 786464 | tf_op jit(solution)/shard_map/ppermute | solution.py:149
  96.3 0.4 collective-permute-start.8
  96.6 2.4 collective-permute-start.9
  99.0 14.2 %collective-permute-done.8.refs_7_ = bf16[512,768]{1,0:T(8,128)(2,1)S(1)} collective-permute-done((bf16[512,768]{1,0:T(8,128)(2,1)S(1)}, bf16[512,768]{1,0:T(8,128)(2,1)S(1)}, u32[]{:S(2)}, u32[]{:S(2)}) %collective-permute-start.8) | collective-permute-done | bytes 786464 | tf_op jit(solution)/shard_map/ppermute | solution.py:149
  113.3 0.1 collective-permute-start.10
  113.4 2.7 collective-permute-start.11
  116.0 9.9 %up_step.3.refs_9_ = f32[512,1536]{1,0:T(8,128)} custom-call(s32[1]{0:T(128)} %bitcast.11.refs_0_, bf16[512,4096]{1,0:T(8,128)(2,1)} %bitcast.10.refs_1_.refs_2_.refs_3_.refs_4_.refs_5_.refs_6_.refs_7_.refs_8_, bf16[512,4096]{1,0:T(8,128)(2,1)} %bitcast.10.refs_1_.refs_2_.refs_3_.refs_4_.refs_5_.refs_6_.refs_7_.refs_8_, ...), custom_call_target="tpu_custom_call" | custom-call | flops 2000000000 | bytes 4000000 | tf_op jit(solution)/shard_map/up_step/pallas_call | solution.py:95
  126.0 3.4 %collective-permute-done.10.refs_5_ = bf16[512,768]{1,0:T(8,128)(2,1)} collective-permute-done((bf16[512,768]{1,0:T(8,128)(2,1)S(1)}, bf16[512,768]{1,0:T(8,128)(2,1)}, u32[]{:S(2)}, u32[]{:S(2)}) %collective-permute-start.10) | collective-permute-done | bytes 786464 | tf_op jit(solution)/shard_map/ppermute | solution.py:149
  129.5 2.7 collective-permute-start.13
  132.1 7.8 %up_step.4.refs_9_ = f32[512,1536]{1,0:T(8,128)} custom-call(s32[1]{0:T(128)} %bitcast.11.refs_0_, bf16[512,4096]{1,0:T(8,128)(2,1)} %bitcast.10.refs_1_.refs_2_.refs_3_.refs_4_.refs_5_.refs_6_.refs_7_.refs_8_, bf16[512,4096]{1,0:T(8,128)(2,1)} %bitcast.10.refs_1_.refs_2_.refs_3_.refs_4_.refs_5_.refs_6_.refs_7_.refs_8_, ...), custom_call_target="tpu_custom_call" | custom-call | flops 2000000000 | bytes 4000000 | tf_op jit(solution)/shard_map/up_step/pallas_call | solution.py:95
  140.0 5.2 %collective-permute-done.12.refs_7_ = bf16[512,768]{1,0:T(8,128)(2,1)S(1)} collective-permute-done((bf16[512,768]{1,0:T(8,128)(2,1)}, bf16[512,768]{1,0:T(8,128)(2,1)S(1)}, u32[]{:S(2)}, u32[]{:S(2)}) %collective-permute-start.12) | collective-permute-done | bytes 786464 | tf_op jit(solution)/shard_map/ppermute | solution.py:149
  145.3 2.8 collective-permute-start.15
  148.1 7.5 %up_step.5.refs_0_ = bf16[512,1536]{1,0:T(8,128)(2,1)} custom-call(s32[1]{0:T(128)} %bitcast.11.refs_0_, bf16[512,4096]{1,0:T(8,128)(2,1)} %bitcast.10.refs_1_.refs_2_.refs_3_.refs_4_.refs_5_.refs_6_.refs_7_.refs_8_, bf16[512,4096]{1,0:T(8,128)(2,1)} %bitcast.10.refs_1_.refs_2_.refs_3_.refs_4_.refs_5_.refs_6_.refs_7_.refs_8_, ...), custom_call_target="tpu_custom_call" | custom-call | flops 2000000000 | bytes 4000000 | tf_op jit(solution)/shard_map/up_step/pallas_call | solution.py:95
  155.6 5.6 %collective-permute-done.14.refs_3_ = bf16[1536,256]{1,0:T(8,128)(2,1)S(1)} collective-permute-done((bf16[1536,256]{1,0:T(8,128)(2,1)S(1)}, bf16[1536,256]{1,0:T(8,128)(2,1)S(1)}, u32[]{:S(2)}, u32[]{:S(2)}) %collective-permute-start.14) | collective-permute-done | bytes 786464 | tf_op jit(solution)/shard_map/ppermute | solution.py:149
  161.3 2.7 collective-permute-start.17
  164.0 5.3 %down_step.5 = bf16[512,1024]{1,0:T(8,128)(2,1)} custom-call(bf16[512,1536]{1,0:T(8,128)(2,1)} %up_step.5.refs_0_, bf16[1536,256]{1,0:T(8,128)(2,1)} %get-tuple-element.70.refs_1_, bf16[1536,256]{1,0:T(8,128)(2,1)} %get-tuple-element.71.refs_2_, bf16[1536,256]{1,0:T(8,128)(2,1)} %copy-done.18, bf16[1536,256]{1,0:T(8,128)(2,1)} %copy-done.19), custom_call_target="tpu_custom_call" | custom-call | flops 2000000000 | bytes 4000000 | tf_op jit(solution)/shard_map/down_step/pallas_call | solution.py:132
  169.3 7.9 %collective-permute-done.16.refs_1_ = bf16[1536,256]{1,0:T(8,128)(2,1)S(1)} collective-permute-done((bf16[1536,256]{1,0:T(8,128)(2,1)S(1)}, bf16[1536,256]{1,0:T(8,128)(2,1)S(1)}, u32[]{:S(2)}, u32[]{:S(2)}) %collective-permute-start.16) | collective-permute-done | bytes 786464 | tf_op jit(solution)/shard_map/ppermute | solution.py:149
  177.2 2.9 collective-permute-start.19
  180.1 18.0 %all-to-all-start.1 = ((bf16[32,16,1024]{2,1,0:T(8,128)(2,1)}), bf16[32,16,1024]{2,1,0:T(8,128)(2,1)S(1)}, u32[]{:S(2)}, u32[]{:S(2)}) async-start(bf16[32,16,1024]{2,1,0:T(8,128)(2,1)} %bitcast.117), calls=%async_computation.1 | async-start | bytes 2097152 | tf_op jit(solution)/shard_map/all_to_all | solution.py:200
  198.2 2.7 collective-permute-start.21
  201.0 0.1 select_reduce_fusion
  201.3 0.1 eq.57
  201.4 0.1 fusion.3
  201.6 5.3 %down_step.6 = bf16[512,1024]{1,0:T(8,128)(2,1)} custom-call(bf16[512,1536]{1,0:T(8,128)(2,1)} %up_step.5.refs_0_, bf16[1536,256]{1,0:T(8,128)(2,1)} %copy-done.13, bf16[1536,256]{1,0:T(8,128)(2,1)} %collective-permute-done.17.refs_2_, bf16[1536,256]{1,0:T(8,128)(2,1)} %collective-permute-done.18.refs_3_, bf16[1536,256]{1,0:T(8,128)(2,1)} %collective-permute-done.19.refs_4_), custom_call_target="tpu_custom_call" | custom-call | flops 2000000000 | bytes 4000000 | tf_op jit(solution)/shard_map/down_step/pallas_call | solution.py:132
  206.8 8.2 %all-to-all-done.1 = bf16[32,16,1024]{2,1,0:T(8,128)(2,1)S(1)} async-done(((bf16[32,16,1024]{2,1,0:T(8,128)(2,1)}), bf16[32,16,1024]{2,1,0:T(8,128)(2,1)S(1)}, u32[]{:S(2)}, u32[]{:S(2)}) %all-to-all-start.1) | async-done | bytes 1048608 | tf_op jit(solution)/shard_map/all_to_all | solution.py:200
  215.0 2.7 collective-permute-start.23
  217.7 0.1 pad_maximum_fusion
  217.8 12.3 %all-to-all-start.2 = ((bf16[32,16,1024]{2,1,0:T(8,128)(2,1)}), bf16[32,16,1024]{2,1,0:T(8,128)(2,1)S(1)}, u32[]{:S(2)}, u32[]{:S(2)}) async-start(bf16[32,16,1024]{2,1,0:T(8,128)(2,1)} %bitcast.118), calls=%async_computation.2 | async-start | bytes 2097152 | tf_op jit(solution)/shard_map/all_to_all | solution.py:200
  230.1 0.3 fusion.33
  230.5 0.4 collective-permute-done.22.refs_3_
  230.9 0.9 copy-done.17
  231.8 2.7 collective-permute-start.25
  234.5 5.3 %down_step.7 = bf16[512,1024]{1,0:T(8,128)(2,1)} custom-call(bf16[512,1536]{1,0:T(8,128)(2,1)} %up_step.5.refs_0_, bf16[1536,256]{1,0:T(8,128)(2,1)} %collective-permute-done.20.refs_1_, bf16[1536,256]{1,0:T(8,128)(2,1)} %collective-permute-done.21.refs_2_, bf16[1536,256]{1,0:T(8,128)(2,1)} %copy-done.17, bf16[1536,256]{1,0:T(8,128)(2,1)} %collective-permute-done.23.refs_4_), custom_call_target="tpu_custom_call" | custom-call | flops 2000000000 | bytes 4000000 | tf_op jit(solution)/shard_map/down_step/pallas_call | solution.py:132
  239.8 7.2 %all-to-all-done.2 = bf16[32,16,1024]{2,1,0:T(8,128)(2,1)S(1)} async-done(((bf16[32,16,1024]{2,1,0:T(8,128)(2,1)}), bf16[32,16,1024]{2,1,0:T(8,128)(2,1)S(1)}, u32[]{:S(2)}, u32[]{:S(2)}) %all-to-all-start.2) | async-done | bytes 1048608 | tf_op jit(solution)/shard_map/all_to_all | solution.py:200
  247.0 6.5 %all-to-all-start.3 = ((bf16[32,16,1024]{2,1,0:T(8,128)(2,1)}), bf16[32,16,1024]{2,1,0:T(8,128)(2,1)S(1)}, u32[]{:S(2)}, u32[]{:S(2)}) async-start(bf16[32,16,1024]{2,1,0:T(8,128)(2,1)} %bitcast.119), calls=%async_computation.3 | async-start | bytes 2097152 | tf_op jit(solution)/shard_map/all_to_all | solution.py:200
  253.6 2.7 collective-permute-start.27
  256.3 0.3 fusion.34
  256.7 3.7 %down_step.8.refs_3_ = bf16[512,1024]{1,0:T(8,128)(2,1)} custom-call(bf16[512,1536]{1,0:T(8,128)(2,1)} %up_step.5.refs_0_, bf16[1536,256]{1,0:T(8,128)(2,1)} %copy-done.16, bf16[1536,256]{1,0:T(8,128)(2,1)} %collective-permute-done.25.refs_2_), custom_call_target="tpu_custom_call" | custom-call | flops 2000000000 | bytes 4000000 | tf_op jit(solution)/shard_map/down_step/pallas_call | solution.py:132
  260.4 10.0 %all-to-all-done.3 = bf16[32,16,1024]{2,1,0:T(8,128)(2,1)S(1)} async-done(((bf16[32,16,1024]{2,1,0:T(8,128)(2,1)}), bf16[32,16,1024]{2,1,0:T(8,128)(2,1)S(1)}, u32[]{:S(2)}, u32[]{:S(2)}) %all-to-all-start.3) | async-done | bytes 1048608 | tf_op jit(solution)/shard_map/all_to_all | solution.py:200
  270.4 0.3 fusion.35
  270.7 3.1 %collective-permute-done.26.refs_1_ = bf16[1536,256]{1,0:T(8,128)(2,1)} collective-permute-done((bf16[1536,256]{1,0:T(8,128)(2,1)S(1)}, bf16[1536,256]{1,0:T(8,128)(2,1)}, u32[]{:S(2)}, u32[]{:S(2)}) %collective-permute-start.26) | collective-permute-done | bytes 786464 | tf_op jit(solution)/shard_map/ppermute | solution.py:149
  273.8 3.7 %down_step.9 = bf16[512,1024]{1,0:T(8,128)(2,1)} custom-call(bf16[512,1536]{1,0:T(8,128)(2,1)} %up_step.5.refs_0_, bf16[1536,256]{1,0:T(8,128)(2,1)} %collective-permute-done.26.refs_1_, bf16[1536,256]{1,0:T(8,128)(2,1)} %collective-permute-done.27.refs_2_, bf16[512,1024]{1,0:T(8,128)(2,1)} %down_step.8.refs_3_), custom_call_target="tpu_custom_call", output_to_operand_aliasing={{}: (3, {})} | custom-call | flops 2000000000 | bytes 4000000 | tf_op jit(solution)/shard_map/down_step/pallas_call | solution.py:132
  277.5 8.1 %all-to-all-start.4 = ((bf16[32,16,1024]{2,1,0:T(8,128)(2,1)}), bf16[32,16,1024]{2,1,0:T(8,128)(2,1)S(1)}, u32[]{:S(2)}, u32[]{:S(2)}) async-start(bf16[32,16,1024]{2,1,0:T(8,128)(2,1)} %bitcast.120), calls=%async_computation.4 | async-start | bytes 2097152 | tf_op jit(solution)/shard_map/all_to_all | solution.py:200
  285.7 16.8 %all-to-all-done.4 = bf16[32,16,1024]{2,1,0:T(8,128)(2,1)S(1)} async-done(((bf16[32,16,1024]{2,1,0:T(8,128)(2,1)}), bf16[32,16,1024]{2,1,0:T(8,128)(2,1)S(1)}, u32[]{:S(2)}, u32[]{:S(2)}) %all-to-all-start.4) | async-done | bytes 1048608 | tf_op jit(solution)/shard_map/all_to_all | solution.py:200
  302.5 0.3 fusion.36
  302.9 0.7 copy-done.11
  303.6 0.6 fusion.9
  (94 shorter events, 1.2 us)
Async XLA Ops:
  0.0 1.3 copy-start
  4.5 108.8 %all-to-all-start = ((bf16[32,16,4096]{2,1,0:T(8,128)(2,1)}), bf16[32,16,4096]{2,1,0:T(8,128)(2,1)}, u32[]{:S(2)}, u32[]{:S(2)}) async-start(bf16[32,16,4096]{2,1,0:T(8,128)(2,1)} %bitcast.112), calls=%async_computation | async-start | bytes 8388608 | tf_op jit(solution)/shard_map/all_to_all | solution.py:191
  16.2 23.6 %collective-permute-start = (bf16[512,768]{1,0:T(8,128)(2,1)}, bf16[512,768]{1,0:T(8,128)(2,1)S(1)}, u32[]{:S(2)}, u32[]{:S(2)}) collective-permute-start(bf16[512,768]{1,0:T(8,128)(2,1)} %get-tuple-element.50.refs_9_), channel_id=1, source_target_pairs={{0,32},{32,64},{64,96},{96,128},{128,160},{160,192},{192,224},{224... | collective-permute-start | bytes 2359304 | tf_op jit(solution)/shard_map/ppermute | solution.py:149
  17.8 21.9 %collective-permute-start.1 = (bf16[512,768]{1,0:T(8,128)(2,1)}, bf16[512,768]{1,0:T(8,128)(2,1)S(1)}, u32[]{:S(2)}, u32[]{:S(2)}) collective-permute-start(bf16[512,768]{1,0:T(8,128)(2,1)} %get-tuple-element.51.refs_10_), channel_id=1, source_target_pairs={{0,224},{32,0},{64,32},{96,64},{128,96},{160,128},{192,160},{224,1... | collective-permute-start | bytes 2359304 | tf_op jit(solution)/shard_map/ppermute | solution.py:149
  39.8 19.8 %copy-start.5 = (bf16[512,768]{1,0:T(8,128)(2,1)}, bf16[512,768]{1,0:T(8,128)(2,1)S(1)}, u32[]{:S(2)}) copy-start(bf16[512,768]{1,0:T(8,128)(2,1)S(1)} %collective-permute-done.refs_11_) | copy-start | bytes 2359300
  39.8 19.8 %copy-start.6 = (bf16[512,768]{1,0:T(8,128)(2,1)}, bf16[512,768]{1,0:T(8,128)(2,1)S(1)}, u32[]{:S(2)}) copy-start(bf16[512,768]{1,0:T(8,128)(2,1)S(1)} %collective-permute-done.1.refs_12_) | copy-start | bytes 2359300
  39.8 19.8 %collective-permute-start.2 = (bf16[512,768]{1,0:T(8,128)(2,1)S(1)}, bf16[512,768]{1,0:T(8,128)(2,1)S(1)}, u32[]{:S(2)}, u32[]{:S(2)}) collective-permute-start(bf16[512,768]{1,0:T(8,128)(2,1)S(1)} %collective-permute-done.refs_11_), channel_id=1, source_target_pairs={{0,32},{32,64},{64,96},{96,128},{128,160},{160,192},{192,224},{224... | collective-permute-start | bytes 2359304 | tf_op jit(solution)/shard_map/ppermute | solution.py:149
  39.9 19.7 %collective-permute-start.3 = (bf16[512,768]{1,0:T(8,128)(2,1)S(1)}, bf16[512,768]{1,0:T(8,128)(2,1)S(1)}, u32[]{:S(2)}, u32[]{:S(2)}) collective-permute-start(bf16[512,768]{1,0:T(8,128)(2,1)S(1)} %collective-permute-done.1.refs_12_), channel_id=1, source_target_pairs={{0,224},{32,0},{64,32},{96,64},{128,96},{160,128},{192,160},{224,1... | collective-permute-start | bytes 2359304 | tf_op jit(solution)/shard_map/ppermute | solution.py:149
  59.5 2.8 copy-start.1
  59.6 5.8 %copy-start.7 = (bf16[512,768]{1,0:T(8,128)(2,1)}, bf16[512,768]{1,0:T(8,128)(2,1)S(1)}, u32[]{:S(2)}) copy-start(bf16[512,768]{1,0:T(8,128)(2,1)S(1)} %collective-permute-done.3.refs_14_) | copy-start | bytes 2359300
  59.6 18.8 %collective-permute-start.4 = (bf16[512,768]{1,0:T(8,128)(2,1)S(1)}, bf16[512,768]{1,0:T(8,128)(2,1)S(1)}, u32[]{:S(2)}, u32[]{:S(2)}) collective-permute-start(bf16[512,768]{1,0:T(8,128)(2,1)S(1)} %collective-permute-done.2.refs_4_.refs_13_), channel_id=1, source_target_pairs={{0,32},{32,64},{64,96},{96,128},{128,160},{160,192},{192,224},{224... | collective-permute-start | bytes 2359304 | tf_op jit(solution)/shard_map/ppermute | solution.py:149
  60.3 18.1 %collective-permute-start.5 = (bf16[512,768]{1,0:T(8,128)(2,1)S(1)}, bf16[512,768]{1,0:T(8,128)(2,1)}, u32[]{:S(2)}, u32[]{:S(2)}) collective-permute-start(bf16[512,768]{1,0:T(8,128)(2,1)S(1)} %collective-permute-done.3.refs_14_), channel_id=1, source_target_pairs={{0,224},{32,0},{64,32},{96,64},{128,96},{160,128},{192,160},{224,1... | collective-permute-start | bytes 2359304 | tf_op jit(solution)/shard_map/ppermute | solution.py:149
  78.4 17.8 %copy-start.8 = (bf16[512,768]{1,0:T(8,128)(2,1)}, bf16[512,768]{1,0:T(8,128)(2,1)S(1)}, u32[]{:S(2)}) copy-start(bf16[512,768]{1,0:T(8,128)(2,1)S(1)} %collective-permute-done.4.refs_15_) | copy-start | bytes 2359300
  78.4 17.8 %collective-permute-start.6 = (bf16[512,768]{1,0:T(8,128)(2,1)S(1)}, bf16[512,768]{1,0:T(8,128)(2,1)S(1)}, u32[]{:S(2)}, u32[]{:S(2)}) collective-permute-start(bf16[512,768]{1,0:T(8,128)(2,1)S(1)} %collective-permute-done.4.refs_15_), channel_id=1, source_target_pairs={{0,32},{32,64},{64,96},{96,128},{128,160},{160,192},{192,224},{224... | collective-permute-start | bytes 2359304 | tf_op jit(solution)/shard_map/ppermute | solution.py:149
  78.8 17.4 %collective-permute-start.7 = (bf16[512,768]{1,0:T(8,128)(2,1)}, bf16[512,768]{1,0:T(8,128)(2,1)S(1)}, u32[]{:S(2)}, u32[]{:S(2)}) collective-permute-start(bf16[512,768]{1,0:T(8,128)(2,1)} %collective-permute-done.5.refs_16_), channel_id=1, source_target_pairs={{0,224},{32,0},{64,32},{96,64},{128,96},{160,128},{192,160},{224,1... | collective-permute-start | bytes 2359304 | tf_op jit(solution)/shard_map/ppermute | solution.py:149
  96.2 29.7 %copy-start.2 = (bf16[512,768]{1,0:T(8,128)(2,1)}, bf16[512,768]{1,0:T(8,128)(2,1)S(1)}, u32[]{:S(2)}) copy-start(bf16[512,768]{1,0:T(8,128)(2,1)S(1)} %collective-permute-done.6.refs_5_) | copy-start | bytes 2359300
  96.3 29.7 %copy-start.3 = (bf16[512,768]{1,0:T(8,128)(2,1)}, bf16[512,768]{1,0:T(8,128)(2,1)S(1)}, u32[]{:S(2)}) copy-start(bf16[512,768]{1,0:T(8,128)(2,1)S(1)} %collective-permute-done.7.refs_6_) | copy-start | bytes 2359300
  96.3 17.0 %collective-permute-start.8 = (bf16[512,768]{1,0:T(8,128)(2,1)S(1)}, bf16[512,768]{1,0:T(8,128)(2,1)S(1)}, u32[]{:S(2)}, u32[]{:S(2)}) collective-permute-start(bf16[512,768]{1,0:T(8,128)(2,1)S(1)} %collective-permute-done.6.refs_5_), channel_id=1, source_target_pairs={{0,32},{32,64},{64,96},{96,128},{128,160},{160,192},{192,224},{224... | collective-permute-start | bytes 2359304 | tf_op jit(solution)/shard_map/ppermute | solution.py:149
  96.6 16.6 %collective-permute-start.9 = (bf16[512,768]{1,0:T(8,128)(2,1)S(1)}, bf16[512,768]{1,0:T(8,128)(2,1)}, u32[]{:S(2)}, u32[]{:S(2)}) collective-permute-start(bf16[512,768]{1,0:T(8,128)(2,1)S(1)} %collective-permute-done.7.refs_6_), channel_id=1, source_target_pairs={{0,224},{32,0},{64,32},{96,64},{128,96},{160,128},{192,160},{224,1... | collective-permute-start | bytes 2359304 | tf_op jit(solution)/shard_map/ppermute | solution.py:149
  113.3 12.7 %copy-start.4 = (bf16[512,768]{1,0:T(8,128)(2,1)}, bf16[512,768]{1,0:T(8,128)(2,1)S(1)}, u32[]{:S(2)}) copy-start(bf16[512,768]{1,0:T(8,128)(2,1)S(1)} %collective-permute-done.8.refs_7_) | copy-start | bytes 2359300
  113.3 16.2 %collective-permute-start.10 = (bf16[512,768]{1,0:T(8,128)(2,1)S(1)}, bf16[512,768]{1,0:T(8,128)(2,1)}, u32[]{:S(2)}, u32[]{:S(2)}) collective-permute-start(bf16[512,768]{1,0:T(8,128)(2,1)S(1)} %collective-permute-done.8.refs_7_), channel_id=1, source_target_pairs={{0,32},{32,64},{64,96},{96,128},{128,160},{160,192},{192,224},{224... | collective-permute-start | bytes 2359304 | tf_op jit(solution)/shard_map/ppermute | solution.py:149
  113.4 16.1 %collective-permute-start.11 = (bf16[512,768]{1,0:T(8,128)(2,1)}, bf16[512,768]{1,0:T(8,128)(2,1)}, u32[]{:S(2)}, u32[]{:S(2)}) collective-permute-start(bf16[512,768]{1,0:T(8,128)(2,1)} %collective-permute-done.9.refs_8_), channel_id=1, source_target_pairs={{0,224},{32,0},{64,32},{96,64},{128,96},{160,128},{192,160},{224,1... | collective-permute-start | bytes 2359304 | tf_op jit(solution)/shard_map/ppermute | solution.py:149
  126.0 19.2 %copy-start.14 = (bf16[1536,256]{1,0:T(8,128)(2,1)S(1)}, bf16[1536,256]{1,0:T(8,128)(2,1)}, u32[]{:S(2)}) copy-start(bf16[1536,256]{1,0:T(8,128)(2,1)} %get-tuple-element.70.refs_1_) | copy-start | bytes 2359300
  126.0 19.3 %copy-start.15 = (bf16[1536,256]{1,0:T(8,128)(2,1)S(1)}, bf16[1536,256]{1,0:T(8,128)(2,1)}, u32[]{:S(2)}) copy-start(bf16[1536,256]{1,0:T(8,128)(2,1)} %get-tuple-element.71.refs_2_) | copy-start | bytes 2359300
  129.5 15.8 %collective-permute-start.12 = (bf16[512,768]{1,0:T(8,128)(2,1)}, bf16[512,768]{1,0:T(8,128)(2,1)S(1)}, u32[]{:S(2)}, u32[]{:S(2)}) collective-permute-start(bf16[512,768]{1,0:T(8,128)(2,1)} %collective-permute-done.10.refs_5_), channel_id=1, source_target_pairs={{0,32},{32,64},{64,96},{96,128},{128,160},{160,192},{192,224},{224... | collective-permute-start | bytes 2359304 | tf_op jit(solution)/shard_map/ppermute | solution.py:149
  129.5 15.8 %collective-permute-start.13 = (bf16[512,768]{1,0:T(8,128)(2,1)}, bf16[512,768]{1,0:T(8,128)(2,1)S(1)}, u32[]{:S(2)}, u32[]{:S(2)}) collective-permute-start(bf16[512,768]{1,0:T(8,128)(2,1)} %collective-permute-done.11.refs_6_), channel_id=1, source_target_pairs={{0,224},{32,0},{64,32},{96,64},{128,96},{160,128},{192,160},{224,1... | collective-permute-start | bytes 2359304 | tf_op jit(solution)/shard_map/ppermute | solution.py:149
  145.2 2.9 copy-start.9
  145.2 2.9 copy-start.10
  145.2 16.0 %collective-permute-start.14 = (bf16[1536,256]{1,0:T(8,128)(2,1)S(1)}, bf16[1536,256]{1,0:T(8,128)(2,1)S(1)}, u32[]{:S(2)}, u32[]{:S(2)}) collective-permute-start(bf16[1536,256]{1,0:T(8,128)(2,1)S(1)} %copy-done.14), channel_id=1, source_target_pairs={{0,32},{32,64},{64,96},{96,128},{128,160},{160,192},{192,224},{224... | collective-permute-start | bytes 2359304 | tf_op jit(solution)/shard_map/ppermute | solution.py:149
  145.3 15.9 %collective-permute-start.15 = (bf16[1536,256]{1,0:T(8,128)(2,1)S(1)}, bf16[1536,256]{1,0:T(8,128)(2,1)S(1)}, u32[]{:S(2)}, u32[]{:S(2)}) collective-permute-start(bf16[1536,256]{1,0:T(8,128)(2,1)S(1)} %copy-done.15), channel_id=1, source_target_pairs={{0,224},{32,0},{64,32},{96,64},{128,96},{160,128},{192,160},{224,1... | collective-permute-start | bytes 2359304 | tf_op jit(solution)/shard_map/ppermute | solution.py:149
  155.6 45.2 %copy-start.12 = (f32[1,1,32,8]{2,3,1,0:T(8,128)S(1)}, f32[1,1,32,8]{2,3,1,0:T(8,128)}, u32[]{:S(2)}) copy-start(f32[1,1,32,8]{2,3,1,0:T(8,128)} %param.6) | copy-start | bytes 3076
  161.2 2.8 copy-start.18
  161.3 2.8 copy-start.19
  161.3 15.9 %collective-permute-start.16 = (bf16[1536,256]{1,0:T(8,128)(2,1)S(1)}, bf16[1536,256]{1,0:T(8,128)(2,1)S(1)}, u32[]{:S(2)}, u32[]{:S(2)}) collective-permute-start(bf16[1536,256]{1,0:T(8,128)(2,1)S(1)} %collective-permute-done.14.refs_3_), channel_id=1, source_target_pairs={{0,32},{32,64},{64,96},{96,128},{128,160},{160,192},{192,224},{224... | collective-permute-start | bytes 2359304 | tf_op jit(solution)/shard_map/ppermute | solution.py:149
  161.3 15.9 %collective-permute-start.17 = (bf16[1536,256]{1,0:T(8,128)(2,1)S(1)}, bf16[1536,256]{1,0:T(8,128)(2,1)}, u32[]{:S(2)}, u32[]{:S(2)}) collective-permute-start(bf16[1536,256]{1,0:T(8,128)(2,1)S(1)} %collective-permute-done.15.refs_4_), channel_id=1, source_target_pairs={{0,224},{32,0},{64,32},{96,64},{128,96},{160,128},{192,160},{224,1... | collective-permute-start | bytes 2359304 | tf_op jit(solution)/shard_map/ppermute | solution.py:149
  177.2 24.4 %copy-start.13 = (bf16[1536,256]{1,0:T(8,128)(2,1)}, bf16[1536,256]{1,0:T(8,128)(2,1)S(1)}, u32[]{:S(2)}) copy-start(bf16[1536,256]{1,0:T(8,128)(2,1)S(1)} %collective-permute-done.16.refs_1_) | copy-start | bytes 2359300
  177.2 20.9 %collective-permute-start.18 = (bf16[1536,256]{1,0:T(8,128)(2,1)S(1)}, bf16[1536,256]{1,0:T(8,128)(2,1)}, u32[]{:S(2)}, u32[]{:S(2)}) collective-permute-start(bf16[1536,256]{1,0:T(8,128)(2,1)S(1)} %collective-permute-done.16.refs_1_), channel_id=1, source_target_pairs={{0,32},{32,64},{64,96},{96,128},{128,160},{160,192},{192,224},{224... | collective-permute-start | bytes 2359304 | tf_op jit(solution)/shard_map/ppermute | solution.py:149
  177.2 20.9 %collective-permute-start.19 = (bf16[1536,256]{1,0:T(8,128)(2,1)}, bf16[1536,256]{1,0:T(8,128)(2,1)}, u32[]{:S(2)}, u32[]{:S(2)}) collective-permute-start(bf16[1536,256]{1,0:T(8,128)(2,1)} %collective-permute-done.17.refs_2_), channel_id=1, source_target_pairs={{0,224},{32,0},{64,32},{96,64},{128,96},{160,128},{192,160},{224,1... | collective-permute-start | bytes 2359304 | tf_op jit(solution)/shard_map/ppermute | solution.py:149
  180.1 34.9 %all-to-all-start.1 = ((bf16[32,16,1024]{2,1,0:T(8,128)(2,1)}), bf16[32,16,1024]{2,1,0:T(8,128)(2,1)S(1)}, u32[]{:S(2)}, u32[]{:S(2)}) async-start(bf16[32,16,1024]{2,1,0:T(8,128)(2,1)} %bitcast.117), calls=%async_computation.1 | async-start | bytes 2097152 | tf_op jit(solution)/shard_map/all_to_all | solution.py:200
  198.1 16.9 %collective-permute-start.20 = (bf16[1536,256]{1,0:T(8,128)(2,1)}, bf16[1536,256]{1,0:T(8,128)(2,1)}, u32[]{:S(2)}, u32[]{:S(2)}) collective-permute-start(bf16[1536,256]{1,0:T(8,128)(2,1)} %collective-permute-done.18.refs_3_), channel_id=1, source_target_pairs={{0,32},{32,64},{64,96},{96,128},{128,160},{160,192},{192,224},{224... | collective-permute-start | bytes 2359304 | tf_op jit(solution)/shard_map/ppermute | solution.py:149
  198.2 16.8 %collective-permute-start.21 = (bf16[1536,256]{1,0:T(8,128)(2,1)}, bf16[1536,256]{1,0:T(8,128)(2,1)}, u32[]{:S(2)}, u32[]{:S(2)}) collective-permute-start(bf16[1536,256]{1,0:T(8,128)(2,1)} %collective-permute-done.19.refs_4_), channel_id=1, source_target_pairs={{0,224},{32,0},{64,32},{96,64},{128,96},{160,128},{192,160},{224,1... | collective-permute-start | bytes 2359304 | tf_op jit(solution)/shard_map/ppermute | solution.py:149
  215.0 15.9 %collective-permute-start.22 = (bf16[1536,256]{1,0:T(8,128)(2,1)}, bf16[1536,256]{1,0:T(8,128)(2,1)S(1)}, u32[]{:S(2)}, u32[]{:S(2)}) collective-permute-start(bf16[1536,256]{1,0:T(8,128)(2,1)} %collective-permute-done.20.refs_1_), channel_id=1, source_target_pairs={{0,32},{32,64},{64,96},{96,128},{128,160},{160,192},{192,224},{224... | collective-permute-start | bytes 2359304 | tf_op jit(solution)/shard_map/ppermute | solution.py:149
  215.0 16.8 %collective-permute-start.23 = (bf16[1536,256]{1,0:T(8,128)(2,1)}, bf16[1536,256]{1,0:T(8,128)(2,1)}, u32[]{:S(2)}, u32[]{:S(2)}) collective-permute-start(bf16[1536,256]{1,0:T(8,128)(2,1)} %collective-permute-done.21.refs_2_), channel_id=1, source_target_pairs={{0,224},{32,0},{64,32},{96,64},{128,96},{160,128},{192,160},{224,1... | collective-permute-start | bytes 2359304 | tf_op jit(solution)/shard_map/ppermute | solution.py:149
  217.8 29.2 %all-to-all-start.2 = ((bf16[32,16,1024]{2,1,0:T(8,128)(2,1)}), bf16[32,16,1024]{2,1,0:T(8,128)(2,1)S(1)}, u32[]{:S(2)}, u32[]{:S(2)}) async-start(bf16[32,16,1024]{2,1,0:T(8,128)(2,1)} %bitcast.118), calls=%async_computation.2 | async-start | bytes 2097152 | tf_op jit(solution)/shard_map/all_to_all | solution.py:200
  230.9 0.9 copy-start.17
  231.8 21.7 %collective-permute-start.24 = (bf16[1536,256]{1,0:T(8,128)(2,1)}, bf16[1536,256]{1,0:T(8,128)(2,1)S(1)}, u32[]{:S(2)}, u32[]{:S(2)}) collective-permute-start(bf16[1536,256]{1,0:T(8,128)(2,1)} %copy-done.17), channel_id=1, source_target_pairs={{0,32},{32,64},{64,96},{96,128},{128,160},{160,192},{192,224},{224... | collective-permute-start | bytes 2359304 | tf_op jit(solution)/shard_map/ppermute | solution.py:149
  231.8 21.7 %collective-permute-start.25 = (bf16[1536,256]{1,0:T(8,128)(2,1)}, bf16[1536,256]{1,0:T(8,128)(2,1)}, u32[]{:S(2)}, u32[]{:S(2)}) collective-permute-start(bf16[1536,256]{1,0:T(8,128)(2,1)} %collective-permute-done.23.refs_4_), channel_id=1, source_target_pairs={{0,224},{32,0},{64,32},{96,64},{128,96},{160,128},{192,160},{224,1... | collective-permute-start | bytes 2359304 | tf_op jit(solution)/shard_map/ppermute | solution.py:149
  247.0 23.4 %all-to-all-start.3 = ((bf16[32,16,1024]{2,1,0:T(8,128)(2,1)}), bf16[32,16,1024]{2,1,0:T(8,128)(2,1)S(1)}, u32[]{:S(2)}, u32[]{:S(2)}) async-start(bf16[32,16,1024]{2,1,0:T(8,128)(2,1)} %bitcast.119), calls=%async_computation.3 | async-start | bytes 2097152 | tf_op jit(solution)/shard_map/all_to_all | solution.py:200
  253.5 3.2 %copy-start.16 = (bf16[1536,256]{1,0:T(8,128)(2,1)}, bf16[1536,256]{1,0:T(8,128)(2,1)S(1)}, u32[]{:S(2)}) copy-start(bf16[1536,256]{1,0:T(8,128)(2,1)S(1)} %collective-permute-done.24.refs_1_) | copy-start | bytes 2359300
  253.5 20.3 %collective-permute-start.26 = (bf16[1536,256]{1,0:T(8,128)(2,1)S(1)}, bf16[1536,256]{1,0:T(8,128)(2,1)}, u32[]{:S(2)}, u32[]{:S(2)}) collective-permute-start(bf16[1536,256]{1,0:T(8,128)(2,1)S(1)} %collective-permute-done.24.refs_1_), channel_id=1, source_target_pairs={{0,32},{32,64},{64,96},{96,128},{128,160},{160,192},{192,224},{224... | collective-permute-start | bytes 2359304 | tf_op jit(solution)/shard_map/ppermute | solution.py:149
  253.6 20.2 %collective-permute-start.27 = (bf16[1536,256]{1,0:T(8,128)(2,1)}, bf16[1536,256]{1,0:T(8,128)(2,1)}, u32[]{:S(2)}, u32[]{:S(2)}) collective-permute-start(bf16[1536,256]{1,0:T(8,128)(2,1)} %collective-permute-done.25.refs_2_), channel_id=1, source_target_pairs={{0,224},{32,0},{64,32},{96,64},{128,96},{160,128},{192,160},{224,1... | collective-permute-start | bytes 2359304 | tf_op jit(solution)/shard_map/ppermute | solution.py:149
  277.5 25.0 %all-to-all-start.4 = ((bf16[32,16,1024]{2,1,0:T(8,128)(2,1)}), bf16[32,16,1024]{2,1,0:T(8,128)(2,1)S(1)}, u32[]{:S(2)}, u32[]{:S(2)}) async-start(bf16[32,16,1024]{2,1,0:T(8,128)(2,1)} %bitcast.120), calls=%async_computation.4 | async-start | bytes 2097152 | tf_op jit(solution)/shard_map/all_to_all | solution.py:200
  302.9 0.7 copy-start.11
